TPU v7x, 32 devices: a whole 2x2x4 slice. The times are simulated.
32 devices in a mesh: dp: 16 (over z, x, core), seq: 2 (over y).
Axes of the slice: x: 2, y: 2, z: 4, core: 2. Of those that a mesh axis runs over, the one named last changes fastest.
Arguments:
- text_input: bfloat16 [32, 100, 768], P(('dp', 'seq')), may hold values from -6 to 6
- image_input: bfloat16 [32, 36, 1024], P(('dp', 'seq')), may hold values from -6 to 6
- caption_lengths: int32 [32], P('dp'), may hold values from 1 to 100, as said below
- text_cotangent: bfloat16 [32, 100, 768], P(('dp', 'seq')), may hold values from -6 to 6
- image_cotangent: bfloat16 [32, 36, 1024], P(('dp', 'seq')), may hold values from -6 to 6
- cross_text_proj: bfloat16 [3, 768, 1024], P(None, ('dp', 'seq')), may hold values from -0.21875 to 0.21875
- cross_image_proj: bfloat16 [3, 1024, 1024], P(None, ('dp', 'seq')), may hold values from -0.1875 to 0.1875
- cross_text_out: bfloat16 [1024, 768], P(('dp', 'seq')), may hold values from -0.4375 to 0.4375
- cross_image_out: bfloat16 [1024, 1024], P(('dp', 'seq')), may hold values from -0.5 to 0.5
- cross_text_up: bfloat16 [768, 3072], P(('dp', 'seq')), may hold values from -0.21875 to 0.21875
- cross_text_down: bfloat16 [3072, 768], P(('dp', 'seq')), may hold values from -0.109375 to 0.109375
- cross_image_up: bfloat16 [1024, 1024], P(('dp', 'seq')), may hold values from -0.1875 to 0.1875
- cross_image_down: bfloat16 [1024, 1024], P(('dp', 'seq')), may hold values from -0.1875 to 0.1875
- self_text_proj: bfloat16 [3, 768, 768], P(None, ('dp', 'seq')), may hold values from -0.21875 to 0.21875
- self_text_out: bfloat16 [768, 768], P(('dp', 'seq')), may hold values from -0.5 to 0.5
- self_text_up: bfloat16 [768, 3072], P(('dp', 'seq')), may hold values from -0.21875 to 0.21875
- self_text_down: bfloat16 [3072, 768], P(('dp', 'seq')), may hold values from -0.109375 to 0.109375
- self_image_proj: bfloat16 [3, 1024, 1024], P(None, ('dp', 'seq')), may hold values from -0.1875 to 0.1875
- self_image_out: bfloat16 [1024, 1024], P(('dp', 'seq')), may hold values from -0.4375 to 0.4375
- self_image_up: bfloat16 [1024, 1024], P(('dp', 'seq')), may hold values from -0.1875 to 0.1875
- self_image_down: bfloat16 [1024, 1024], P(('dp', 'seq')), may hold values from -0.1875 to 0.1875
- text_gains: float32 [4, 768], replicated, may hold values from 0.5 to 1.5
- image_gains: float32 [4, 1024], replicated, may hold values from 0.5 to 1.5
Outputs:
- text_output: bfloat16 [32, 100, 768], P(('dp', 'seq'))
- image_output: bfloat16 [32, 36, 1024], P(('dp', 'seq'))
- text_input_grad: float32 [32, 100, 768], P(('dp', 'seq'))
- image_input_grad: float32 [32, 36, 1024], P(('dp', 'seq'))
- cross_text_proj_grad: float32 [3, 768, 1024], P(None, None, ('dp', 'seq'))
- cross_image_proj_grad: float32 [3, 1024, 1024], P(None, None, ('dp', 'seq'))
- cross_text_out_grad: float32 [1024, 768], P(('dp', 'seq'))
- cross_image_out_grad: float32 [1024, 1024], P(('dp', 'seq'))
- cross_text_up_grad: float32 [768, 3072], P(None, ('dp', 'seq'))
- cross_text_down_grad: float32 [3072, 768], P(('dp', 'seq'))
- cross_image_up_grad: float32 [1024, 1024], P(None, ('dp', 'seq'))
- cross_image_down_grad: float32 [1024, 1024], P(('dp', 'seq'))
- self_text_proj_grad: float32 [3, 768, 768], P(None, None, ('dp', 'seq'))
- self_text_out_grad: float32 [768, 768], P(('dp', 'seq'))
- self_text_up_grad: float32 [768, 3072], P(None, ('dp', 'seq'))
- self_text_down_grad: float32 [3072, 768], P(None, ('dp', 'seq'))
- self_image_proj_grad: float32 [3, 1024, 1024], P(None, None, ('dp', 'seq'))
- self_image_out_grad: float32 [1024, 1024], P(('dp', 'seq'))
- self_image_up_grad: float32 [1024, 1024], P(None, ('dp', 'seq'))
- self_image_down_grad: float32 [1024, 1024], P(None, ('dp', 'seq'))
- text_gains_grad: float32 [4, 768], P(None, ('dp', 'seq'))
- image_gains_grad: float32 [4, 1024], P(None, ('dp', 'seq'))
Inputs may be any that keep to these rules, and one draw needn't show every extreme that they name: A pair's caption uses its first caption_lengths tokens; some pair in every draw uses all 100.
All inputs are finite; a program needn't handle non-finite values.
Results may differ from a plain program's by a relative error of at most 0.024.
Values may be sent and summed in bfloat16 or wider, within the bound.
No kernel may reach another device: no remote copies, remote signals or barrier semaphores. Data moves between devices by JAX's collectives and lax.ppermute only.
A program may use at most 320 MiB of HBM per device.

v0:
```python
import jax
import jax.numpy as jnp
from jax import lax
from jax.sharding import PartitionSpec as P

H_T = 12
H_V = 8
H_C = 8


EPSILON = 1e-05
NEGATIVE = -1000000000.0
FLOAT = jnp.float32
BFLOAT = jnp.bfloat16


def as_sent(array):

    def short(part):
        return part.astype(jnp.bfloat16) if part.dtype == jnp.float32 else part

    return jax.tree.map(short, array)


def layer_norm(stream, gain_vec):
    center = stream - jnp.mean(stream, axis=-1, keepdims=True)
    spread = jnp.mean(center * center, axis=-1, keepdims=True)
    return center * lax.rsqrt(spread + EPSILON) * gain_vec


def norm_back(stream, gain_vec, upstream):
    unused, pullback = jax.vjp(layer_norm, stream, gain_vec)
    return pullback(upstream)


def gelu_back(upper, upstream):
    unused, pullback = jax.vjp(jax.nn.gelu, upper)
    return pullback(upstream)[0]


def project(stream_low, weights, heads):
    packed = jnp.einsum("pld,edw->plew", stream_low, weights, preferred_element_type=FLOAT).astype(
        BFLOAT
    )
    return packed.reshape(packed.shape[0], packed.shape[1], 3, heads, packed.shape[3] // heads)


def proj_back(stream_low, grad_packed, weights):
    grad_stream = jnp.einsum("plew,edw->pld", grad_packed, weights, preferred_element_type=FLOAT)
    grad_weights = jnp.einsum(
        "pld,plew->edw", stream_low, grad_packed, preferred_element_type=FLOAT
    )
    return (grad_stream, grad_weights)


def score_block(queries, key_rows, valid_keys):
    scale_factor = queries.shape[-1] ** (-0.5)
    scores = (
        jnp.einsum("pqhd,pkhd->phqk", queries, key_rows, preferred_element_type=FLOAT)
        * scale_factor
    )
    return (jnp.where(valid_keys[:, None, None, :], scores, NEGATIVE), scale_factor)


def attend(queries, key_rows, value_rows, valid_keys):
    scores, unused = score_block(queries, key_rows, valid_keys)
    maxima = jnp.max(scores, axis=-1, keepdims=True)
    expo_terms = jnp.exp(scores - maxima)
    totals = jnp.sum(expo_terms, axis=-1, keepdims=True)
    weights_low = (expo_terms / totals).astype(BFLOAT)
    mixed = jnp.einsum("phqk,pkhd->pqhd", weights_low, value_rows, preferred_element_type=FLOAT)
    return (mixed.astype(BFLOAT), maxima + jnp.log(totals))


def attend_back(queries, key_rows, value_rows, valid_keys, log_totals, grad_mixed):
    scores, scale_factor = score_block(queries, key_rows, valid_keys)
    attn_probs = jnp.exp(scores - log_totals)
    grad_probs = jnp.einsum("pqhd,pkhd->phqk", grad_mixed, value_rows, preferred_element_type=FLOAT)
    inner_sum = jnp.sum(grad_probs * attn_probs, axis=-1, keepdims=True)
    grad_scores = (attn_probs * (grad_probs - inner_sum)).astype(BFLOAT)
    grad_queries = (
        jnp.einsum("phqk,pkhd->pqhd", grad_scores, key_rows, preferred_element_type=FLOAT)
        * scale_factor
    )
    grad_keys = (
        jnp.einsum("phqk,pqhd->pkhd", grad_scores, queries, preferred_element_type=FLOAT)
        * scale_factor
    )
    grad_values = jnp.einsum(
        "phqk,pqhd->pkhd", attn_probs.astype(BFLOAT), grad_mixed, preferred_element_type=FLOAT
    )
    return (grad_queries, grad_keys, grad_values)


def to_heads(packed):
    return lax.all_to_all(packed, "seq", split_axis=3, concat_axis=0, tiled=True)


def from_heads(mixed):
    mixed = lax.all_to_all(mixed, "seq", split_axis=0, concat_axis=2, tiled=True)
    return mixed.reshape(mixed.shape[0], mixed.shape[1], mixed.shape[2] * mixed.shape[3])


def grad_to_heads(grad_low, heads):
    grad_low = grad_low.reshape(
        grad_low.shape[0], grad_low.shape[1], heads, grad_low.shape[2] // heads
    )
    grad_low = lax.all_to_all(grad_low, "seq", split_axis=2, concat_axis=0, tiled=True)
    return grad_low


def grad_from_heads(grad_packed):
    grad_packed = lax.all_to_all(grad_packed, "seq", split_axis=0, concat_axis=3, tiled=True)
    return grad_packed.reshape(
        grad_packed.shape[0], grad_packed.shape[1], 3, grad_packed.shape[3] * grad_packed.shape[4]
    )


def tail_forward(residual, attn_low, out_mat, up_mat, down_mat, gain_pair):
    first_sum = residual + jnp.einsum(
        "plc,cd->pld", attn_low, out_mat, preferred_element_type=FLOAT
    )
    first_norm = layer_norm(first_sum, gain_pair[0])
    hidden_low = first_norm.astype(BFLOAT)
    upper = jnp.einsum("pld,df->plf", hidden_low, up_mat, preferred_element_type=FLOAT)
    active = jax.nn.gelu(upper).astype(BFLOAT)
    second_sum = first_norm + jnp.einsum(
        "plf,fd->pld", active, down_mat, preferred_element_type=FLOAT
    )
    return (
        layer_norm(second_sum, gain_pair[1]),
        (first_sum, hidden_low, upper, active, second_sum),
    )


def tail_backward(grad_result, kept, attn_low, out_mat, up_mat, down_mat, gain_pair):
    first_sum, hidden_low, upper, active, second_sum = kept
    grad_second, gain_two = norm_back(second_sum, gain_pair[1], grad_result)
    grad_down_in = grad_second.astype(BFLOAT)
    grad_down = jnp.einsum("plf,pld->fd", active, grad_down_in, preferred_element_type=FLOAT)
    grad_active = jnp.einsum("pld,fd->plf", grad_down_in, down_mat, preferred_element_type=FLOAT)
    grad_upper = gelu_back(upper, grad_active).astype(BFLOAT)
    grad_up = jnp.einsum("pld,plf->df", hidden_low, grad_upper, preferred_element_type=FLOAT)
    grad_norm = grad_second + jnp.einsum(
        "plf,df->pld", grad_upper, up_mat, preferred_element_type=FLOAT
    )
    grad_first, gain_one = norm_back(first_sum, gain_pair[0], grad_norm)
    grad_first_low = grad_first.astype(BFLOAT)
    grad_out = jnp.einsum("plc,pld->cd", attn_low, grad_first_low, preferred_element_type=FLOAT)
    grad_attn = jnp.einsum(
        "pld,cd->plc", grad_first_low, out_mat, preferred_element_type=FLOAT
    ).astype(BFLOAT)
    return (grad_first, grad_attn, grad_out, grad_up, grad_down, jnp.stack([gain_one, gain_two]))


def self_forward(hidden, proj_mat, out_mat, up_mat, down_mat, gain_pair, heads, valid_keys):
    hidden_low = hidden.astype(BFLOAT)
    packed = to_heads(project(hidden_low, proj_mat, heads))
    mixed, log_totals = attend(packed[:, :, 0], packed[:, :, 1], packed[:, :, 2], valid_keys)
    attn_low = from_heads(mixed)
    result, tail_kept = tail_forward(hidden, attn_low, out_mat, up_mat, down_mat, gain_pair)
    return (result, (hidden_low, packed, log_totals, attn_low, tail_kept))


def self_backward(
    grad_result, saved, proj_mat, out_mat, up_mat, down_mat, gain_pair, heads, valid_keys
):
    hidden_low, packed, log_totals, attn_low, tail_kept = saved
    grad_resid, grad_attn, grad_out, grad_up, grad_down, gain_grads = tail_backward(
        grad_result, tail_kept, attn_low, out_mat, up_mat, down_mat, gain_pair
    )
    grad_heads = grad_to_heads(grad_attn, heads)
    grad_queries, grad_keys, grad_values = attend_back(
        packed[:, :, 0], packed[:, :, 1], packed[:, :, 2], valid_keys, log_totals, grad_heads
    )
    grad_packed = grad_from_heads(
        jnp.stack([grad_queries, grad_keys, grad_values], axis=2).astype(BFLOAT)
    )
    grad_stream, grad_proj = proj_back(hidden_low, grad_packed, proj_mat)
    return (grad_resid + grad_stream, (grad_proj, grad_out, grad_up, grad_down), gain_grads)


def to_rows(grads, dims):
    rows = []
    for member, axis_pick in zip(grads, dims):
        moved = jnp.moveaxis(member, axis_pick, 0)
        rows.append(moved.reshape(1, moved.shape[0], -1))
    return tuple(rows)


def from_rows(pieces, grads, dims):
    rebuilt = []
    for piece, member, axis_pick in zip(pieces, grads, dims):
        moved_shape = (
            (piece.shape[0],)
            + tuple(member.shape[:axis_pick])
            + tuple(member.shape[axis_pick + 1 :])
        )
        rebuilt.append(jnp.moveaxis(piece.reshape(moved_shape), 0, axis_pick))
    return tuple(rebuilt)


def add_parts(parts):
    return tuple((jnp.sum(member, axis=0) for member in parts))


def on_device(
    text_input,
    image_input,
    caption_lengths,
    text_cotangent,
    image_cotangent,
    cross_text_proj,
    cross_image_proj,
    cross_text_out,
    cross_image_out,
    cross_text_up,
    cross_text_down,
    cross_image_up,
    cross_image_down,
    self_text_proj,
    self_text_out,
    self_text_up,
    self_text_down,
    self_image_proj,
    self_image_out,
    self_image_up,
    self_image_down,
    text_gains,
    image_gains,
):
    (
        cross_text_proj,
        cross_image_proj,
        cross_text_out,
        cross_image_out,
        cross_text_up,
        cross_text_down,
        cross_image_up,
        cross_image_down,
        self_text_proj,
        self_text_out,
        self_text_up,
        self_text_down,
        self_image_proj,
        self_image_out,
        self_image_up,
        self_image_down,
    ) = (
        lax.all_gather(cross_text_proj, ("dp", "seq"), axis=1, tiled=True),
        lax.all_gather(cross_image_proj, ("dp", "seq"), axis=1, tiled=True),
        lax.all_gather(cross_text_out, ("dp", "seq"), axis=0, tiled=True),
        lax.all_gather(cross_image_out, ("dp", "seq"), axis=0, tiled=True),
        lax.all_gather(cross_text_up, ("dp", "seq"), axis=0, tiled=True),
        lax.all_gather(cross_text_down, ("dp", "seq"), axis=0, tiled=True),
        lax.all_gather(cross_image_up, ("dp", "seq"), axis=0, tiled=True),
        lax.all_gather(cross_image_down, ("dp", "seq"), axis=0, tiled=True),
        lax.all_gather(self_text_proj, ("dp", "seq"), axis=1, tiled=True),
        lax.all_gather(self_text_out, ("dp", "seq"), axis=0, tiled=True),
        lax.all_gather(self_text_up, ("dp", "seq"), axis=0, tiled=True),
        lax.all_gather(self_text_down, ("dp", "seq"), axis=0, tiled=True),
        lax.all_gather(self_image_proj, ("dp", "seq"), axis=1, tiled=True),
        lax.all_gather(self_image_out, ("dp", "seq"), axis=0, tiled=True),
        lax.all_gather(self_image_up, ("dp", "seq"), axis=0, tiled=True),
        lax.all_gather(self_image_down, ("dp", "seq"), axis=0, tiled=True),
    )
    caption_valid = jnp.arange(text_input.shape[1])[None, :] < caption_lengths[:, None]
    image_valid = jnp.ones((caption_valid.shape[0], image_input.shape[1]), dtype=jnp.bool_)
    text_packed = to_heads(project(text_input, cross_text_proj, H_C))
    image_packed = to_heads(project(image_input, cross_image_proj, H_C))
    text_mixed, text_log_totals = attend(
        text_packed[:, :, 0], image_packed[:, :, 1], image_packed[:, :, 2], image_valid
    )
    image_mixed, image_log_totals = attend(
        image_packed[:, :, 0], text_packed[:, :, 1], text_packed[:, :, 2], caption_valid
    )
    text_attn = from_heads(text_mixed)
    image_attn = from_heads(image_mixed)
    text_cross, text_cross_kept = tail_forward(
        text_input.astype(FLOAT),
        text_attn,
        cross_text_out,
        cross_text_up,
        cross_text_down,
        text_gains[0:2],
    )
    image_cross, image_cross_kept = tail_forward(
        image_input.astype(FLOAT),
        image_attn,
        cross_image_out,
        cross_image_up,
        cross_image_down,
        image_gains[0:2],
    )
    text_final, text_self_kept = self_forward(
        text_cross,
        self_text_proj,
        self_text_out,
        self_text_up,
        self_text_down,
        text_gains[2:4],
        H_T,
        caption_valid,
    )
    image_final, image_self_kept = self_forward(
        image_cross,
        self_image_proj,
        self_image_out,
        self_image_up,
        self_image_down,
        image_gains[2:4],
        H_V,
        image_valid,
    )
    text_back, text_self_grads, text_self_gains = self_backward(
        text_cotangent.astype(FLOAT),
        text_self_kept,
        self_text_proj,
        self_text_out,
        self_text_up,
        self_text_down,
        text_gains[2:4],
        H_T,
        caption_valid,
    )
    image_back, image_self_grads, image_self_gains = self_backward(
        image_cotangent.astype(FLOAT),
        image_self_kept,
        self_image_proj,
        self_image_out,
        self_image_up,
        self_image_down,
        image_gains[2:4],
        H_V,
        image_valid,
    )
    text_resid, text_grad_attn, text_out_grad, text_up_grad, text_down_grad, text_cross_gains = (
        tail_backward(
            text_back,
            text_cross_kept,
            text_attn,
            cross_text_out,
            cross_text_up,
            cross_text_down,
            text_gains[0:2],
        )
    )
    (
        image_resid,
        image_grad_attn,
        image_out_grad,
        image_up_grad,
        image_down_grad,
        image_cross_gains,
    ) = tail_backward(
        image_back,
        image_cross_kept,
        image_attn,
        cross_image_out,
        cross_image_up,
        cross_image_down,
        image_gains[0:2],
    )
    text_heads = grad_to_heads(text_grad_attn, H_C)
    image_heads = grad_to_heads(image_grad_attn, H_C)
    text_query_grad, image_key_grad, image_value_grad = attend_back(
        text_packed[:, :, 0],
        image_packed[:, :, 1],
        image_packed[:, :, 2],
        image_valid,
        text_log_totals,
        text_heads,
    )
    image_query_grad, text_key_grad, text_value_grad = attend_back(
        image_packed[:, :, 0],
        text_packed[:, :, 1],
        text_packed[:, :, 2],
        caption_valid,
        image_log_totals,
        image_heads,
    )
    text_grad_packed = grad_from_heads(
        jnp.stack([text_query_grad, text_key_grad, text_value_grad], axis=2).astype(BFLOAT)
    )
    image_grad_packed = grad_from_heads(
        jnp.stack([image_query_grad, image_key_grad, image_value_grad], axis=2).astype(BFLOAT)
    )
    text_stream_grad, text_proj_grad = proj_back(text_input, text_grad_packed, cross_text_proj)
    image_stream_grad, image_proj_grad = proj_back(image_input, image_grad_packed, cross_image_proj)
    text_input_grad = text_resid + text_stream_grad
    image_input_grad = image_resid + image_stream_grad
    all_grads = (
        text_proj_grad,
        image_proj_grad,
        text_out_grad,
        image_out_grad,
        text_up_grad,
        text_down_grad,
        image_up_grad,
        image_down_grad,
        text_self_grads[0],
        text_self_grads[1],
        text_self_grads[2],
        text_self_grads[3],
        image_self_grads[0],
        image_self_grads[1],
        image_self_grads[2],
        image_self_grads[3],
        jnp.concatenate([text_cross_gains, text_self_gains], axis=0),
        jnp.concatenate([image_cross_gains, image_self_gains], axis=0),
    )
    all_dims = (2, 2, 0, 0, 1, 0, 1, 0, 2, 0, 1, 1, 2, 0, 1, 1, 1, 1)
    all_parts = lax.all_to_all(
        as_sent(to_rows(all_grads, all_dims)), "dp", split_axis=1, concat_axis=0, tiled=True
    )
    all_rows = jax.tree.map(
        lambda part: part.astype(jnp.float32),
        lax.psum_scatter(as_sent(add_parts(all_parts)), "seq", scatter_dimension=0, tiled=True),
    )
    final_grads = from_rows(all_rows, all_grads, all_dims)
    return (
        text_final.astype(BFLOAT),
        image_final.astype(BFLOAT),
        text_input_grad,
        image_input_grad,
    ) + tuple(final_grads)


def solution(mesh):
    in_specs = (
        P(("dp", "seq"), None, None),
        P(("dp", "seq"), None, None),
        P("dp"),
        P(("dp", "seq"), None, None),
        P(("dp", "seq"), None, None),
        P(None, ("dp", "seq"), None),
        P(None, ("dp", "seq"), None),
        P(("dp", "seq"), None),
        P(("dp", "seq"), None),
        P(("dp", "seq"), None),
        P(("dp", "seq"), None),
        P(("dp", "seq"), None),
        P(("dp", "seq"), None),
        P(None, ("dp", "seq"), None),
        P(("dp", "seq"), None),
        P(("dp", "seq"), None),
        P(("dp", "seq"), None),
        P(None, ("dp", "seq"), None),
        P(("dp", "seq"), None),
        P(("dp", "seq"), None),
        P(("dp", "seq"), None),
        P(),
        P(),
    )
    out_specs = (
        P(("dp", "seq"), None, None),
        P(("dp", "seq"), None, None),
        P(("dp", "seq"), None, None),
        P(("dp", "seq"), None, None),
        P(None, None, ("dp", "seq")),
        P(None, None, ("dp", "seq")),
        P(("dp", "seq"), None),
        P(("dp", "seq"), None),
        P(None, ("dp", "seq")),
        P(("dp", "seq"), None),
        P(None, ("dp", "seq")),
        P(("dp", "seq"), None),
        P(None, None, ("dp", "seq")),
        P(("dp", "seq"), None),
        P(None, ("dp", "seq")),
        P(None, ("dp", "seq")),
        P(None, None, ("dp", "seq")),
        P(("dp", "seq"), None),
        P(None, ("dp", "seq")),
        P(None, ("dp", "seq")),
        P(None, ("dp", "seq")),
        P(None, ("dp", "seq")),
    )
    return jax.shard_map(
        on_device, mesh=mesh, in_specs=in_specs, out_specs=out_specs, check_vma=False
    )
```

profile of v0, /device:TPU:0, one launch (start us, length us, event | category | flops | bytes accessed | tf_op | source)
XLA Modules:
  0.0 2829.8 jit_solution(8436591589380398131)
XLA Ops:
  19.4 58.0 %all-gather.19.cloned.1.call-done = bf16[3,768,1024]{2,1,0:T(8,128)(2,1)} async-done(((bf16[3,24,1024]{2,1,0:T(8,128)(2,1)}), bf16[3,768,1024]{2,1,0:T(8,128)(2,1)}) %all-gather.19.cloned.1.call-update) | async-done | bytes 4718608 | tf_op jit(solution)/shard_map/all_gather | solution.py:250
  85.4 64.2 %all-gather.17.cloned.1.call-done = bf16[3,1024,1024]{2,1,0:T(8,128)(2,1)} async-done(((bf16[3,32,1024]{2,1,0:T(8,128)(2,1)}), bf16[3,1024,1024]{2,1,0:T(8,128)(2,1)}) %all-gather.17.cloned.1.call-update) | async-done | bytes 6291472 | tf_op jit(solution)/shard_map/all_gather | solution.py:251
  176.8 31.4 %all-gather.35.cloned.1.call-done = bf16[1024,1024]{1,0:T(8,128)(2,1)} async-done(((bf16[32,1024]{1,0:T(8,128)(2,1)}), bf16[1024,1024]{1,0:T(8,128)(2,1)}) %all-gather.35.cloned.1.call-update) | async-done | bytes 2097168 | tf_op jit(solution)/shard_map/all_gather | solution.py:253
  210.6 55.9 %all-gather.37.cloned.1.call-done = bf16[1024,1024]{1,0:T(8,128)(2,1)} async-done(((bf16[32,1024]{1,0:T(8,128)(2,1)}), bf16[1024,1024]{1,0:T(8,128)(2,1)}) %all-gather.37.cloned.1.call-update) | async-done | bytes 2097168 | tf_op jit(solution)/shard_map/all_gather | solution.py:256
  268.7 56.2 %all-gather.39.cloned.1.call-done = bf16[1024,1024]{1,0:T(8,128)(2,1)} async-done(((bf16[32,1024]{1,0:T(8,128)(2,1)}), bf16[1024,1024]{1,0:T(8,128)(2,1)}) %all-gather.39.cloned.1.call-update) | async-done | bytes 2097168 | tf_op jit(solution)/shard_map/all_gather | solution.py:257
  327.3 68.6 %all-gather.41.cloned.1.call-done = bf16[3,1024,1024]{2,1,0:T(8,128)(2,1)} async-done(((bf16[3,32,1024]{2,1,0:T(8,128)(2,1)}), bf16[3,1024,1024]{2,1,0:T(8,128)(2,1)}) %all-gather.41.cloned.1.call-update) | async-done | bytes 6291472 | tf_op jit(solution)/shard_map/all_gather | solution.py:262
  405.1 47.7 %all-gather.21.cloned.1.call-done = bf16[1024,768]{1,0:T(8,128)(2,1)} async-done(((bf16[32,768]{1,0:T(8,128)(2,1)}), bf16[1024,768]{1,0:T(8,128)(2,1)}) %all-gather.21.cloned.1.call-update) | async-done | bytes 1572880 | tf_op jit(solution)/shard_map/all_gather | solution.py:252
  454.9 63.3 %all-gather.23.cloned.1.call-done = bf16[768,3072]{1,0:T(8,128)(2,1)} async-done(((bf16[24,3072]{1,0:T(8,128)(2,1)}), bf16[768,3072]{1,0:T(8,128)(2,1)}) %all-gather.23.cloned.1.call-update) | async-done | bytes 4718608 | tf_op jit(solution)/shard_map/all_gather | solution.py:254
  521.5 62.2 %all-gather.25.cloned.1.call-done = bf16[3072,768]{1,0:T(8,128)(2,1)} async-done(((bf16[96,768]{1,0:T(8,128)(2,1)}), bf16[3072,768]{1,0:T(8,128)(2,1)}) %all-gather.25.cloned.1.call-update) | async-done | bytes 4718608 | tf_op jit(solution)/shard_map/all_gather | solution.py:255
  597.6 44.4 %all-gather.43.cloned.1.call-done = bf16[1024,1024]{1,0:T(8,128)(2,1)} async-done(((bf16[32,1024]{1,0:T(8,128)(2,1)}), bf16[1024,1024]{1,0:T(8,128)(2,1)}) %all-gather.43.cloned.1.call-update) | async-done | bytes 2097168 | tf_op jit(solution)/shard_map/all_gather | solution.py:263
  644.4 56.1 %all-gather.45.cloned.1.call-done = bf16[1024,1024]{1,0:T(8,128)(2,1)} async-done(((bf16[32,1024]{1,0:T(8,128)(2,1)}), bf16[1024,1024]{1,0:T(8,128)(2,1)}) %all-gather.45.cloned.1.call-update) | async-done | bytes 2097168 | tf_op jit(solution)/shard_map/all_gather | solution.py:264
  702.6 56.2 %all-gather.47.cloned.1.call-done = bf16[1024,1024]{1,0:T(8,128)(2,1)} async-done(((bf16[32,1024]{1,0:T(8,128)(2,1)}), bf16[1024,1024]{1,0:T(8,128)(2,1)}) %all-gather.47.cloned.1.call-update) | async-done | bytes 2097168 | tf_op jit(solution)/shard_map/all_gather | solution.py:265
  779.0 41.8 %all-gather.27.cloned.1.call-done = bf16[3,768,768]{2,1,0:T(8,128)(2,1)} async-done(((bf16[3,24,768]{2,1,0:T(8,128)(2,1)}), bf16[3,768,768]{2,1,0:T(8,128)(2,1)}) %all-gather.27.cloned.1.call-update) | async-done | bytes 3538960 | tf_op jit(solution)/shard_map/all_gather | solution.py:258
  878.8 63.3 %all-gather.31.cloned.1.call-done = bf16[768,3072]{1,0:T(8,128)(2,1)} async-done(((bf16[24,3072]{1,0:T(8,128)(2,1)}), bf16[768,3072]{1,0:T(8,128)(2,1)}) %all-gather.31.cloned.1.call-update) | async-done | bytes 4718608 | tf_op jit(solution)/shard_map/all_gather | solution.py:260
  945.4 62.0 %all-gather.33.cloned.1.call-done = bf16[3072,768]{1,0:T(8,128)(2,1)} async-done(((bf16[96,768]{1,0:T(8,128)(2,1)}), bf16[3072,768]{1,0:T(8,128)(2,1)}) %all-gather.33.cloned.1.call-update) | async-done | bytes 4718608 | tf_op jit(solution)/shard_map/all_gather | solution.py:261
  1479.9 75.1 %reduce.110 = bf16[768,2304]{1,0:T(8,128)(2,1)S(1)} reduce(bf16[768,1,2304]{2,1,0:T(2,128)(2,1)} %bitcast.616, bf16[]{:T(256)} %broadcast.765), dimensions={1}, to_apply=%bitcast.443.reduce_sub_computation | reduce | bytes 7077890
  1570.5 66.9 %copy.258 = bf16[1,3072,768]{2,0,1:T(2,128)(2,1)} copy(bf16[1,3072,768]{2,1,0:T(8,128)(2,1)S(1)} %fusion.2) | data formatting | bytes 9437184 | tf_op jit(solution)/shard_map/convert_element_type | solution.py:20
  1637.4 48.9 %reduce.112 = bf16[3072,768]{1,0:T(8,128)(2,1)} reduce(bf16[3072,1,768]{2,1,0:T(2,128)(2,1)} %bitcast.606, bf16[]{:T(256)} %broadcast.765), dimensions={1}, to_apply=%bitcast.582.reduce_sub_computation | reduce | bytes 9437186
  1706.3 43.6 %copy.257 = bf16[1,768,3072]{2,0,1:T(2,128)(2,1)} copy(bf16[1,768,3072]{2,1,0:T(8,128)(2,1)S(1)} %fusion.3) | data formatting | bytes 9437184 | tf_op jit(solution)/shard_map/convert_element_type | solution.py:20
  1749.9 28.9 %reduce.113 = bf16[768,3072]{1,0:T(8,128)(2,1)} reduce(bf16[768,1,3072]{2,1,0:T(2,128)(2,1)} %bitcast.607, bf16[]{:T(256)} %broadcast.765), dimensions={1}, to_apply=%bitcast.581.reduce_sub_computation | reduce | bytes 9437186
  1814.9 66.9 %copy.260 = bf16[1,3072,768]{2,0,1:T(2,128)(2,1)} copy(bf16[1,3072,768]{2,1,0:T(8,128)(2,1)S(1)} %fusion) | data formatting | bytes 9437184 | tf_op jit(solution)/shard_map/convert_element_type | solution.py:20
  1881.7 48.9 %reduce.106 = bf16[3072,768]{1,0:T(8,128)(2,1)} reduce(bf16[3072,1,768]{2,1,0:T(2,128)(2,1)} %bitcast.608, bf16[]{:T(256)} %broadcast.765), dimensions={1}, to_apply=%bitcast.584.reduce_sub_computation | reduce | bytes 9437186
  1951.0 66.9 %copy.259 = bf16[1,3072,768]{2,0,1:T(2,128)(2,1)} copy(bf16[1,3072,768]{2,1,0:T(8,128)(2,1)S(1)} %fusion.1) | data formatting | bytes 9437184 | tf_op jit(solution)/shard_map/convert_element_type | solution.py:20
  2017.9 48.9 %reduce.107 = bf16[3072,768]{1,0:T(8,128)(2,1)} reduce(bf16[3072,1,768]{2,1,0:T(2,128)(2,1)} %bitcast.609, bf16[]{:T(256)} %broadcast.765), dimensions={1}, to_apply=%bitcast.583.reduce_sub_computation | reduce | bytes 9437186
  2114.4 48.9 %reduce.102 = bf16[1024,2304]{1,0:T(8,128)(2,1)} reduce(bf16[1024,1,2304]{2,1,0:T(2,128)(2,1)} %bitcast.610, bf16[]{:T(256)} %broadcast.765), dimensions={1}, to_apply=%bitcast.439.reduce_sub_computation | reduce | bytes 9437186
  2198.1 26.7 copy.199
  2224.8 37.7 %reduce.114 = bf16[1024,3072]{1,0:T(8,128)(2,1)} reduce(bf16[1024,1,3072]{2,1,0:T(2,128)(2,1)} %bitcast.605, bf16[]{:T(256)} %broadcast.765), dimensions={1}, to_apply=%bitcast.445.reduce_sub_computation | reduce | bytes 12582914
  2279.3 22.0 all-to-all-start.28
  2310.2 26.7 copy.187
  2336.9 37.7 %reduce.103 = bf16[1024,3072]{1,0:T(8,128)(2,1)} reduce(bf16[1024,1,3072]{2,1,0:T(2,128)(2,1)} %bitcast.604, bf16[]{:T(256)} %broadcast.765), dimensions={1}, to_apply=%bitcast.441.reduce_sub_computation | reduce | bytes 12582914
  2387.6 27.9 all-to-all-done.28
  2415.5 28.1 all-to-all-start.17
  (757 shorter events, 1229.5 us)
Async XLA Ops:
  8.7 199.5 %all-gather.35.cloned.1.call-start = ((), (), s32[]{:S(2)}) async-start(), calls=%async_computation.60 | async-start | bytes 2162688 | tf_op jit(solution)/shard_map/all_gather | solution.py:253
  9.4 257.1 %all-gather.37.cloned.1.call-start = ((), (), s32[]{:S(2)}) async-start(), calls=%async_computation.61 | async-start | bytes 2162688 | tf_op jit(solution)/shard_map/all_gather | solution.py:256
  10.0 314.9 %all-gather.39.cloned.1.call-start = ((), (), s32[]{:S(2)}) async-start(), calls=%async_computation.62 | async-start | bytes 2162688 | tf_op jit(solution)/shard_map/all_gather | solution.py:257
  10.6 385.3 %all-gather.41.cloned.1.call-start = ((), (), s32[]{:S(2)}) async-start(), calls=%async_computation.63 | async-start | bytes 6488064 | tf_op jit(solution)/shard_map/all_gather | solution.py:262
  11.1 441.6 %all-gather.21.cloned.1.call-start = ((), (), s32[]{:S(2)}) async-start(), calls=%async_computation.53 | async-start | bytes 1622016 | tf_op jit(solution)/shard_map/all_gather | solution.py:252
  11.9 506.3 %all-gather.23.cloned.1.call-start = ((), (), s32[]{:S(2)}) async-start(), calls=%async_computation.54 | async-start | bytes 4866048 | tf_op jit(solution)/shard_map/all_gather | solution.py:254
  12.6 571.0 %all-gather.25.cloned.1.call-start = ((), (), s32[]{:S(2)}) async-start(), calls=%async_computation.55 | async-start | bytes 4866048 | tf_op jit(solution)/shard_map/all_gather | solution.py:255
  13.4 628.6 %all-gather.43.cloned.1.call-start = ((), (), s32[]{:S(2)}) async-start(), calls=%async_computation.64 | async-start | bytes 2162688 | tf_op jit(solution)/shard_map/all_gather | solution.py:263
  14.0 686.5 %all-gather.45.cloned.1.call-start = ((), (), s32[]{:S(2)}) async-start(), calls=%async_computation.65 | async-start | bytes 2162688 | tf_op jit(solution)/shard_map/all_gather | solution.py:264
  14.7 744.1 %all-gather.47.cloned.1.call-start = ((), (), s32[]{:S(2)}) async-start(), calls=%async_computation.66 | async-start | bytes 2162688 | tf_op jit(solution)/shard_map/all_gather | solution.py:265
  15.3 805.6 %all-gather.27.cloned.1.call-start = ((), (), s32[]{:S(2)}) async-start(), calls=%async_computation.56 | async-start | bytes 3649536 | tf_op jit(solution)/shard_map/all_gather | solution.py:258
  16.0 860.7 %all-gather.29.cloned.1.call-start = ((), (), s32[]{:S(2)}) async-start(), calls=%async_computation.57 | async-start | bytes 1216512 | tf_op jit(solution)/shard_map/all_gather | solution.py:259
  16.6 925.5 %all-gather.31.cloned.1.call-start = ((), (), s32[]{:S(2)}) async-start(), calls=%async_computation.58 | async-start | bytes 4866048 | tf_op jit(solution)/shard_map/all_gather | solution.py:260
  17.2 990.2 %all-gather.33.cloned.1.call-start = ((), (), s32[]{:S(2)}) async-start(), calls=%async_computation.59 | async-start | bytes 4866048 | tf_op jit(solution)/shard_map/all_gather | solution.py:261
  173.3 227.5 %all-to-all-start.2 = ((bf16[2,100,4,128]{3,2,1,0:T(4,128)(2,1)}), bf16[2,100,4,128]{3,2,1,0:T(4,128)(2,1)S(1)}, u32[]{:S(2)}, u32[]{:S(2)}) async-start(bf16[2,100,4,128]{3,2,1,0:T(4,128)(2,1)} %copy.155), calls=%async_computation.2 | async-start | bytes 409600 | tf_op jit(solution)/shard_map/all_to_all | solution.py:100
  400.7 186.6 %all-to-all-start.6 = ((bf16[1,36,3,8,128]{4,1,2,0,3:T(8,128)(2,1)}), bf16[1,36,3,8,128]{4,1,2,0,3:T(8,128)(2,1)}, u32[]{:S(2)}, u32[]{:S(2)}) async-start(bf16[1,36,3,8,128]{4,1,2,0,3:T(8,128)(2,1)} %copy.163), calls=%async_computation.6 | async-start | bytes 491520 | tf_op jit(solution)/shard_map/all_to_all | solution.py:96
  1790.6 150.8 %all-to-all-start.27 = ((bf16[16,2,73728]{2,1,0:T(2,128)(2,1)}), bf16[16,2,73728]{2,1,0:T(2,128)(2,1)}, u32[]{:S(2)}, u32[]{:S(2)}) async-start(bf16[16,2,73728]{2,1,0:T(2,128)(2,1)} %reshape.1144), calls=%async_computation.38 | async-start | bytes 9437184 | tf_op jit(solution)/shard_map/all_to_all | solution.py:413
  2415.5 361.3 %all-to-all-start.17 = ((bf16[16,2,98304]{2,1,0:T(2,128)(2,1)}), bf16[16,2,98304]{2,1,0:T(2,128)(2,1)}, u32[]{:S(2)}, u32[]{:S(2)}) async-start(bf16[16,2,98304]{2,1,0:T(2,128)(2,1)} %reshape.1122), calls=%async_computation.18 | async-start | bytes 12582912 | tf_op jit(solution)/shard_map/all_to_all | solution.py:413
  2443.6 247.5 %reduce-scatter.53.cloned.1.call-start = ((), (), s32[]{:S(2)}) async-start(), calls=%async_computation.83 | async-start | bytes 24576
  2449.7 282.8 %reduce-scatter.39.cloned.1.call-start = ((), (), s32[]{:S(2)}) async-start(), calls=%async_computation.76 | async-start | bytes 110592 | tf_op jit(solution)/shard_map/reduce_scatter | solution.py:418
  2460.6 273.3 %reduce-scatter.25.cloned.1.call-start = ((), (), s32[]{:S(2)}) async-start(), calls=%async_computation.69 | async-start | bytes 147456 | tf_op jit(solution)/shard_map/reduce_scatter | solution.py:418
  2476.4 288.0 %reduce-scatter.49.cloned.1.call-start = ((), (), s32[]{:S(2)}) async-start(), calls=%async_computation.81 | async-start | bytes 196608 | tf_op jit(solution)/shard_map/reduce_scatter | solution.py:418
  2493.9 272.0 %reduce-scatter.47.cloned.1.call-start = ((), (), s32[]{:S(2)}) async-start(), calls=%async_computation.80 | async-start | bytes 196608 | tf_op jit(solution)/shard_map/reduce_scatter | solution.py:418
  2511.5 255.9 %reduce-scatter.51.cloned.1.call-start = ((), (), s32[]{:S(2)}) async-start(), calls=%async_computation.82 | async-start | bytes 196608 | tf_op jit(solution)/shard_map/reduce_scatter | solution.py:418
  2529.1 239.8 %reduce-scatter.27.cloned.1.call-start = ((), (), s32[]{:S(2)}) async-start(), calls=%async_computation.70 | async-start | bytes 196608 | tf_op jit(solution)/shard_map/reduce_scatter | solution.py:418
  2547.1 223.3 %reduce-scatter.35.cloned.1.call-start = ((), (), s32[]{:S(2)}) async-start(), calls=%async_computation.74 | async-start | bytes 196608 | tf_op jit(solution)/shard_map/reduce_scatter | solution.py:418
  2564.7 207.2 %reduce-scatter.33.cloned.1.call-start = ((), (), s32[]{:S(2)}) async-start(), calls=%async_computation.73 | async-start | bytes 196608 | tf_op jit(solution)/shard_map/reduce_scatter | solution.py:418
  2582.2 191.2 %reduce-scatter.37.cloned.1.call-start = ((), (), s32[]{:S(2)}) async-start(), calls=%async_computation.75 | async-start | bytes 331776 | tf_op jit(solution)/shard_map/reduce_scatter | solution.py:418
  2595.1 180.0 %reduce-scatter.41.cloned.1.call-start = ((), (), s32[]{:S(2)}) async-start(), calls=%async_computation.77 | async-start | bytes 442368 | tf_op jit(solution)/shard_map/reduce_scatter | solution.py:418
  2618.4 187.2 %reduce-scatter.43.cloned.1.call-start = ((), (), s32[]{:S(2)}) async-start(), calls=%async_computation.78 | async-start | bytes 442368 | tf_op jit(solution)/shard_map/reduce_scatter | solution.py:418
  2642.9 164.3 %reduce-scatter.31.cloned.1.call-start = ((), (), s32[]{:S(2)}) async-start(), calls=%async_computation.72 | async-start | bytes 442368 | tf_op jit(solution)/shard_map/reduce_scatter | solution.py:418
  2666.3 142.5 %reduce-scatter.29.cloned.1.call-start = ((), (), s32[]{:S(2)}) async-start(), calls=%async_computation.71 | async-start | bytes 442368 | tf_op jit(solution)/shard_map/reduce_scatter | solution.py:418
  (181 other events, 12800.1 us)
Sparse Core Ops, SparseCore 0:
  11.0 66.3 all-gather.18
  80.4 69.1 all-gather.16
  152.7 55.4 all-gather.34
  211.1 55.3 all-gather.36
  269.5 55.3 all-gather.38
  327.8 67.9 all-gather.40
  398.7 53.9 all-gather.20
  455.7 62.5 all-gather.22
  521.2 62.4 all-gather.24
  586.6 55.3 all-gather.42
  645.1 55.3 all-gather.44
  703.4 55.3 all-gather.46
  761.8 59.0 all-gather.26
  823.6 53.0 all-gather.28
  879.5 62.5 all-gather.30
  944.9 62.4 all-gather.32
  2449.8 11.5 reduce-scatter.52
  2476.7 11.5 reduce-scatter.24
  2494.0 12.0 reduce-scatter.48
  2511.6 11.9 reduce-scatter.46
  2529.2 11.9 reduce-scatter.50
  2547.2 11.8 reduce-scatter.26
  2564.8 11.8 reduce-scatter.34
  2582.4 11.8 reduce-scatter.32
  2596.9 11.2 reduce-scatter.36
  2618.5 13.6 reduce-scatter.40
  2643.0 13.6 reduce-scatter.42
  2666.5 13.6 reduce-scatter.30
  2689.9 13.7 reduce-scatter.28
  2721.8 13.6 reduce-scatter.20
  2764.4 14.7 reduce-scatter.44
  2805.7 14.7 reduce-scatter.22
  (1 shorter events, 9.9 us)
where the time goes:
time: 2850 us; the launch traced here: 2830 us
  waiting for transfers between devices  1040 us (36%)
  local copies, waits for them, and re-layouts  811 us (28%)
  other arithmetic  557 us (20%)
  starting transfers between devices  272 us (10%)
  matrix products  125 us (4%)
    unnamed x19, other arithmetic  478 us
    unnamed x355, local copies, waits for them, and re-layouts  406 us
    convert_element_type x18, local copies, waits for them, and re-layouts, short(): return part.astype(jnp.bfloat16) if part.dtype == jnp.float32 else part  370 us
    all_to_all x18, starting transfers between devices, on_device(): lax.all_to_all(as_sent(to_rows(all_grads, all_dims)), 'dp', split_axis=1,...  203 us
    all_to_all x18, waiting for transfers between devices, on_device(): lax.all_to_all(as_sent(to_rows(all_grads, all_dims)), 'dp', split_axis=1,...  152 us
    all_gather x1, waiting for transfers between devices, on_device(): lax.all_gather(self_image_proj, ('dp', 'seq'), axis=1, tiled=True)  68.6 us
    all_gather x1, waiting for transfers between devices, on_device(): lax.all_gather(cross_image_proj, ('dp', 'seq'), axis=1, tiled=True)  64.2 us
    all_gather x1, waiting for transfers between devices, on_device(): lax.all_gather(cross_text_up, ('dp', 'seq'), axis=0, tiled=True)  63.3 us
  transfers between devices with their start and end apart: 67, of which 37 were waited for; matrix products, arithmetic and copies ran while one was open for 52% of the time, Pallas kernels for 0%

commit v1 on v0

v1 whole, which is shorter than its diff:
```python
import jax
import jax.numpy as jnp
from jax import lax
from jax.experimental import pallas as pl
from jax.experimental.pallas import tpu as pltpu
from jax.sharding import PartitionSpec as P

H_T = 12
H_V = 8
H_C = 8

EPSILON = 1e-05
NEGATIVE = -1000000000.0
FLOAT = jnp.float32
BFLOAT = jnp.bfloat16
ALL = ("dp", "seq")
FREE = pl.CostEstimate(flops=0, bytes_accessed=0, transcendentals=0)


def device_bits():
    return (lax.axis_size("dp").bit_length() - 1, lax.axis_size("seq").bit_length() - 1)


def my_index():
    return lax.axis_index("dp") * lax.axis_size("seq") + lax.axis_index("seq")


def swap(block, bit):
    size = lax.axis_size("dp") * lax.axis_size("seq")
    return lax.ppermute(block, ALL, [(i, i ^ (1 << bit)) for i in range(size)])


def orders():
    dp_bits, seq_bits = device_bits()
    total = dp_bits + seq_bits
    core = seq_bits
    rest = [b for b in range(total) if b != core]
    seq_first = [core] + rest
    dp_first = [core] + rest[1:2] + rest[0:1] + rest[2:]
    far_first = [core] + rest[2:3] + rest[1:2] + rest[0:1] + rest[3:]
    return seq_first, dp_first, far_first


def take(block, which):
    return lax.dynamic_index_in_dim(block, which, 0, keepdims=False)


def add_low(left, right):
    return (left.astype(FLOAT) + right.astype(FLOAT)).astype(BFLOAT)


def join_blocks(held, came, order, splits):
    count, rows, width = held.shape
    bits = len(order)
    near = order.index(0)
    low = 1 << near
    pairs = (count // (2 * low), 2, low, rows, width)

    def out_index(j, at):
        place = jnp.int32(0)
        for k, b in enumerate(order[:-1]):
            if b != 0:
                bit = lax.rem(lax.shift_right_logical(j, k if k < near else k - 1), 2)
                place = place + lax.shift_left(bit, b)
        block = jnp.bitwise_xor(at[0], place)
        return (lax.shift_right_logical(block, 2), 0, 0, 0, 0)

    def body(at_ref, held_ref, came_ref, *outs):
        side = lax.rem(lax.shift_right_logical(at_ref[0], 1), 2)
        mine = lax.rem(at_ref[0], 2)
        start = 0
        for out, many in zip(outs, splits):
            for step in range(2):
                y = jnp.bitwise_xor(mine, step)
                out[0, side, y] = held_ref[0, step, 0, start : start + many]
                out[0, 1 - side, y] = came_ref[0, step, 0, start : start + many]
            start += many

    def in_index(j, at):
        return (lax.div(j, low), 0, lax.rem(j, low), 0, 0)

    outs = pl.pallas_call(
        body,
        grid_spec=pltpu.PrefetchScalarGridSpec(
            num_scalar_prefetch=1,
            grid=(count // 2,),
            in_specs=[pl.BlockSpec((1, 2, 1, rows, width), in_index)] * 2,
            out_specs=[pl.BlockSpec((1, 2, 2, many, width), out_index) for many in splits],
        ),
        out_shape=[
            jax.ShapeDtypeStruct((1 << (bits - 2), 2, 2, many, width), held.dtype) for many in splits
        ],
        compiler_params=pltpu.CompilerParams(vmem_limit_bytes=32 * 1024 * 1024),
        cost_estimate=FREE,
    )(my_index().astype(jnp.int32).reshape(1), held.reshape(pairs), came.reshape(pairs))
    return [out.reshape(-1, width) for out in outs]


class Gather:
    def __init__(self, shard, order, splits=None):
        self.order = order
        self.held = shard[None]
        self.splits = splits or [shard.shape[0]]
        self.step = 0

    def start(self):
        self.came = swap(self.held, self.order[self.step])
        self.step += 1

    def absorb(self):
        if self.step == len(self.order):
            self.full = join_blocks(self.held, self.came, self.order, self.splits)
        else:
            self.held = jnp.concatenate([self.held, self.came], axis=0)


def close_round(movers, *arrays):
    came = [m.came for m in movers]
    came, arrays = lax.optimization_barrier((came, arrays))
    for m, block in zip(movers, came):
        m.came = block
    for m in movers:
        m.absorb()
    return arrays


def sides_of(order):
    at = my_index()
    return [lax.rem(lax.shift_right_logical(at, b), 2) for b in order]


def panels_of(other, width):
    return other.shape[1] // width


def rows_in_order(rows, first, own, size, order):
    total = len(order)
    part = rows[:, first : first + own * size]
    split = part.reshape((part.shape[0],) + (2,) * total + (own,))
    axes = [1 + (total - 1 - b) for b in order] + [1 + total, 0]
    return split.transpose(axes).reshape(size * own, part.shape[0])


def pack_plain(items, width, order):
    size = 1 << len(order)
    parts = []
    for rows, first, span, other in items:
        own = span // size
        block = mm(rows_in_order(rows, first, own, size, order), other).astype(BFLOAT)
        block = block.reshape(size, own, panels_of(other, width), width).transpose(0, 2, 1, 3)
        parts.append(block.reshape(size, -1, width))
    return jnp.concatenate(parts, axis=1)


def pack_kernel(items, width, order, natural):
    total = len(order)
    size = 1 << total
    groups = size // 4
    core_side = sides_of(order[:1])[0]
    owns = [span // size for rows, first, span, other in items]
    panels = [panels_of(other, width) for rows, first, span, other in items]
    count = len(items)
    total_rows = sum(o * p for o, p in zip(owns, panels))
    lefts, left_specs = [], []
    for (rows, first, span, other), own in zip(items, owns):
        length = rows.shape[0]
        at = first // (4 * own)
        if (4 * own) % 128 == 0:
            lefts.append(rows)
            left_specs.append(pl.BlockSpec((length, 4 * own), lambda g, core, at=at: (0, at + g)))
        else:
            lefts.append(rows.reshape(length, -1, 4 * own).transpose(1, 0, 2))
            left_specs.append(pl.BlockSpec((None, length, 4 * own), lambda g, core, at=at: (at + g, 0, 0)))
    rights, used = [], []
    for item in items:
        match = [i for i, other in enumerate(rights) if other is item[3]]
        if not match:
            rights.append(item[3])
        used.append(match[0] if match else len(rights) - 1)
    right_specs = [pl.BlockSpec(other.shape, lambda g, core: (0, 0)) for other in rights]
    rest = order[1:]

    def out_index(g, core):
        return tuple(0 if b == 0 else lax.rem(lax.shift_right_logical(g, b - 2), 2) for b in rest) + (0, 0)

    out_shape = (2,) * len(rest) + (total_rows, width)
    out_block = tuple(2 if b == 0 else None for b in rest) + (total_rows, width)
    outs = 1 if natural else 2
    if natural:
        out_shape = (size, total_rows, width)
        out_block = (4, total_rows, width)
        out_index = lambda g, core: (g, 0, 0)

    def body(core_ref, *refs):
        left_refs = refs[:count]
        right_refs = refs[count : count + len(rights)]
        pack_refs = refs[count + len(rights) : count + len(rights) + outs]
        held = refs[count + len(rights) + outs :]
        core = core_ref[0]
        for left, right, keepers in zip(left_refs, used, held):
            keepers[...] = t_mm(left[...], right_refs[right][...])
        if natural:
            targets = [(pack_refs[0], i, i) for i in range(4)]
        else:
            targets = [(pack_refs[0], i, 2 * (1 - core) + i) for i in range(2)]
            targets += [(pack_refs[1], i, 2 * core + i) for i in range(2)]
        for ref, near, which in targets:
            pieces = []
            for keepers, own, many in zip(held, owns, panels):
                start = which * own if natural else pl.multiple_of(which * own, 8)
                for p in range(many):
                    pieces.append(keepers[pl.ds(start, own), p * width : (p + 1) * width])
            ref[near] = jnp.concatenate(pieces, axis=0).astype(BFLOAT)

    flops = sum(2 * rows.shape[0] * span * other.shape[1] for rows, first, span, other in items)
    packed = pl.pallas_call(
        body,
        grid_spec=pltpu.PrefetchScalarGridSpec(
            num_scalar_prefetch=1,
            grid=(groups,),
            in_specs=left_specs + right_specs,
            out_specs=[pl.BlockSpec(out_block, out_index)] * outs,
            scratch_shapes=[
                pltpu.VMEM((4 * own, other.shape[1]), FLOAT)
                for own, (rows, first, span, other) in zip(owns, items)
            ],
        ),
        out_shape=[jax.ShapeDtypeStruct(out_shape, BFLOAT)] * outs,
        compiler_params=pltpu.CompilerParams(vmem_limit_bytes=32 * 1024 * 1024),
        cost_estimate=FREE,
    )(core_side.astype(jnp.int32).reshape(1), *lefts, *rights)
    if natural:
        return packed[0]
    flat = (size // 2, total_rows, width)
    return packed[0].reshape(flat), packed[1].reshape(flat)


def aligned_items(items, size):
    return all(span % (8 * size) == 0 for rows, first, span, other in items)


def pack_natural(items, width):
    bits = sum(device_bits())
    if aligned_items(items, 1 << bits):
        return pack_kernel(items, width, list(range(bits)), True)
    return pack_plain(items, width, list(range(bits))[::-1])


def pack(items, width, order):
    size = 1 << len(order)
    if aligned_items(items, size) and order[0] == 1:
        return pack_kernel(items, width, order, False)
    block = pack_plain(items, width, order)
    block = block.reshape((2, size // 2) + block.shape[1:])
    at = sides_of(order[:1])[0]
    return take(block, 1 - at), take(block, at)


class Whole:
    def __init__(self, items, width):
        self.block = pack_natural(items, width)

    def launch(self):
        flat = self.block.reshape(-1, self.block.shape[-1])
        self.sum = lax.psum_scatter(flat, ALL, scatter_dimension=0, tiled=True)

    def finish(self):
        return self.sum.astype(FLOAT)


class Chunk:
    def __init__(self, items, width, order):
        self.order = order
        self.sides = sides_of(order)
        self.send, self.keep = pack(items, width, order)
        self.step = 0

    def start(self):
        self.came = swap(self.send, self.order[self.step])
        self.step += 1

    def absorb(self):
        if self.step == len(self.order):
            self.full = (self.came.astype(FLOAT) + self.keep.astype(FLOAT))[0]
            return
        half = self.came.shape[0] // 2
        came = self.came.reshape((2, half) + self.came.shape[1:])
        keep = self.keep.reshape((2, half) + self.keep.shape[1:])
        at = self.sides[self.step]
        self.send = add_low(take(came, 1 - at), take(keep, 1 - at))
        self.keep = add_low(take(came, at), take(keep, at))


class Small(Chunk):
    def __init__(self, block, order):
        total = len(order)
        tail = block.shape[1:]
        held = block.reshape((2,) * total + tail)
        held = held.transpose([total - 1 - b for b in order] + [total + i for i in range(len(tail))])
        held = held.reshape((2, -1) + tail)
        self.order = order
        self.sides = sides_of(order)
        self.send, self.keep = take(held, 1 - self.sides[0]), take(held, self.sides[0])
        self.step = 0


def mm(left, right):
    return jnp.dot(left, right, preferred_element_type=FLOAT)


def mm_t(left, right):
    return lax.dot_general(left, right, (((1,), (1,)), ((), ())), preferred_element_type=FLOAT)


def t_mm(left, right):
    return lax.dot_general(left, right, (((0,), (0,)), ((), ())), preferred_element_type=FLOAT)


def layer_norm(stream, gain_vec):
    center = stream - jnp.mean(stream, axis=-1, keepdims=True)
    spread = jnp.mean(center * center, axis=-1, keepdims=True)
    return center * lax.rsqrt(spread + EPSILON) * gain_vec


def norm_back(stream, gain_vec, upstream):
    center = stream - jnp.mean(stream, axis=-1, keepdims=True)
    scale = lax.rsqrt(jnp.mean(center * center, axis=-1, keepdims=True) + EPSILON)
    unit = center * scale
    weighted = upstream * gain_vec
    inner = jnp.mean(weighted * unit, axis=-1, keepdims=True)
    grad = (weighted - jnp.mean(weighted, axis=-1, keepdims=True) - unit * inner) * scale
    return grad, (upstream * unit).astype(BFLOAT)


def gelu_back(upper, upstream):
    unused, pullback = jax.vjp(jax.nn.gelu, upper)
    return pullback(upstream)[0]


def head_blocks(width, heads):
    size = width // heads
    block = max(size, 128)
    return [(h * size // block * block, block, h * size % block, size) for h in range(heads)]


def only_head(value, start, size):
    if size == value.shape[1]:
        return value
    lane = lax.broadcasted_iota(jnp.int32, value.shape, 1)
    return jnp.where((lane >= start) & (lane < start + size), value, jnp.zeros_like(value))


def head_probs(query, key, size, valid):
    scores = mm_t(query, key) * (size ** (-0.5))
    if valid is not None:
        lane = lax.broadcasted_iota(jnp.int32, scores.shape, 1)
        scores = jnp.where(lane < valid, scores, NEGATIVE)
    expo = jnp.exp(scores - jnp.max(scores, axis=-1, keepdims=True))
    return expo / jnp.sum(expo, axis=-1, keepdims=True)


def attend_block(q_ref, k_ref, v_ref, q_at, k_at, v_at, out_ref, heads, valid):
    width = out_ref.shape[1]
    parts = {}
    for base, block, start, size in head_blocks(width, heads):
        q = only_head(q_ref[:, q_at + base : q_at + base + block], start, size)
        k = k_ref[:, k_at + base : k_at + base + block]
        v = only_head(v_ref[:, v_at + base : v_at + base + block], start, size)
        part = mm(head_probs(q, k, size, valid).astype(BFLOAT), v)
        parts[base] = part if base not in parts else parts[base] + part
        if start + size == block:
            out_ref[:, base : base + block] = parts[base].astype(BFLOAT)


def attend_block_back(
    q_ref, k_ref, v_ref, q_at, k_at, v_at, g_ref, dq_ref, dk_ref, dv_ref, heads, valid
):
    width = g_ref.shape[1]
    parts = {}
    for base, block, start, size in head_blocks(width, heads):
        q = only_head(q_ref[:, q_at + base : q_at + base + block], start, size)
        k = only_head(k_ref[:, k_at + base : k_at + base + block], start, size)
        v = v_ref[:, v_at + base : v_at + base + block]
        g = only_head(g_ref[:, base : base + block], start, size)
        probs = head_probs(q, k, size, valid)
        grad_probs = mm_t(g, v)
        inner = jnp.sum(grad_probs * probs, axis=-1, keepdims=True)
        grad_scores = (probs * (grad_probs - inner)).astype(BFLOAT)
        scale = size ** (-0.5)
        news = (mm(grad_scores, k) * scale, t_mm(grad_scores, q) * scale, t_mm(probs.astype(BFLOAT), g))
        if base in parts:
            news = tuple(x + y for x, y in zip(parts[base], news))
        parts[base] = news
        if start + size == block:
            for ref, at, new in zip((dq_ref, dk_ref, dv_ref), (q_at, k_at, v_at), news):
                ref[:, at + base : at + base + block] = new.astype(BFLOAT)


def vmem_call(body, count, outs, scalar, flops, *operands):
    return pl.pallas_call(
        body,
        in_specs=[pl.BlockSpec(memory_space=pltpu.SMEM)] + [pl.BlockSpec(memory_space=pltpu.VMEM)] * count,
        out_specs=[pl.BlockSpec(memory_space=pltpu.VMEM)] * len(outs),
        out_shape=[jax.ShapeDtypeStruct(shape, BFLOAT) for shape in outs],
        compiler_params=pltpu.CompilerParams(vmem_limit_bytes=32 * 1024 * 1024),
        cost_estimate=FREE,
    )(scalar, *operands)


def cross_attend(text, image, length):
    width = text.shape[1] // 3

    def body(len_ref, text_ref, image_ref, t_ref, i_ref):
        attend_block(text_ref, image_ref, image_ref, 0, width, 2 * width, t_ref, H_C, None)
        attend_block(image_ref, text_ref, text_ref, 0, width, 2 * width, i_ref, H_C, len_ref[0])

    flops = 8 * text.shape[0] * image.shape[0] * width * 8
    outs = [(text.shape[0], width), (image.shape[0], width)]
    return vmem_call(body, 2, outs, length, flops, text, image)


def cross_attend_back(text, image, length, t_grad, i_grad):
    width = text.shape[1] // 3

    def body(len_ref, text_ref, image_ref, tg_ref, ig_ref, dt_ref, di_ref):
        attend_block_back(
            text_ref, image_ref, image_ref, 0, width, 2 * width, tg_ref, dt_ref, di_ref, di_ref, H_C, None
        )
        attend_block_back(
            image_ref, text_ref, text_ref, 0, width, 2 * width, ig_ref, di_ref, dt_ref, dt_ref, H_C, len_ref[0]
        )

    flops = 20 * text.shape[0] * image.shape[0] * width * 8
    return vmem_call(body, 4, [text.shape, image.shape], length, flops, text, image, t_grad, i_grad)


def self_attend(packed, heads, length, masked):
    width = packed.shape[1] // 3

    def body(len_ref, ref, out_ref):
        attend_block(ref, ref, ref, 0, width, 2 * width, out_ref, heads, len_ref[0] if masked else None)

    flops = 4 * packed.shape[0] * packed.shape[0] * width * 8
    return vmem_call(body, 1, [(packed.shape[0], width)], length, flops, packed)[0]


def self_attend_back(packed, heads, length, masked, grad):
    width = packed.shape[1] // 3

    def body(len_ref, ref, g_ref, d_ref):
        attend_block_back(
            ref, ref, ref, 0, width, 2 * width, g_ref, d_ref, d_ref, d_ref, heads, len_ref[0] if masked else None
        )

    flops = 10 * packed.shape[0] * packed.shape[0] * width * 8
    return vmem_call(body, 2, [packed.shape], length, flops, packed, grad)[0]


def tail_forward(residual, attn_low, out_mat, up_mat, down_mat, gain_pair):
    first_sum = residual + mm(attn_low, out_mat)
    first_norm = layer_norm(first_sum, gain_pair[0])
    hidden_low = first_norm.astype(BFLOAT)
    upper = mm(hidden_low, up_mat)
    active = jax.nn.gelu(upper).astype(BFLOAT)
    second_sum = first_norm + mm(active, down_mat)
    return layer_norm(second_sum, gain_pair[1]), (first_sum, hidden_low, upper, active, second_sum)


def tail_backward(grad_result, kept, attn_low, out_mat, up_mat, down_mat, gain_pair, down_natural):
    first_sum, hidden_low, upper, active, second_sum = kept
    grad_second, gain_two = norm_back(second_sum, gain_pair[1], grad_result)
    low = grad_second.astype(BFLOAT)
    grad_down = whole_item(active, low) if down_natural else whole_item(low, active)
    grad_upper = gelu_back(upper, mm_t(low, down_mat)).astype(BFLOAT)
    grad_up = whole_item(grad_upper, hidden_low)
    grad_norm = grad_second + mm_t(grad_upper, up_mat)
    grad_first, gain_one = norm_back(first_sum, gain_pair[0], grad_norm)
    grad_first_low = grad_first.astype(BFLOAT)
    grad_out = whole_item(attn_low, grad_first_low)
    grad_attn = mm_t(grad_first_low, out_mat).astype(BFLOAT)
    return grad_first, grad_attn, [grad_down, grad_up, grad_out], [gain_one, gain_two]


def project(stream_low, proj):
    return mm(stream_low, proj).astype(BFLOAT)


def whole_item(rows, other):
    return (rows, 0, rows.shape[1], other)


def third_items(packed, other):
    span = packed.shape[1] // 3
    return [(packed, e * span, span, other) for e in range(3)]


def side(shards):
    return jnp.concatenate(shards, axis=1)


def on_device(
    text_input,
    image_input,
    caption_lengths,
    text_cotangent,
    image_cotangent,
    cross_text_proj,
    cross_image_proj,
    cross_text_out,
    cross_image_out,
    cross_text_up,
    cross_text_down,
    cross_image_up,
    cross_image_down,
    self_text_proj,
    self_text_out,
    self_text_up,
    self_text_down,
    self_image_proj,
    self_image_out,
    self_image_up,
    self_image_down,
    text_gains,
    image_gains,
):
    d_t = text_input.shape[2]
    d_v = image_input.shape[2]
    co = cross_text_proj.shape[2]
    ff_t = cross_text_up.shape[1]
    n_text = text_input.shape[1]

    size = lax.axis_size("dp") * lax.axis_size("seq")
    bits = sum(device_bits())
    by_permute = size == 1 << bits and all(
        m.shape[-2] % 8 == 0 for m in (cross_text_out, cross_text_down, self_text_down)
    )

    def gather_columns(parts):
        return lax.all_gather(side(parts), ALL, axis=0, tiled=True)

    own_t, own_v = d_t // size, d_v // size
    own_f, own_c = ff_t // size, co // size
    text_parts = list(cross_text_proj) + [cross_text_up] + list(self_text_proj)
    text_wide = gather_columns(text_parts + [self_text_out, self_text_up])
    image_parts = [cross_image_out, cross_image_up, cross_image_down] + list(self_image_proj)
    image_wide = gather_columns(image_parts + [self_image_out, self_image_up, self_image_down])
    w_ctp = text_wide[:, : 3 * co]

    high = list(range(3, bits))[::-1]
    x_first = high + [2, 0, 1]
    y_first = high + [0, 2, 1]
    shards = [
        (side(list(cross_image_proj)), y_first, None),
        (jnp.concatenate([cross_text_down, cross_text_out], axis=0), x_first, [own_f, own_c]),
        (self_text_down, x_first, None),
    ]

    panel = 128
    my_len = lax.dynamic_index_in_dim(caption_lengths, lax.axis_index("seq"), 0, keepdims=True)
    x_t = text_input[0]
    x_v = image_input[0]

    if by_permute:
        movers = [Gather(*item) for item in shards]
        for turn_at in range(bits):
            active = movers[:2] + ([movers[2]] if turn_at >= 2 else [])
            for m in active:
                m.start()
            close_round(active)
        w_cip = movers[0].full[0]
        w_ctd, w_cto = movers[1].full
        movers[2].start()
        t_packed = project(x_t, w_ctp)
        i_packed = project(x_v, w_cip)
        t_attn, i_attn = cross_attend(t_packed, i_packed, my_len)
        t_attn, i_attn = close_round(movers[2:], t_attn, i_attn)
        movers[2].start()
    else:
        full = [lax.all_gather(shard, ALL, axis=0) for shard, order, splits in shards]
        w_ctd, w_cto = full[1][:, :own_f], full[1][:, own_f:]
        w_cip, w_ctd, w_cto, w_std = (w.reshape(-1, w.shape[-1]) for w in (full[0], w_ctd, w_cto, full[2]))
        t_packed = project(x_t, w_ctp)
        i_packed = project(x_v, w_cip)
        t_attn, i_attn = cross_attend(t_packed, i_packed, my_len)

    w_ctu = text_wide[:, 3 * co : 3 * co + ff_t]
    text_self = text_wide[:, 3 * co + ff_t :]
    w_stp, w_sto, w_stu = text_self[:, : 3 * d_t], text_self[:, 3 * d_t : 4 * d_t], text_self[:, 4 * d_t :]

    def halving(*picks):
        return [1] + list(picks) + [b for b in range(bits) if b != 1 and b not in picks]

    t_cross, t_kept = tail_forward(x_t.astype(FLOAT), t_attn, w_cto, w_ctu, w_ctd, text_gains[0:2])
    t_low = t_cross.astype(BFLOAT)
    if by_permute:
        t_cross, t_kept = close_round(movers[2:], t_cross, t_kept)
        w_std = movers[2].full[0]
        t_low = t_cross.astype(BFLOAT)
    st_packed = project(t_low, w_stp)
    st_attn = self_attend(st_packed, H_T, my_len, True)
    t_final, st_kept = tail_forward(t_cross, st_attn, w_sto, w_stu, w_std, text_gains[2:4])
    t_res, t_ga, t_pairs, t_gain_s = tail_backward(
        text_cotangent[0].astype(FLOAT), st_kept, st_attn, w_sto, w_stu, w_std, text_gains[2:4], False
    )
    c1t = Whole(t_pairs, d_t)
    c1t.block, t_ga, t_res, i_attn = close_round([], c1t.block, t_ga, t_res, i_attn)
    c1t.launch()
    st_grads = self_attend_back(st_packed, H_T, my_len, True, t_ga)
    t_back = t_res + mm_t(st_grads, w_stp)
    c2t = Chunk(third_items(st_grads, t_low), d_t, halving(2, 3, 0))
    c2t.send, c2t.keep, t_back, i_attn = close_round([], c2t.send, c2t.keep, t_back, i_attn)

    w_cio, w_ciu, w_cid = (image_wide[:, i * d_v : (i + 1) * d_v] for i in range(3))
    w_sip = image_wide[:, 3 * d_v : 6 * d_v]
    w_sio, w_siu, w_sid = (image_wide[:, (6 + i) * d_v : (7 + i) * d_v] for i in range(3))

    c2t.start()
    i_cross, i_kept = tail_forward(x_v.astype(FLOAT), i_attn, w_cio, w_ciu, w_cid, image_gains[0:2])
    i_low = i_cross.astype(BFLOAT)
    si_packed = project(i_low, w_sip)
    si_attn = self_attend(si_packed, H_V, my_len, False)
    i_final, si_kept = tail_forward(i_cross, si_attn, w_sio, w_siu, w_sid, image_gains[2:4])
    i_res, i_ga, i_pairs, i_gain_s = tail_backward(
        image_cotangent[0].astype(FLOAT), si_kept, si_attn, w_sio, w_siu, w_sid, image_gains[2:4], False
    )
    c1i = Chunk(i_pairs, d_v, halving(0, 2))
    c1i.send, c1i.keep, i_ga, i_res, t_back = close_round(
        [c2t], c1i.send, c1i.keep, i_ga, i_res, t_back
    )

    c2t.start()
    c1i.start()
    si_grads = self_attend_back(si_packed, H_V, my_len, False, i_ga)
    i_back = i_res + mm_t(si_grads, w_sip)
    c2i = Chunk(third_items(si_grads, i_low), d_v, halving(3, 0, 2))
    c2i.send, c2i.keep, i_back, t_back = close_round(
        [c2t, c1i], c2i.send, c2i.keep, i_back, t_back
    )

    for m in (c1i, c2i, c2t):
        m.start()
    t_res, t_ga, t_pairs, t_gain_c = tail_backward(
        t_back, t_kept, t_attn, w_cto, w_ctu, w_ctd, text_gains[0:2], True
    )
    c3a = Chunk(t_pairs[:1], d_t, halving(2, 0))
    c3a.send, c3a.keep, t_res, t_ga, i_back = close_round(
        [c1i, c2i, c2t], c3a.send, c3a.keep, t_res, t_ga, i_back
    )

    for m in (c2i, c1i, c2t, c3a):
        m.start()
    i_res, i_ga, i_pairs, i_gain_c = tail_backward(
        i_back, i_kept, i_attn, w_cio, w_ciu, w_cid, image_gains[0:2], True
    )
    c3b = Whole(t_pairs[1:] + i_pairs, 2 * panel)
    c3b.block, i_res, i_ga, t_ga = close_round([c2i, c1i, c2t, c3a], c3b.block, i_res, i_ga, t_ga)
    c3b.launch()

    for m in (c3a, c2i, c1i, c2t):
        m.start()
    t_grads, i_grads = cross_attend_back(t_packed, i_packed, my_len, t_ga, i_ga)
    t_grads, i_grads = close_round([c3a, c2i, c1i, c2t], t_grads, i_grads)

    for m in (c3a, c2i, c1i):
        m.start()

    def gain_item(products):
        rows = jnp.concatenate(products, axis=0)
        which = jnp.arange(rows.shape[0])[:, None] // products[0].shape[0]
        return whole_item(rows, (which == jnp.arange(panel)[None, :]).astype(BFLOAT))

    c4t = Chunk(third_items(t_grads, x_t) + [gain_item(t_gain_c + t_gain_s)], panel, halving(2, 0))
    c4i = Chunk(third_items(i_grads, x_v) + [gain_item(i_gain_c + i_gain_s)], panel, halving(0, 2))
    c4t.send, c4t.keep, c4i.send, c4i.keep, t_grads, i_grads = close_round(
        [c3a, c2i], c4t.send, c4t.keep, c4i.send, c4i.keep, t_grads, i_grads
    )

    c4t.start()
    c4i.start()
    t_grads, i_grads = close_round([c4t, c4i, c1i], t_grads, i_grads)
    for m in (c4t, c4i, c3a, c2i):
        m.start()
    text_input_grad = t_res + mm_t(t_grads, w_ctp)
    image_input_grad = i_res + mm_t(i_grads, w_cip)
    text_input_grad, image_input_grad, c1t.sum = close_round(
        [c4t, c4i, c3a, c2i], text_input_grad, image_input_grad, c1t.sum
    )
    for m in (c4t, c4i, c3a):
        m.start()
    close_round([c4t, c4i, c3a])
    for last_turn in range(2, bits - 1):
        for m in (c4t, c4i):
            m.start()
        if last_turn == bits - 2:
            (c3b.sum,) = close_round([c4t, c4i], c3b.sum)
        else:
            close_round([c4t, c4i])
    for m in (c1i, c2t, c2i, c3a, c4t, c4i):
        while m.step < bits:
            m.start()
            m.absorb()

    def cut(block, rows):
        out, at = [], 0
        for r in rows:
            out.append(block[at : at + r])
            at += r
        return out

    def widen(block, rows, width):
        wide = block.shape[1]
        return block.reshape(width // wide, rows, wide).transpose(1, 0, 2).reshape(rows, width)

    def thirds(block, rows, width):
        many = rows * (width // panel)
        return jnp.concatenate(
            [widen(block[e * many : (e + 1) * many], rows, width) for e in range(3)], axis=0
        )

    g_std, g_stu, g_sto = cut(c1t.finish(), (ff_t // d_t * own_t, own_f, own_t))
    g_sid, g_siu, g_sio = cut(c1i.full, (own_v,) * 3)
    g_ctd = c3a.full
    kinds = [(own_f, d_t), (own_c, d_t)] + [(own_v, d_v)] * 3
    parts = cut(c3b.finish(), [rows * (width // (2 * panel)) for rows, width in kinds])
    g_ctu, g_cto, g_cid, g_ciu, g_cio = (widen(p, *kind) for p, kind in zip(parts, kinds))
    g_std = g_std.reshape(ff_t // d_t, own_t, d_t).transpose(1, 0, 2).reshape(own_t, ff_t)
    g_stp, g_sip = c2t.full, c2i.full
    g_ctp, g_cip = thirds(c4t.full, own_c, d_t), thirds(c4i.full, own_c, d_v)
    t_gain = c4t.full[-own_t:, :4].T
    i_gain = c4i.full[-own_v:, :4].T

    def by_three(rows):
        return rows.reshape(3, rows.shape[0] // 3, rows.shape[1]).transpose(0, 2, 1)

    o_stu, o_ctu, o_ctd = g_stu.T, g_ctu.T, g_ctd
    o_std, o_sto = g_std.T, g_sto
    o_stp = by_three(g_stp)
    o_sid, o_siu, o_sio = g_sid.T, g_siu.T, g_sio
    o_sip = by_three(g_sip)
    o_cid, o_ciu, o_cio, o_cto = g_cid, g_ciu.T, g_cio, g_cto
    o_cip = by_three(g_cip)
    o_ctp = by_three(g_ctp)
    o_tg, o_ig = t_gain, i_gain
    return (
        t_final.astype(BFLOAT)[None],
        i_final.astype(BFLOAT)[None],
        text_input_grad[None],
        image_input_grad[None],
        o_ctp,
        o_cip,
        o_cto,
        o_cio,
        o_ctu,
        o_ctd,
        o_ciu,
        o_cid,
        o_stp,
        o_sto,
        o_stu,
        o_std,
        o_sip,
        o_sio,
        o_siu,
        o_sid,
        o_tg,
        o_ig,
    )


def solution(mesh):
    row = P(ALL, None)
    batch = P(ALL, None, None)
    col = P(None, ALL)
    proj = P(None, ALL, None)
    proj_grad = P(None, None, ALL)
    in_specs = (batch, batch, P("dp"), batch, batch, proj, proj, row, row, row, row, row, row)
    in_specs += (proj, row, row, row, proj, row, row, row, P(), P())
    out_specs = (batch, batch, batch, batch, proj_grad, proj_grad, row, row, col, row, col, row)
    out_specs += (proj_grad, row, col, col, proj_grad, row, col, col, col, col)
    return jax.shard_map(
        on_device, mesh=mesh, in_specs=in_specs, out_specs=out_specs, check_vma=False
    )
```

time: 2850 us -> 742 us (0.26)
  local copies, waits for them, and re-layouts: 811 us -> 63.8 us
  waiting for transfers between devices: 1040 us -> 370 us
  other arithmetic: 557 us -> 64.3 us
  starting transfers between devices: 272 us -> 48.8 us
  Pallas kernels: 0 us -> 76.8 us
  matrix products: 125 us -> 92.1 us
    all_gather x16 -> x2, waiting for transfers between devices: 840 us -> 19.4 us  [gather_columns(): return lax.all_gather(side(parts), ALL, axis=0, tiled=True)]
    unnamed x19 -> x4, other arithmetic: 478 us -> 0.7 us
    convert_element_type x23 -> x0, local copies, waits for them, and re-layouts: 374 us -> none  [the longest x18 370 us: short(): return part.astype(jnp.bfloat16) if part.dtype == jnp.float32 else part]
    unnamed x355 -> x249, local copies, waits for them, and re-layouts: 406 us -> 40.5 us
    ppermute x0 -> x45, waiting for transfers between devices: none -> 350 us  [swap(): return lax.ppermute(block, ALL, [(i, i ^ 1 << bit) for i in range(size)])]
    all_to_all x34 -> x0, starting transfers between devices: 270 us -> none  [the longest x18 203 us: on_device(): lax.all_to_all(as_sent(to_rows(all_grads, all_dims)), 'dp', split_axis=1,...]
    all_to_all x34 -> x0, waiting for transfers between devices: 185 us -> none  [the longest x18 152 us: on_device(): lax.all_to_all(as_sent(to_rows(all_grads, all_dims)), 'dp', split_axis=1,...]
    pallas_call x0 -> x17, Pallas kernels: none -> 76.8 us  [the longest x8 35.9 us: pack_kernel(): pl.pallas_call(body, grid_spec=pltpu.PrefetchScalarGridSpec(num_scalar_pr...]
  transfers between devices with their start and end apart: 67 -> 49, of which waited for: 37 -> 31; matrix products, arithmetic and copies ran while one was open for 52% -> 25% of each run, Pallas kernels for 0% -> 10%
where the time goes in v1:
time: 742 us; the launch traced here: 732 us
  waiting for transfers between devices  370 us (50%)
  matrix products  92.1 us (12%)
  Pallas kernels  76.8 us (10%)
  other arithmetic  64.3 us (9%)
  local copies, waits for them, and re-layouts  63.8 us (9%)
  starting transfers between devices  48.8 us (7%)
  between operations  16.2 us (2%)
    ppermute x45, waiting for transfers between devices, swap(): return lax.ppermute(block, ALL, [(i, i ^ 1 << bit) for i in range(size)])  350 us
    dot_general x16, matrix products, mm_t(): lax.dot_general(left, right, (((1,), (1,)), ((), ())), preferred_element_...  52.1 us
    ppermute x45, starting transfers between devices, swap(): return lax.ppermute(block, ALL, [(i, i ^ 1 << bit) for i in range(size)])  48.5 us
    unnamed x249, local copies, waits for them, and re-layouts  40.5 us
    dot_general x16, matrix products, mm(): return jnp.dot(left, right, preferred_element_type=FLOAT)  40 us
    convert_element_type x24, other arithmetic, add_low(): return (left.astype(FLOAT) + right.astype(FLOAT)).astype(BFLOAT)  36.2 us
    pallas_call x8, Pallas kernels, pack_kernel(): pl.pallas_call(body, grid_spec=pltpu.PrefetchScalarGridSpec(num_scalar_pr...  35.9 us
    pallas_call x6, Pallas kernels, vmem_call(): pl.pallas_call(body, in_specs=[pl.BlockSpec(memory_space=pltpu.SMEM)] + [...  25.1 us
  transfers between devices with their start and end apart: 49, of which 31 were waited for; matrix products, arithmetic and copies ran while one was open for 25% of the time, Pallas kernels for 10%

profile of v1, /device:TPU:0, one launch (start us, length us, event | category | flops | bytes accessed | tf_op | source)
XLA Modules:
  0.0 731.9 jit_solution(11474331598483959620)
XLA Ops:
  21.1 22.1 %collective-permute-done = bf16[1,32,3072]{2,1,0:T(8,128)(2,1)S(1)} collective-permute-done((bf16[1,32,3072]{2,1,0:T(8,128)(2,1)S(1)}, bf16[1,32,3072]{2,1,0:T(8,128)(2,1)S(1)}, u32[]{:S(2)}, u32[]{:S(2)}) %collective-permute-start) | collective-permute-done | bytes 196640 | tf_op jit(solution)/shard_map/ppermute | solution.py:30
  43.3 7.9 %collective-permute-done.1 = bf16[1,128,768]{2,1,0:T(8,128)(2,1)S(1)} collective-permute-done((bf16[1,128,768]{2,1,0:T(8,128)(2,1)S(1)}, bf16[1,128,768]{2,1,0:T(8,128)(2,1)S(1)}, u32[]{:S(2)}, u32[]{:S(2)}) %collective-permute-start.1) | collective-permute-done | bytes 196640 | tf_op jit(solution)/shard_map/ppermute | solution.py:30
  53.4 21.3 %collective-permute-done.3 = bf16[2,128,768]{2,1,0:T(8,128)(2,1)S(1)} collective-permute-done((bf16[2,128,768]{2,1,0:T(8,128)(2,1)S(1)}, bf16[2,128,768]{2,1,0:T(8,128)(2,1)S(1)}, u32[]{:S(2)}, u32[]{:S(2)}) %collective-permute-start.3) | collective-permute-done | bytes 393248 | tf_op jit(solution)/shard_map/ppermute | solution.py:30
  74.7 20.8 %collective-permute-done.2 = bf16[2,32,3072]{2,1,0:T(8,128)(2,1)S(1)} collective-permute-done((bf16[2,32,3072]{2,1,0:T(8,128)(2,1)S(1)}, bf16[2,32,3072]{2,1,0:T(8,128)(2,1)S(1)}, u32[]{:S(2)}, u32[]{:S(2)}) %collective-permute-start.2) | collective-permute-done | bytes 393248 | tf_op jit(solution)/shard_map/ppermute | solution.py:30
  101.7 12.1 %collective-permute-done.6 = bf16[1,96,768]{2,1,0:T(8,128)(2,1)S(1)} collective-permute-done((bf16[1,96,768]{2,1,0:T(8,128)(2,1)S(1)}, bf16[1,96,768]{2,1,0:T(8,128)(2,1)S(1)}, u32[]{:S(2)}, u32[]{:S(2)}) %collective-permute-start.6) | collective-permute-done | bytes 147488 | tf_op jit(solution)/shard_map/ppermute | solution.py:30
  113.8 6.8 collective-permute-done.5
  130.2 7.9 %collective-permute-done.9 = bf16[2,96,768]{2,1,0:T(8,128)(2,1)S(1)} collective-permute-done((bf16[2,96,768]{2,1,0:T(8,128)(2,1)S(1)}, bf16[2,96,768]{2,1,0:T(8,128)(2,1)S(1)}, u32[]{:S(2)}, u32[]{:S(2)}) %collective-permute-start.9) | collective-permute-done | bytes 294944 | tf_op jit(solution)/shard_map/ppermute | solution.py:30
  138.1 38.1 %collective-permute-done.8 = bf16[8,128,768]{2,1,0:T(8,128)(2,1)S(1)} collective-permute-done((bf16[8,128,768]{2,1,0:T(8,128)(2,1)S(1)}, bf16[8,128,768]{2,1,0:T(8,128)(2,1)S(1)}, u32[]{:S(2)}, u32[]{:S(2)}) %collective-permute-start.8) | collective-permute-done | bytes 1572896 | tf_op jit(solution)/shard_map/ppermute | solution.py:30
  182.8 12.1 %collective-permute-done.12 = bf16[4,96,768]{2,1,0:T(8,128)(2,1)} collective-permute-done((bf16[4,96,768]{2,1,0:T(8,128)(2,1)}, bf16[4,96,768]{2,1,0:T(8,128)(2,1)}, u32[]{:S(2)}, u32[]{:S(2)}) %collective-permute-start.12) | collective-permute-done | bytes 589856 | tf_op jit(solution)/shard_map/ppermute | solution.py:30
  205.5 5.7 shard_map.392
  223.4 5.5 collective-permute-done.13
  269.1 5.4 fusion.62.refs_1_
  290.1 6.0 shard_map.396
  307.8 19.4 %all-gather.5.cloned.1.call-done = bf16[1024,9216]{1,0:T(8,128)(2,1)} async-done(((bf16[32,9216]{1,0:T(8,128)(2,1)}), bf16[1024,9216]{1,0:T(8,128)(2,1)}) %all-gather.5.cloned.1.call-update) | async-done | bytes 18874384 | tf_op jit(solution)/shard_map/all_gather | solution.py:539
  388.5 11.7 %collective-permute-done.16 = bf16[8,72,768]{2,1,0:T(8,128)(2,1)S(1)} collective-permute-done((bf16[8,72,768]{2,1,0:T(8,128)(2,1)S(1)}, bf16[8,72,768]{2,1,0:T(8,128)(2,1)S(1)}, u32[]{:S(2)}, u32[]{:S(2)}) %collective-permute-start.16) | collective-permute-done | bytes 884768 | tf_op jit(solution)/shard_map/ppermute | solution.py:30
  419.9 9.4 %collective-permute-done.20 = bf16[4,72,768]{2,1,0:T(8,128)(2,1)S(1)} collective-permute-done((bf16[4,72,768]{2,1,0:T(8,128)(2,1)S(1)}, bf16[4,72,768]{2,1,0:T(8,128)(2,1)S(1)}, u32[]{:S(2)}, u32[]{:S(2)}) %collective-permute-start.20) | collective-permute-done | bytes 442400 | tf_op jit(solution)/shard_map/ppermute | solution.py:30
  429.3 21.5 %collective-permute-done.18 = bf16[8,96,1024]{2,1,0:T(8,128)(2,1)S(1)} collective-permute-done((bf16[8,96,1024]{2,1,0:T(8,128)(2,1)S(1)}, bf16[8,96,1024]{2,1,0:T(8,128)(2,1)S(1)}, u32[]{:S(2)}, u32[]{:S(2)}) %collective-permute-start.18) | collective-permute-done | bytes 1572896 | tf_op jit(solution)/shard_map/ppermute | solution.py:30
  465.6 5.5 shard_map.403
  478.0 35.8 %collective-permute-done.21 = bf16[8,96,1024]{2,1,0:T(8,128)(2,1)S(1)} collective-permute-done((bf16[8,96,1024]{2,1,0:T(8,128)(2,1)S(1)}, bf16[8,96,1024]{2,1,0:T(8,128)(2,1)S(1)}, u32[]{:S(2)}, u32[]{:S(2)}) %collective-permute-start.21) | collective-permute-done | bytes 1572896 | tf_op jit(solution)/shard_map/ppermute | solution.py:30
  529.3 8.0 %shard_map.404 = (bf16[100,3072]{1,0:T(8,128)(2,1)S(1)}, bf16[36,3072]{1,0:T(8,128)(2,1)S(1)}) custom-call(s32[1]{0:T(128)} %dynamic_slice.264.len_ref, bf16[100,3072]{1,0:T(8,128)(2,1)S(1)} %fusion.19.text_ref, bf16[36,3072]{1,0:T(8,128)(2,1)S(1)} %copy-done.13, bf16[100,1024]{1,0:T(8,128)(2,1)S(1)} %convolution_convert_fusion.2.tg_ref, ...), custom_call_target="tpu_custom_call" | custom-call | tf_op jit(solution)/shard_map/pallas_call | solution.py:400
  543.1 5.6 collective-permute-done.25
  567.6 23.3 %collective-permute-done.33 = bf16[1,96,1024]{2,1,0:T(8,128)(2,1)S(1)} collective-permute-done((bf16[1,96,1024]{2,1,0:T(8,128)(2,1)S(1)}, bf16[1,96,1024]{2,1,0:T(8,128)(2,1)S(1)}, u32[]{:S(2)}, u32[]{:S(2)}) %collective-permute-start.33) | collective-permute-done | bytes 196640 | tf_op jit(solution)/shard_map/ppermute | solution.py:30
  609.1 6.8 collective-permute-done.37
  615.9 6.8 collective-permute-done.36
  622.7 5.7 collective-permute-done.34
  628.5 11.7 %collective-permute-done.35 = bf16[8,800,128]{2,1,0:T(8,128)(2,1)} collective-permute-done((bf16[8,800,128]{2,1,0:T(8,128)(2,1)}, bf16[8,800,128]{2,1,0:T(8,128)(2,1)}, u32[]{:S(2)}, u32[]{:S(2)}) %collective-permute-start.35) | collective-permute-done | bytes 1638432 | tf_op jit(solution)/shard_map/ppermute | solution.py:30
  648.9 7.7 %collective-permute-done.40 = bf16[1,96,768]{2,1,0:T(8,128)(2,1)S(1)} collective-permute-done((bf16[1,96,768]{2,1,0:T(8,128)(2,1)S(1)}, bf16[1,96,768]{2,1,0:T(8,128)(2,1)S(1)}, u32[]{:S(2)}, u32[]{:S(2)}) %collective-permute-start.40) | collective-permute-done | bytes 147488 | tf_op jit(solution)/shard_map/ppermute | solution.py:30
  656.7 8.1 %collective-permute-done.39 = bf16[4,800,128]{2,1,0:T(8,128)(2,1)S(1)} collective-permute-done((bf16[4,800,128]{2,1,0:T(8,128)(2,1)S(1)}, bf16[4,800,128]{2,1,0:T(8,128)(2,1)S(1)}, u32[]{:S(2)}, u32[]{:S(2)}) %collective-permute-start.39) | collective-permute-done | bytes 819232 | tf_op jit(solution)/shard_map/ppermute | solution.py:30
  673.3 7.8 %collective-permute-done.41 = bf16[2,600,128]{2,1,0:T(8,128)(2,1)S(1)} collective-permute-done((bf16[2,600,128]{2,1,0:T(8,128)(2,1)S(1)}, bf16[2,600,128]{2,1,0:T(8,128)(2,1)S(1)}, u32[]{:S(2)}, u32[]{:S(2)}) %collective-permute-start.41) | collective-permute-done | bytes 307232 | tf_op jit(solution)/shard_map/ppermute | solution.py:30
  681.2 5.4 collective-permute-done.42
  686.6 9.2 %collective-permute-start.43 = (bf16[1,600,128]{2,1,0:T(8,128)(2,1)S(1)}, bf16[1,600,128]{2,1,0:T(8,128)(2,1)S(1)}, u32[]{:S(2)}, u32[]{:S(2)}) collective-permute-start(bf16[1,600,128]{2,1,0:T(8,128)(2,1)S(1)} %fusion.140), channel_id=1, source_target_pairs={{0,16},{1,17},{2,18},{3,19},{4,20},{5,21},{6,22},{7,23},{8,24},{9,... | collective-permute-start | bytes 460808 | tf_op jit(solution)/shard_map/ppermute | solution.py:30
  697.6 14.6 %collective-permute-done.43 = bf16[1,600,128]{2,1,0:T(8,128)(2,1)S(1)} collective-permute-done((bf16[1,600,128]{2,1,0:T(8,128)(2,1)S(1)}, bf16[1,600,128]{2,1,0:T(8,128)(2,1)S(1)}, u32[]{:S(2)}, u32[]{:S(2)}) %collective-permute-start.43) | collective-permute-done | bytes 153632 | tf_op jit(solution)/shard_map/ppermute | solution.py:30
  (532 shorter events, 319.7 us)
Async XLA Ops:
  7.3 209.3 %all-gather.3.cloned.1.call-start = ((), (), s32[]{:S(2)}) async-start(), calls=%async_computation.2 | async-start | bytes 19464192 | tf_op jit(solution)/shard_map/all_gather | solution.py:539
  15.7 311.5 %all-gather.5.cloned.1.call-start = ((), (), s32[]{:S(2)}) async-start(), calls=%async_computation.3 | async-start | bytes 19464192 | tf_op jit(solution)/shard_map/all_gather | solution.py:539
  16.8 605.9 %reduce-scatter.3.cloned.1.call-start = ((), (), s32[]{:S(2)}) async-start(), calls=%async_computation.4 | async-start | bytes 10948608 | tf_op jit(solution)/shard_map/reduce_scatter | solution.py:265
  16.9 26.4 %collective-permute-start = (bf16[1,32,3072]{2,1,0:T(8,128)(2,1)S(1)}, bf16[1,32,3072]{2,1,0:T(8,128)(2,1)S(1)}, u32[]{:S(2)}, u32[]{:S(2)}) collective-permute-start(bf16[1,32,3072]{2,1,0:T(8,128)(2,1)S(1)} %maximum_bitcast_fusion), channel_id=1, source_target_pairs={{0,16},{1,17},{2,18},{3,19},{4,20},{5,21},{6,22},{7,23},{8,24},{9,... | collective-permute-start | bytes 589832 | tf_op jit(solution)/shard_map/ppermute | solution.py:30
  21.1 30.2 %collective-permute-start.1 = (bf16[1,128,768]{2,1,0:T(8,128)(2,1)S(1)}, bf16[1,128,768]{2,1,0:T(8,128)(2,1)S(1)}, u32[]{:S(2)}, u32[]{:S(2)}) collective-permute-start(bf16[1,128,768]{2,1,0:T(8,128)(2,1)S(1)} %maximum_bitcast_fusion.1), channel_id=1, source_target_pairs={{0,16},{1,17},{2,18},{3,19},{4,20},{5,21},{6,22},{7,23},{8,24},{9,... | collective-permute-start | bytes 589832 | tf_op jit(solution)/shard_map/ppermute | solution.py:30
  51.3 23.4 %collective-permute-start.3 = (bf16[2,128,768]{2,1,0:T(8,128)(2,1)S(1)}, bf16[2,128,768]{2,1,0:T(8,128)(2,1)S(1)}, u32[]{:S(2)}, u32[]{:S(2)}) collective-permute-start(bf16[2,128,768]{2,1,0:T(8,128)(2,1)S(1)} %pad_maximum_fusion.8), channel_id=1, source_target_pairs={{0,8},{1,9},{2,10},{3,11},{4,12},{5,13},{6,14},{7,15},{8,0},{9,1},... | collective-permute-start | bytes 1179656 | tf_op jit(solution)/shard_map/ppermute | solution.py:30
  52.1 43.4 %collective-permute-start.2 = (bf16[2,32,3072]{2,1,0:T(8,128)(2,1)S(1)}, bf16[2,32,3072]{2,1,0:T(8,128)(2,1)S(1)}, u32[]{:S(2)}, u32[]{:S(2)}) collective-permute-start(bf16[2,32,3072]{2,1,0:T(8,128)(2,1)S(1)} %pad_maximum_fusion.7), channel_id=1, source_target_pairs={{0,8},{1,9},{2,10},{3,11},{4,12},{5,13},{6,14},{7,15},{8,0},{9,1},... | collective-permute-start | bytes 1179656 | tf_op jit(solution)/shard_map/ppermute | solution.py:30
  95.7 25.0 %collective-permute-start.5 = (bf16[4,128,768]{2,1,0:T(8,128)(2,1)S(1)}, bf16[4,128,768]{2,1,0:T(8,128)(2,1)S(1)}, u32[]{:S(2)}, u32[]{:S(2)}) collective-permute-start(bf16[4,128,768]{2,1,0:T(8,128)(2,1)S(1)} %pad_maximum_fusion.4), channel_id=1, source_target_pairs={{0,4},{1,5},{2,6},{3,7},{4,0},{5,1},{6,2},{7,3},{8,12},{9,13},{10,... | collective-permute-start | bytes 2359304 | tf_op jit(solution)/shard_map/ppermute | solution.py:30
  96.8 27.7 %collective-permute-start.4 = (bf16[4,32,3072]{2,1,0:T(8,128)(2,1)S(1)}, bf16[4,32,3072]{2,1,0:T(8,128)(2,1)S(1)}, u32[]{:S(2)}, u32[]{:S(2)}) collective-permute-start(bf16[4,32,3072]{2,1,0:T(8,128)(2,1)S(1)} %pad_maximum_fusion.3), channel_id=1, source_target_pairs={{0,1},{1,0},{2,3},{3,2},{4,5},{5,4},{6,7},{7,6},{8,9},{9,8},{10,11... | collective-permute-start | bytes 2359304 | tf_op jit(solution)/shard_map/ppermute | solution.py:30
  124.7 51.5 %collective-permute-start.8 = (bf16[8,128,768]{2,1,0:T(8,128)(2,1)S(1)}, bf16[8,128,768]{2,1,0:T(8,128)(2,1)S(1)}, u32[]{:S(2)}, u32[]{:S(2)}) collective-permute-start(bf16[8,128,768]{2,1,0:T(8,128)(2,1)S(1)} %pad_maximum_fusion.1), channel_id=1, source_target_pairs={{0,1},{1,0},{2,3},{3,2},{4,5},{5,4},{6,7},{7,6},{8,9},{9,8},{10,11... | collective-permute-start | bytes 4718600 | tf_op jit(solution)/shard_map/ppermute | solution.py:30
  127.4 48.8 %collective-permute-start.7 = (bf16[8,32,3072]{2,1,0:T(8,128)(2,1)S(1)}, bf16[8,32,3072]{2,1,0:T(8,128)(2,1)S(1)}, u32[]{:S(2)}, u32[]{:S(2)}) collective-permute-start(bf16[8,32,3072]{2,1,0:T(8,128)(2,1)S(1)} %pad_maximum_fusion), channel_id=1, source_target_pairs={{0,4},{1,5},{2,6},{3,7},{4,0},{5,1},{6,2},{7,3},{8,12},{9,13},{10,... | collective-permute-start | bytes 4718600 | tf_op jit(solution)/shard_map/ppermute | solution.py:30
  197.2 31.8 %collective-permute-start.13 = (bf16[8,96,768]{2,1,0:T(8,128)(2,1)}, bf16[8,96,768]{2,1,0:T(8,128)(2,1)}, u32[]{:S(2)}, u32[]{:S(2)}) collective-permute-start(bf16[8,96,768]{2,1,0:T(8,128)(2,1)} %pad_maximum_fusion.2), channel_id=1, source_target_pairs={{0,1},{1,0},{2,3},{3,2},{4,5},{5,4},{6,7},{7,6},{8,9},{9,8},{10,11... | collective-permute-start | bytes 3538952 | tf_op jit(solution)/shard_map/ppermute | solution.py:30
  307.6 408.4 %reduce-scatter.5.cloned.1.call-start = ((), (), s32[]{:S(2)}) async-start(), calls=%async_computation.5 | async-start | bytes 12976128 | tf_op jit(solution)/shard_map/reduce_scatter | solution.py:265
  340.9 24.0 %collective-permute-start.15 = (bf16[16,72,768]{2,1,0:T(8,128)(2,1)S(1)}, bf16[16,72,768]{2,1,0:T(8,128)(2,1)S(1)}, u32[]{:S(2)}, u32[]{:S(2)}) collective-permute-start(bf16[16,72,768]{2,1,0:T(8,128)(2,1)S(1)} %bitcast.404), channel_id=1, source_target_pairs={{0,2},{1,3},{2,0},{3,1},{4,6},{5,7},{6,4},{7,5},{8,10},{9,11},{10,... | collective-permute-start | bytes 5308424 | tf_op jit(solution)/shard_map/ppermute | solution.py:30
  366.1 34.1 %collective-permute-start.17 = (bf16[16,96,1024]{2,1,0:T(8,128)(2,1)}, bf16[16,96,1024]{2,1,0:T(8,128)(2,1)}, u32[]{:S(2)}, u32[]{:S(2)}) collective-permute-start(bf16[16,96,1024]{2,1,0:T(8,128)(2,1)} %bitcast.45), channel_id=1, source_target_pairs={{0,2},{1,3},{2,0},{3,1},{4,6},{5,7},{6,4},{7,5},{8,10},{9,11},{10,... | collective-permute-start | bytes 9437192 | tf_op jit(solution)/shard_map/ppermute | solution.py:30
  373.4 26.8 %collective-permute-start.16 = (bf16[8,72,768]{2,1,0:T(8,128)(2,1)S(1)}, bf16[8,72,768]{2,1,0:T(8,128)(2,1)S(1)}, u32[]{:S(2)}, u32[]{:S(2)}) collective-permute-start(bf16[8,72,768]{2,1,0:T(8,128)(2,1)S(1)} %get-tuple-element.353), channel_id=1, source_target_pairs={{0,4},{1,5},{2,6},{3,7},{4,0},{5,1},{6,2},{7,3},{8,12},{9,13},{10,... | collective-permute-start | bytes 2654216 | tf_op jit(solution)/shard_map/ppermute | solution.py:30
  400.5 28.8 %collective-permute-start.20 = (bf16[4,72,768]{2,1,0:T(8,128)(2,1)S(1)}, bf16[4,72,768]{2,1,0:T(8,128)(2,1)S(1)}, u32[]{:S(2)}, u32[]{:S(2)}) collective-permute-start(bf16[4,72,768]{2,1,0:T(8,128)(2,1)S(1)} %get-tuple-element.365), channel_id=1, source_target_pairs={{0,8},{1,9},{2,10},{3,11},{4,12},{5,13},{6,14},{7,15},{8,0},{9,1},... | collective-permute-start | bytes 1327112 | tf_op jit(solution)/shard_map/ppermute | solution.py:30
  400.5 50.2 %collective-permute-start.19 = (bf16[16,96,1024]{2,1,0:T(8,128)(2,1)S(1)}, bf16[16,96,1024]{2,1,0:T(8,128)(2,1)S(1)}, u32[]{:S(2)}, u32[]{:S(2)}) collective-permute-start(bf16[16,96,1024]{2,1,0:T(8,128)(2,1)S(1)} %bitcast.401), channel_id=1, source_target_pairs={{0,2},{1,3},{2,0},{3,1},{4,6},{5,7},{6,4},{7,5},{8,10},{9,11},{10,... | collective-permute-start | bytes 9437192 | tf_op jit(solution)/shard_map/ppermute | solution.py:30
  404.5 46.3 %collective-permute-start.18 = (bf16[8,96,1024]{2,1,0:T(8,128)(2,1)S(1)}, bf16[8,96,1024]{2,1,0:T(8,128)(2,1)S(1)}, u32[]{:S(2)}, u32[]{:S(2)}) collective-permute-start(bf16[8,96,1024]{2,1,0:T(8,128)(2,1)S(1)} %get-tuple-element.347), channel_id=1, source_target_pairs={{0,1},{1,0},{2,3},{3,2},{4,5},{5,4},{6,7},{7,6},{8,9},{9,8},{10,11... | collective-permute-start | bytes 4718600 | tf_op jit(solution)/shard_map/ppermute | solution.py:30
  452.3 25.7 %collective-permute-start.22 = (bf16[4,96,1024]{2,1,0:T(8,128)(2,1)S(1)}, bf16[4,96,1024]{2,1,0:T(8,128)(2,1)S(1)}, u32[]{:S(2)}, u32[]{:S(2)}) collective-permute-start(bf16[4,96,1024]{2,1,0:T(8,128)(2,1)S(1)} %get-tuple-element.359), channel_id=1, source_target_pairs={{0,4},{1,5},{2,6},{3,7},{4,0},{5,1},{6,2},{7,3},{8,12},{9,13},{10,... | collective-permute-start | bytes 2359304 | tf_op jit(solution)/shard_map/ppermute | solution.py:30
  454.8 59.1 %collective-permute-start.24 = (bf16[16,96,768]{2,1,0:T(8,128)(2,1)S(1)}, bf16[16,96,768]{2,1,0:T(8,128)(2,1)S(1)}, u32[]{:S(2)}, u32[]{:S(2)}) collective-permute-start(bf16[16,96,768]{2,1,0:T(8,128)(2,1)S(1)} %bitcast.403), channel_id=1, source_target_pairs={{0,2},{1,3},{2,0},{3,1},{4,6},{5,7},{6,4},{7,5},{8,10},{9,11},{10,... | collective-permute-start | bytes 7077896 | tf_op jit(solution)/shard_map/ppermute | solution.py:30
  456.6 57.2 %collective-permute-start.21 = (bf16[8,96,1024]{2,1,0:T(8,128)(2,1)S(1)}, bf16[8,96,1024]{2,1,0:T(8,128)(2,1)S(1)}, u32[]{:S(2)}, u32[]{:S(2)}) collective-permute-start(bf16[8,96,1024]{2,1,0:T(8,128)(2,1)S(1)} %get-tuple-element.345), channel_id=1, source_target_pairs={{0,8},{1,9},{2,10},{3,11},{4,12},{5,13},{6,14},{7,15},{8,0},{9,1},... | collective-permute-start | bytes 4718600 | tf_op jit(solution)/shard_map/ppermute | solution.py:30
  520.4 28.3 %collective-permute-start.25 = (bf16[8,96,768]{2,1,0:T(8,128)(2,1)}, bf16[8,96,768]{2,1,0:T(8,128)(2,1)}, u32[]{:S(2)}, u32[]{:S(2)}) collective-permute-start(bf16[8,96,768]{2,1,0:T(8,128)(2,1)} %get-tuple-element.350), channel_id=1, source_target_pairs={{0,4},{1,5},{2,6},{3,7},{4,0},{5,1},{6,2},{7,3},{8,12},{9,13},{10,... | collective-permute-start | bytes 3538952 | tf_op jit(solution)/shard_map/ppermute | solution.py:30
  566.9 24.0 %collective-permute-start.32 = (bf16[16,800,128]{2,1,0:T(8,128)(2,1)S(1)}, bf16[16,800,128]{2,1,0:T(8,128)(2,1)S(1)}, u32[]{:S(2)}, u32[]{:S(2)}) collective-permute-start(bf16[16,800,128]{2,1,0:T(8,128)(2,1)S(1)} %bitcast.400), channel_id=1, source_target_pairs={{0,2},{1,3},{2,0},{3,1},{4,6},{5,7},{6,4},{7,5},{8,10},{9,11},{10,... | collective-permute-start | bytes 9830408 | tf_op jit(solution)/shard_map/ppermute | solution.py:30
  566.9 23.9 %collective-permute-start.31 = (bf16[16,600,128]{2,1,0:T(8,128)(2,1)S(1)}, bf16[16,600,128]{2,1,0:T(8,128)(2,1)S(1)}, u32[]{:S(2)}, u32[]{:S(2)}) collective-permute-start(bf16[16,600,128]{2,1,0:T(8,128)(2,1)S(1)} %bitcast.402), channel_id=1, source_target_pairs={{0,2},{1,3},{2,0},{3,1},{4,6},{5,7},{6,4},{7,5},{8,10},{9,11},{10,... | collective-permute-start | bytes 7372808 | tf_op jit(solution)/shard_map/ppermute | solution.py:30
  567.5 23.4 %collective-permute-start.33 = (bf16[1,96,1024]{2,1,0:T(8,128)(2,1)S(1)}, bf16[1,96,1024]{2,1,0:T(8,128)(2,1)S(1)}, u32[]{:S(2)}, u32[]{:S(2)}) collective-permute-start(bf16[1,96,1024]{2,1,0:T(8,128)(2,1)S(1)} %fusion.133), channel_id=1, source_target_pairs={{0,16},{1,17},{2,18},{3,19},{4,20},{5,21},{6,22},{7,23},{8,24},{9,... | collective-permute-start | bytes 589832 | tf_op jit(solution)/shard_map/ppermute | solution.py:30
  593.1 47.1 %collective-permute-start.35 = (bf16[8,800,128]{2,1,0:T(8,128)(2,1)}, bf16[8,800,128]{2,1,0:T(8,128)(2,1)}, u32[]{:S(2)}, u32[]{:S(2)}) collective-permute-start(bf16[8,800,128]{2,1,0:T(8,128)(2,1)} %get-tuple-element.343), channel_id=1, source_target_pairs={{0,1},{1,0},{2,3},{3,2},{4,5},{5,4},{6,7},{7,6},{8,9},{9,8},{10,11... | collective-permute-start | bytes 4915208 | tf_op jit(solution)/shard_map/ppermute | solution.py:30
  595.4 33.1 %collective-permute-start.34 = (bf16[8,600,128]{2,1,0:T(8,128)(2,1)}, bf16[8,600,128]{2,1,0:T(8,128)(2,1)}, u32[]{:S(2)}, u32[]{:S(2)}) collective-permute-start(bf16[8,600,128]{2,1,0:T(8,128)(2,1)} %get-tuple-element.349), channel_id=1, source_target_pairs={{0,4},{1,5},{2,6},{3,7},{4,0},{5,1},{6,2},{7,3},{8,12},{9,13},{10,... | collective-permute-start | bytes 3686408 | tf_op jit(solution)/shard_map/ppermute | solution.py:30
  598.7 24.0 %collective-permute-start.36 = (bf16[2,96,768]{2,1,0:T(8,128)(2,1)S(1)}, bf16[2,96,768]{2,1,0:T(8,128)(2,1)}, u32[]{:S(2)}, u32[]{:S(2)}) collective-permute-start(bf16[2,96,768]{2,1,0:T(8,128)(2,1)S(1)} %get-tuple-element.375), channel_id=1, source_target_pairs={{0,8},{1,9},{2,10},{3,11},{4,12},{5,13},{6,14},{7,15},{8,0},{9,1},... | collective-permute-start | bytes 884744 | tf_op jit(solution)/shard_map/ppermute | solution.py:30
  667.1 19.5 %collective-permute-start.42 = (bf16[2,800,128]{2,1,0:T(8,128)(2,1)S(1)}, bf16[2,800,128]{2,1,0:T(8,128)(2,1)S(1)}, u32[]{:S(2)}, u32[]{:S(2)}) collective-permute-start(bf16[2,800,128]{2,1,0:T(8,128)(2,1)S(1)} %get-tuple-element.367), channel_id=1, source_target_pairs={{0,8},{1,9},{2,10},{3,11},{4,12},{5,13},{6,14},{7,15},{8,0},{9,1},... | collective-permute-start | bytes 1228808 | tf_op jit(solution)/shard_map/ppermute | solution.py:30
  686.6 25.6 %collective-permute-start.43 = (bf16[1,600,128]{2,1,0:T(8,128)(2,1)S(1)}, bf16[1,600,128]{2,1,0:T(8,128)(2,1)S(1)}, u32[]{:S(2)}, u32[]{:S(2)}) collective-permute-start(bf16[1,600,128]{2,1,0:T(8,128)(2,1)S(1)} %fusion.140), channel_id=1, source_target_pairs={{0,16},{1,17},{2,18},{3,19},{4,20},{5,21},{6,22},{7,23},{8,24},{9,... | collective-permute-start | bytes 460808 | tf_op jit(solution)/shard_map/ppermute | solution.py:30
  695.8 20.1 %collective-permute-start.44 = (bf16[1,800,128]{2,1,0:T(8,128)(2,1)S(1)}, bf16[1,800,128]{2,1,0:T(8,128)(2,1)S(1)}, u32[]{:S(2)}, u32[]{:S(2)}) collective-permute-start(bf16[1,800,128]{2,1,0:T(8,128)(2,1)S(1)} %fusion.124), channel_id=1, source_target_pairs={{0,16},{1,17},{2,18},{3,19},{4,20},{5,21},{6,22},{7,23},{8,24},{9,... | collective-permute-start | bytes 614408 | tf_op jit(solution)/shard_map/ppermute | solution.py:30
  (126 other events, 1009.3 us)
Sparse Core Ops, SparseCore 0:
  15.8 176.8 all-gather.2
  195.6 131.5 all-gather.4
  333.3 178.0 reduce-scatter.2
  517.2 195.5 reduce-scatter.4

commit v2 on v1

--- a/solution.py
+++ b/solution.py
@@ -99,19 +99,19 @@
 class Gather:
     def __init__(self, shard, order, splits=None):
         self.order = order
-        self.held = shard[None]
+        self.send = shard[None]
         self.splits = splits or [shard.shape[0]]
         self.step = 0
 
     def start(self):
-        self.came = swap(self.held, self.order[self.step])
+        self.came = swap(self.send, self.order[self.step])
         self.step += 1
 
     def absorb(self):
         if self.step == len(self.order):
-            self.full = join_blocks(self.held, self.came, self.order, self.splits)
+            self.full = join_blocks(self.send, self.came, self.order, self.splits)
         else:
-            self.held = jnp.concatenate([self.held, self.came], axis=0)
+            self.send = jnp.concatenate([self.send, self.came], axis=0)
 
 
 def close_round(movers, *arrays):
@@ -121,6 +121,10 @@
         m.came = block
     for m in movers:
         m.absorb()
+    going = [m for m in movers if m.step < len(m.order)]
+    sends, arrays = lax.optimization_barrier(([m.send for m in going], arrays))
+    for m, block in zip(going, sends):
+        m.send = block
     return arrays
 
 
@@ -329,7 +333,7 @@
     weighted = upstream * gain_vec
     inner = jnp.mean(weighted * unit, axis=-1, keepdims=True)
     grad = (weighted - jnp.mean(weighted, axis=-1, keepdims=True) - unit * inner) * scale
-    return grad, (upstream * unit).astype(BFLOAT)
+    return grad, jnp.sum(upstream * unit, axis=0)
 
 
 def gelu_back(upper, upstream):
@@ -602,21 +606,54 @@
     t_res, t_ga, t_pairs, t_gain_s = tail_backward(
         text_cotangent[0].astype(FLOAT), st_kept, st_attn, w_sto, w_stu, w_std, text_gains[2:4], False
     )
-    c1t = Whole(t_pairs, d_t)
-    c1t.block, t_ga, t_res, i_attn = close_round([], c1t.block, t_ga, t_res, i_attn)
-    c1t.launch()
+    def start(*movers):
+        for m in movers:
+            if m.step < bits:
+                m.start()
+
+    def by_owner(packed, own):
+        rows = packed.shape[0]
+        blocks = packed.reshape(rows, 3, size, own).transpose(2, 0, 1, 3).reshape(size, rows, 3 * own)
+        return jnp.pad(blocks, ((0, 0), (0, -rows % 8), (0, 3 * (own_v - own))))
+
+    def exchange(*blocks):
+        return lax.all_to_all(
+            jnp.concatenate(blocks, axis=1), ALL, split_axis=0, concat_axis=0, tiled=True
+        )
+
+    c1a = Chunk(t_pairs[:1], d_t, halving(2, 0))
+    c1b = Chunk(t_pairs[1:], d_t, halving(0, 2))
+    t_ga, t_res, i_attn = close_round([], t_ga, t_res, i_attn)
+
+    start(c1a, c1b)
     st_grads = self_attend_back(st_packed, H_T, my_len, True, t_ga)
     t_back = t_res + mm_t(st_grads, w_stp)
-    c2t = Chunk(third_items(st_grads, t_low), d_t, halving(2, 3, 0))
-    c2t.send, c2t.keep, t_back, i_attn = close_round([], c2t.send, c2t.keep, t_back, i_attn)
+    st_grads, t_back, i_attn = close_round([c1a, c1b], st_grads, t_back, i_attn)
+
+    start(c1a, c1b)
+    t_res, t_ga, t_pairs, t_gain_c = tail_backward(
+        t_back, t_kept, t_attn, w_cto, w_ctu, w_ctd, text_gains[0:2], True
+    )
+    c3a = Chunk([t_pairs[0], t_pairs[2]], d_t, halving(2, 0))
+    c3b = Chunk(t_pairs[1:2], d_t, halving(0, 2))
+    c3a.send, c3a.keep, c3b.send, c3b.keep, t_res, t_ga, i_attn = close_round(
+        [c1a, c1b], c3a.send, c3a.keep, c3b.send, c3b.keep, t_res, t_ga, i_attn
+    )
+    start(c1a, c1b, c3a, c3b)
+    (i_attn,) = close_round([c1a, c1b, c3a, c3b], i_attn)
 
     w_cio, w_ciu, w_cid = (image_wide[:, i * d_v : (i + 1) * d_v] for i in range(3))
     w_sip = image_wide[:, 3 * d_v : 6 * d_v]
     w_sio, w_siu, w_sid = (image_wide[:, (6 + i) * d_v : (7 + i) * d_v] for i in range(3))
 
-    c2t.start()
+    start(c3a, c3b, c1a, c1b)
     i_cross, i_kept = tail_forward(x_v.astype(FLOAT), i_attn, w_cio, w_ciu, w_cid, image_gains[0:2])
     i_low = i_cross.astype(BFLOAT)
+    if by_permute:
+        tall = -(-x_t.shape[0] // 8) * 8
+        seen = [x_v.reshape(-1, d_t), i_low.reshape(-1, d_t)]
+        seen += [jnp.pad(m, ((0, tall - m.shape[0]), (0, 0))) for m in (x_t, t_low)]
+        seen = jnp.concatenate(seen, axis=0)
     si_packed = project(i_low, w_sip)
     si_attn = self_attend(si_packed, H_V, my_len, False)
     i_final, si_kept = tail_forward(i_cross, si_attn, w_sio, w_siu, w_sid, image_gains[2:4])
@@ -624,81 +661,97 @@
         image_cotangent[0].astype(FLOAT), si_kept, si_attn, w_sio, w_siu, w_sid, image_gains[2:4], False
     )
     c1i = Chunk(i_pairs, d_v, halving(0, 2))
-    c1i.send, c1i.keep, i_ga, i_res, t_back = close_round(
-        [c2t], c1i.send, c1i.keep, i_ga, i_res, t_back
-    )
-
-    c2t.start()
-    c1i.start()
+    c1i.send, c1i.keep, i_ga, i_res = close_round(
+        [c1a, c1b, c3a, c3b], c1i.send, c1i.keep, i_ga, i_res
+    )
+    if by_permute:
+        seen = lax.all_gather(seen, ALL, axis=0)
+
+    start(c1i, c3a, c3b)
     si_grads = self_attend_back(si_packed, H_V, my_len, False, i_ga)
     i_back = i_res + mm_t(si_grads, w_sip)
-    c2i = Chunk(third_items(si_grads, i_low), d_v, halving(3, 0, 2))
-    c2i.send, c2i.keep, i_back, t_back = close_round(
-        [c2t, c1i], c2i.send, c2i.keep, i_back, t_back
-    )
-
-    for m in (c1i, c2i, c2t):
-        m.start()
-    t_res, t_ga, t_pairs, t_gain_c = tail_backward(
-        t_back, t_kept, t_attn, w_cto, w_ctu, w_ctd, text_gains[0:2], True
-    )
-    c3a = Chunk(t_pairs[:1], d_t, halving(2, 0))
-    c3a.send, c3a.keep, t_res, t_ga, i_back = close_round(
-        [c1i, c2i, c2t], c3a.send, c3a.keep, t_res, t_ga, i_back
-    )
-
-    for m in (c2i, c1i, c2t, c3a):
-        m.start()
+    si_grads, i_back = close_round([c1i, c3a, c3b], si_grads, i_back)
+    self_slices = t_low
+    if by_permute:
+        self_slices = exchange(by_owner(st_grads, own_t), by_owner(si_grads, own_v))
+
+    start(c1i, c3a, c3b)
     i_res, i_ga, i_pairs, i_gain_c = tail_backward(
         i_back, i_kept, i_attn, w_cio, w_ciu, w_cid, image_gains[0:2], True
     )
-    c3b = Whole(t_pairs[1:] + i_pairs, 2 * panel)
-    c3b.block, i_res, i_ga, t_ga = close_round([c2i, c1i, c2t, c3a], c3b.block, i_res, i_ga, t_ga)
-    c3b.launch()
-
-    for m in (c3a, c2i, c1i, c2t):
-        m.start()
+    c3x = Chunk(i_pairs[:1], d_v, halving(2, 0))
+    c3y = Chunk(i_pairs[1:], d_v, halving(0, 2))
+    c3x.send, c3x.keep, c3y.send, c3y.keep, i_res, i_ga, t_ga, self_slices = close_round(
+        [c1i, c3a, c3b], c3x.send, c3x.keep, c3y.send, c3y.keep, i_res, i_ga, t_ga, self_slices
+    )
+
+    start(c3x, c3y, c1i)
     t_grads, i_grads = cross_attend_back(t_packed, i_packed, my_len, t_ga, i_ga)
-    t_grads, i_grads = close_round([c3a, c2i, c1i, c2t], t_grads, i_grads)
-
-    for m in (c3a, c2i, c1i):
-        m.start()
-
-    def gain_item(products):
-        rows = jnp.concatenate(products, axis=0)
-        which = jnp.arange(rows.shape[0])[:, None] // products[0].shape[0]
-        return whole_item(rows, (which == jnp.arange(panel)[None, :]).astype(BFLOAT))
-
-    c4t = Chunk(third_items(t_grads, x_t) + [gain_item(t_gain_c + t_gain_s)], panel, halving(2, 0))
-    c4i = Chunk(third_items(i_grads, x_v) + [gain_item(i_gain_c + i_gain_s)], panel, halving(0, 2))
-    c4t.send, c4t.keep, c4i.send, c4i.keep, t_grads, i_grads = close_round(
-        [c3a, c2i], c4t.send, c4t.keep, c4i.send, c4i.keep, t_grads, i_grads
-    )
-
-    c4t.start()
-    c4i.start()
-    t_grads, i_grads = close_round([c4t, c4i, c1i], t_grads, i_grads)
-    for m in (c4t, c4i, c3a, c2i):
-        m.start()
+    t_grads, i_grads = close_round([c3x, c3y, c1i], t_grads, i_grads)
+
+    t_gain = jnp.stack(t_gain_c + t_gain_s)
+    i_gain = jnp.stack(i_gain_c + i_gain_s)
+    start(c3x, c3y, c1i)
+    if by_permute:
+        gain_rows = [t_gain.reshape(4, size, own_t), i_gain.reshape(4, size, own_v)]
+        gain_rows = [
+            jnp.pad(g.astype(BFLOAT), ((0, 0), (0, 0), (0, 3 * own_v - g.shape[2]))) for g in gain_rows
+        ]
+        gain_rows = jnp.concatenate(gain_rows, axis=0).transpose(1, 0, 2)
+        cross_slices = exchange(by_owner(t_grads, own_c), by_owner(i_grads, own_c), gain_rows)
+    close_round([c3x, c3y, c1i])
+    start(c3x, c3y, c1i)
     text_input_grad = t_res + mm_t(t_grads, w_ctp)
     image_input_grad = i_res + mm_t(i_grads, w_cip)
-    text_input_grad, image_input_grad, c1t.sum = close_round(
-        [c4t, c4i, c3a, c2i], text_input_grad, image_input_grad, c1t.sum
-    )
-    for m in (c4t, c4i, c3a):
-        m.start()
-    close_round([c4t, c4i, c3a])
-    for last_turn in range(2, bits - 1):
-        for m in (c4t, c4i):
-            m.start()
-        if last_turn == bits - 2:
-            (c3b.sum,) = close_round([c4t, c4i], c3b.sum)
-        else:
-            close_round([c4t, c4i])
-    for m in (c1i, c2t, c2i, c3a, c4t, c4i):
+    text_input_grad, image_input_grad = close_round([c3x, c3y, c1i], text_input_grad, image_input_grad)
+    start(c3x, c3y, c3a, c3b)
+    close_round([c3x, c3y, c3a, c3b])
+    start(c3x, c3y, c1a, c1b)
+    close_round([c3x, c3y, c1a, c1b])
+    for m in (c1a, c1b, c3a, c3b, c1i, c3x, c3y):
         while m.step < bits:
             m.start()
             m.absorb()
+
+    def slices_grad(rows, slices, own):
+        grad = t_mm(rows, slices)[:, : 3 * own]
+        return grad.reshape(grad.shape[0], 3, own).transpose(1, 0, 2)
+
+    if by_permute:
+        short = x_v.size // d_t
+        wide_v = x_v.shape[0]
+        tall_v = -(-wide_v // 8) * 8
+
+        def rows_of(at, rows):
+            return seen[:, at : at + rows]
+
+        def flat_slices(slices, at, rows):
+            return slices[:, at : at + rows].reshape(-1, slices.shape[2])
+
+        all_v = rows_of(0, short).reshape(-1, d_v)
+        all_low_v = rows_of(short, short).reshape(-1, d_v)
+        all_t = rows_of(2 * short, tall).reshape(-1, d_t)
+        all_low_t = rows_of(2 * short + tall, tall).reshape(-1, d_t)
+        o_stp = slices_grad(all_low_t, flat_slices(self_slices, 0, tall), own_t)
+        o_sip = slices_grad(all_low_v, flat_slices(self_slices, tall, wide_v), own_v)
+        o_ctp = slices_grad(all_t, flat_slices(cross_slices, 0, tall), own_c)
+        o_cip = slices_grad(all_v, flat_slices(cross_slices, tall, wide_v), own_c)
+        gain_sum = jnp.sum(cross_slices[:, tall + tall_v :].astype(FLOAT), axis=0)
+        o_tg, o_ig = gain_sum[:4, :own_t], gain_sum[4:, :own_v]
+    else:
+
+        def by_scatter(packed, rows):
+            whole = Whole(third_items(packed, rows), rows.shape[1])
+            whole.launch()
+            block = whole.finish()
+            return block.reshape(3, block.shape[0] // 3, block.shape[1]).transpose(0, 2, 1)
+
+        o_stp, o_sip = by_scatter(st_grads, t_low), by_scatter(si_grads, i_low)
+        o_ctp, o_cip = by_scatter(t_grads, x_t), by_scatter(i_grads, x_v)
+        at = my_index()
+        t_gain, i_gain = lax.psum(t_gain, ALL), lax.psum(i_gain, ALL)
+        o_tg = lax.dynamic_slice_in_dim(t_gain, at * own_t, own_t, 1)
+        o_ig = lax.dynamic_slice_in_dim(i_gain, at * own_v, own_v, 1)
 
     def cut(block, rows):
         out, at = [], 0
@@ -707,40 +760,18 @@
             at += r
         return out
 
-    def widen(block, rows, width):
-        wide = block.shape[1]
-        return block.reshape(width // wide, rows, wide).transpose(1, 0, 2).reshape(rows, width)
-
-    def thirds(block, rows, width):
-        many = rows * (width // panel)
-        return jnp.concatenate(
-            [widen(block[e * many : (e + 1) * many], rows, width) for e in range(3)], axis=0
-        )
-
-    g_std, g_stu, g_sto = cut(c1t.finish(), (ff_t // d_t * own_t, own_f, own_t))
+    (g_std,) = cut(c1a.full, (ff_t // d_t * own_t,))
+    g_stu, g_sto = cut(c1b.full, (own_f, own_t))
     g_sid, g_siu, g_sio = cut(c1i.full, (own_v,) * 3)
-    g_ctd = c3a.full
-    kinds = [(own_f, d_t), (own_c, d_t)] + [(own_v, d_v)] * 3
-    parts = cut(c3b.finish(), [rows * (width // (2 * panel)) for rows, width in kinds])
-    g_ctu, g_cto, g_cid, g_ciu, g_cio = (widen(p, *kind) for p, kind in zip(parts, kinds))
+    g_ctd, g_cto = cut(c3a.full, (own_f, own_c))
+    g_ctu, g_cid = c3b.full, c3x.full
+    g_ciu, g_cio = cut(c3y.full, (own_v,) * 2)
     g_std = g_std.reshape(ff_t // d_t, own_t, d_t).transpose(1, 0, 2).reshape(own_t, ff_t)
-    g_stp, g_sip = c2t.full, c2i.full
-    g_ctp, g_cip = thirds(c4t.full, own_c, d_t), thirds(c4i.full, own_c, d_v)
-    t_gain = c4t.full[-own_t:, :4].T
-    i_gain = c4i.full[-own_v:, :4].T
-
-    def by_three(rows):
-        return rows.reshape(3, rows.shape[0] // 3, rows.shape[1]).transpose(0, 2, 1)
 
     o_stu, o_ctu, o_ctd = g_stu.T, g_ctu.T, g_ctd
     o_std, o_sto = g_std.T, g_sto
-    o_stp = by_three(g_stp)
     o_sid, o_siu, o_sio = g_sid.T, g_siu.T, g_sio
-    o_sip = by_three(g_sip)
     o_cid, o_ciu, o_cio, o_cto = g_cid, g_ciu.T, g_cio, g_cto
-    o_cip = by_three(g_cip)
-    o_ctp = by_three(g_ctp)
-    o_tg, o_ig = t_gain, i_gain
     return (
         t_final.astype(BFLOAT)[None],
         i_final.astype(BFLOAT)[None],

time: 742 us -> 726 us (0.978)
  waiting for transfers between devices: 370 us -> 289 us
  starting transfers between devices: 48.8 us -> 80.8 us
  local copies, waits for them, and re-layouts: 63.8 us -> 89.7 us
  Pallas kernels: 76.8 us -> 61.6 us
  other arithmetic: 64.3 us -> 78.5 us
    ppermute x45 -> x50, waiting for transfers between devices: 350 us -> 289 us  [swap(): return lax.ppermute(block, ALL, [(i, i ^ 1 << bit) for i in range(size)])]
    all_to_all x0 -> x2, starting transfers between devices: none -> 23.4 us  [exchange(): lax.all_to_all(jnp.concatenate(blocks, axis=1), ALL, split_axis=0, concat...]
    all_gather x2, waiting for transfers between devices: 19.4 us -> 0.02 us  [gather_columns(): return lax.all_gather(side(parts), ALL, axis=0, tiled=True)]
    convert_element_type x24 -> x28, other arithmetic: 36.2 us -> 51.7 us  [add_low(): return (left.astype(FLOAT) + right.astype(FLOAT)).astype(BFLOAT)]
    pallas_call x3, Pallas kernels: 15.9 us -> 3.65 us  [join_blocks(): pl.pallas_call(body, grid_spec=pltpu.PrefetchScalarGridSpec(num_scalar_pr...]
    slice x2 -> x8, local copies, waits for them, and re-layouts: 0.05 us -> 12.1 us  [the longest x2 9.17 us: rows_of(): return seen[:, at:at + rows]]
    dot_general x0 -> x4, matrix products: none -> 11.4 us  [t_mm(): lax.dot_general(left, right, (((0,), (0,)), ((), ())), preferred_element_...]
    ppermute x45 -> x50, starting transfers between devices: 48.5 us -> 57.3 us  [swap(): return lax.ppermute(block, ALL, [(i, i ^ 1 << bit) for i in range(size)])]
  transfers between devices with their start and end apart: 49 -> 55, of which waited for: 31 -> 23; matrix products, arithmetic and copies ran while one was open for 25% -> 27% of each run, Pallas kernels for 10% -> 9%
where the time goes in v2:
time: 726 us; the launch traced here: 715 us
  waiting for transfers between devices  289 us (40%)
  matrix products  99.1 us (14%)
  local copies, waits for them, and re-layouts  89.7 us (12%)
  starting transfers between devices  80.8 us (11%)
  other arithmetic  78.5 us (11%)
  Pallas kernels  61.6 us (8%)
  between operations  16.1 us (2%)
    ppermute x50, waiting for transfers between devices, swap(): return lax.ppermute(block, ALL, [(i, i ^ 1 << bit) for i in range(size)])  289 us
    ppermute x50, starting transfers between devices, swap(): return lax.ppermute(block, ALL, [(i, i ^ 1 << bit) for i in range(size)])  57.3 us
    convert_element_type x28, other arithmetic, add_low(): return (left.astype(FLOAT) + right.astype(FLOAT)).astype(BFLOAT)  51.7 us
    dot_general x16, matrix products, mm_t(): lax.dot_general(left, right, (((1,), (1,)), ((), ())), preferred_element_...  50.7 us
    unnamed x306, local copies, waits for them, and re-layouts  37.4 us
    dot_general x16, matrix products, mm(): return jnp.dot(left, right, preferred_element_type=FLOAT)  37.1 us
    pallas_call x7, Pallas kernels, pack_kernel(): pl.pallas_call(body, grid_spec=pltpu.PrefetchScalarGridSpec(num_scalar_pr...  33.1 us
    pallas_call x6, Pallas kernels, vmem_call(): pl.pallas_call(body, in_specs=[pl.BlockSpec(memory_space=pltpu.SMEM)] + [...  24.9 us
  transfers between devices with their start and end apart: 55, of which 23 were waited for; matrix products, arithmetic and copies ran while one was open for 27% of the time, Pallas kernels for 9%

profile of v2, /device:TPU:0, one launch (start us, length us, event | category | flops | bytes accessed | tf_op | source)
XLA Modules:
  0.0 715.2 jit_solution(7256623379089730362)
XLA Ops:
  21.1 22.1 %collective-permute-done = bf16[1,32,3072]{2,1,0:T(8,128)(2,1)S(1)} collective-permute-done((bf16[1,32,3072]{2,1,0:T(8,128)(2,1)S(1)}, bf16[1,32,3072]{2,1,0:T(8,128)(2,1)S(1)}, u32[]{:S(2)}, u32[]{:S(2)}) %collective-permute-start) | collective-permute-done | bytes 196640 | tf_op jit(solution)/shard_map/ppermute | solution.py:30
  43.3 7.9 %collective-permute-done.1 = bf16[1,128,768]{2,1,0:T(8,128)(2,1)S(1)} collective-permute-done((bf16[1,128,768]{2,1,0:T(8,128)(2,1)S(1)}, bf16[1,128,768]{2,1,0:T(8,128)(2,1)S(1)}, u32[]{:S(2)}, u32[]{:S(2)}) %collective-permute-start.1) | collective-permute-done | bytes 196640 | tf_op jit(solution)/shard_map/ppermute | solution.py:30
  53.4 21.3 %collective-permute-done.2 = bf16[2,32,3072]{2,1,0:T(8,128)(2,1)S(1)} collective-permute-done((bf16[2,32,3072]{2,1,0:T(8,128)(2,1)S(1)}, bf16[2,32,3072]{2,1,0:T(8,128)(2,1)S(1)}, u32[]{:S(2)}, u32[]{:S(2)}) %collective-permute-start.2) | collective-permute-done | bytes 393248 | tf_op jit(solution)/shard_map/ppermute | solution.py:30
  74.7 20.8 %collective-permute-done.3 = bf16[2,128,768]{2,1,0:T(8,128)(2,1)S(1)} collective-permute-done((bf16[2,128,768]{2,1,0:T(8,128)(2,1)S(1)}, bf16[2,128,768]{2,1,0:T(8,128)(2,1)S(1)}, u32[]{:S(2)}, u32[]{:S(2)}) %collective-permute-start.3) | collective-permute-done | bytes 393248 | tf_op jit(solution)/shard_map/ppermute | solution.py:30
  100.9 12.8 %collective-permute-done.6 = bf16[1,96,768]{2,1,0:T(8,128)(2,1)S(1)} collective-permute-done((bf16[1,96,768]{2,1,0:T(8,128)(2,1)S(1)}, bf16[1,96,768]{2,1,0:T(8,128)(2,1)S(1)}, u32[]{:S(2)}, u32[]{:S(2)}) %collective-permute-start.6) | collective-permute-done | bytes 147488 | tf_op jit(solution)/shard_map/ppermute | solution.py:30
  113.8 6.7 collective-permute-done.4
  127.4 10.5 %collective-permute-done.9 = bf16[2,96,768]{2,1,0:T(8,128)(2,1)S(1)} collective-permute-done((bf16[2,96,768]{2,1,0:T(8,128)(2,1)S(1)}, bf16[2,96,768]{2,1,0:T(8,128)(2,1)S(1)}, u32[]{:S(2)}, u32[]{:S(2)}) %collective-permute-start.9) | collective-permute-done | bytes 294944 | tf_op jit(solution)/shard_map/ppermute | solution.py:30
  137.9 38.3 %collective-permute-done.7 = bf16[8,32,3072]{2,1,0:T(8,128)(2,1)S(1)} collective-permute-done((bf16[8,32,3072]{2,1,0:T(8,128)(2,1)S(1)}, bf16[8,32,3072]{2,1,0:T(8,128)(2,1)S(1)}, u32[]{:S(2)}, u32[]{:S(2)}) %collective-permute-start.7) | collective-permute-done | bytes 1572896 | tf_op jit(solution)/shard_map/ppermute | solution.py:30
  180.7 13.8 %collective-permute-done.12 = bf16[4,96,768]{2,1,0:T(8,128)(2,1)S(1)} collective-permute-done((bf16[4,96,768]{2,1,0:T(8,128)(2,1)S(1)}, bf16[4,96,768]{2,1,0:T(8,128)(2,1)S(1)}, u32[]{:S(2)}, u32[]{:S(2)}) %collective-permute-start.12) | collective-permute-done | bytes 589856 | tf_op jit(solution)/shard_map/ppermute | solution.py:30
  219.3 11.1 %collective-permute-done.13 = bf16[8,96,768]{2,1,0:T(8,128)(2,1)} collective-permute-done((bf16[8,96,768]{2,1,0:T(8,128)(2,1)}, bf16[8,96,768]{2,1,0:T(8,128)(2,1)}, u32[]{:S(2)}, u32[]{:S(2)}) %collective-permute-start.13) | collective-permute-done | bytes 1179680 | tf_op jit(solution)/shard_map/ppermute | solution.py:30
  233.4 4.7 fusion.92
  265.7 5.4 shard_map.396
  275.5 5.4 shard_map.395
  286.6 5.9 shard_map.397
  311.4 5.1 shard_map.399
  318.8 5.7 shard_map.398
  325.8 5.1 collective-permute-done.17
  330.9 5.2 collective-permute-done.18
  343.2 12.9 %collective-permute-done.19 = bf16[4,96,768]{2,1,0:T(8,128)(2,1)} collective-permute-done((bf16[4,96,768]{2,1,0:T(8,128)(2,1)}, bf16[4,96,768]{2,1,0:T(8,128)(2,1)}, u32[]{:S(2)}, u32[]{:S(2)}) %collective-permute-start.19) | collective-permute-done | bytes 589856 | tf_op jit(solution)/shard_map/ppermute | solution.py:30
  404.7 5.5 shard_map.401
  417.1 7.2 %collective-permute-done.25 = bf16[8,128,768]{2,1,0:T(8,128)(2,1)S(1)} collective-permute-done((bf16[8,128,768]{2,1,0:T(8,128)(2,1)S(1)}, bf16[8,128,768]{2,1,0:T(8,128)(2,1)S(1)}, u32[]{:S(2)}, u32[]{:S(2)}) %collective-permute-start.25) | collective-permute-done | bytes 1572896 | tf_op jit(solution)/shard_map/ppermute | solution.py:30
  441.9 5.5 fusion.128
  447.4 11.6 %collective-permute-done.29 = bf16[4,96,768]{2,1,0:T(8,128)(2,1)} collective-permute-done((bf16[4,96,768]{2,1,0:T(8,128)(2,1)}, bf16[4,96,768]{2,1,0:T(8,128)(2,1)}, u32[]{:S(2)}, u32[]{:S(2)}) %collective-permute-start.29) | collective-permute-done | bytes 589856 | tf_op jit(solution)/shard_map/ppermute | solution.py:30
  463.2 5.1 fusion.64
  473.7 19.6 %all-to-all-start = ((bf16[32,144,96]{2,1,0:T(8,128)(2,1)}), bf16[32,144,96]{2,1,0:T(8,128)(2,1)}, u32[]{:S(2)}, u32[]{:S(2)}) async-start(bf16[32,144,96]{2,1,0:T(8,128)(2,1)} %copy.176), calls=%async_computation | async-start | bytes 2359296 | tf_op jit(solution)/shard_map/all_to_all | solution.py:620
  514.5 34.1 %collective-permute-done.32 = bf16[2,96,768]{2,1,0:T(8,128)(2,1)S(1)} collective-permute-done((bf16[2,96,768]{2,1,0:T(8,128)(2,1)}, bf16[2,96,768]{2,1,0:T(8,128)(2,1)S(1)}, u32[]{:S(2)}, u32[]{:S(2)}) %collective-permute-start.32) | collective-permute-done | bytes 294944 | tf_op jit(solution)/shard_map/ppermute | solution.py:30
  557.6 8.0 %shard_map.405 = (bf16[100,3072]{1,0:T(8,128)(2,1)S(1)}, bf16[36,3072]{1,0:T(8,128)(2,1)S(1)}) custom-call(s32[1]{0:T(128)} %dynamic_slice.308.len_ref, bf16[100,3072]{1,0:T(8,128)(2,1)S(1)} %copy-done.14, bf16[36,3072]{1,0:T(8,128)(2,1)S(1)} %fusion.27.image_ref, bf16[100,1024]{1,0:T(8,128)(2,1)S(1)} %copy-done.33, bf16[36,1024]{1,0:T(8,128)(2,1)S(1)} %fusion.131.ig_ref), custom_call_target="tpu_custom_call" | custom-call | tf_op jit(solution)/shard_map/pallas_call | solution.py:404
  565.5 10.1 %collective-permute-done.35 = bf16[4,96,1024]{2,1,0:T(8,128)(2,1)S(1)} collective-permute-done((bf16[4,96,1024]{2,1,0:T(8,128)(2,1)S(1)}, bf16[4,96,1024]{2,1,0:T(8,128)(2,1)S(1)}, u32[]{:S(2)}, u32[]{:S(2)}) %collective-permute-start.35) | collective-permute-done | bytes 786464 | tf_op jit(solution)/shard_map/ppermute | solution.py:30
  612.1 4.8 convolution_add_fusion.4
  624.8 20.3 %collective-permute-done.41 = bf16[1,96,1024]{2,1,0:T(8,128)(2,1)S(1)} collective-permute-done((bf16[1,96,1024]{2,1,0:T(8,128)(2,1)S(1)}, bf16[1,96,1024]{2,1,0:T(8,128)(2,1)S(1)}, u32[]{:S(2)}, u32[]{:S(2)}) %collective-permute-start.41) | collective-permute-done | bytes 196640 | tf_op jit(solution)/shard_map/ppermute | solution.py:30
  683.1 5.1 slice.240
  688.2 5.1 reshape.992
  (617 shorter events, 336.4 us)
Async XLA Ops:
  7.3 205.2 %all-gather.5.cloned.1.call-start = ((), (), s32[]{:S(2)}) async-start(), calls=%async_computation.2 | async-start | bytes 19464192 | tf_op jit(solution)/shard_map/all_gather | solution.py:543
  15.7 355.2 %all-gather.7.cloned.1.call-start = ((), (), s32[]{:S(2)}) async-start(), calls=%async_computation.3 | async-start | bytes 19464192 | tf_op jit(solution)/shard_map/all_gather | solution.py:543
  16.8 662.2 %all-gather.9.cloned.1.call-start = ((), (), s32[]{:S(2)}) async-start(), calls=%async_computation.4 | async-start | bytes 15409152 | tf_op jit(solution)/shard_map/all_gather | solution.py:668
  16.9 26.4 %collective-permute-start = (bf16[1,32,3072]{2,1,0:T(8,128)(2,1)S(1)}, bf16[1,32,3072]{2,1,0:T(8,128)(2,1)S(1)}, u32[]{:S(2)}, u32[]{:S(2)}) collective-permute-start(bf16[1,32,3072]{2,1,0:T(8,128)(2,1)S(1)} %maximum_bitcast_fusion), channel_id=1, source_target_pairs={{0,16},{1,17},{2,18},{3,19},{4,20},{5,21},{6,22},{7,23},{8,24},{9,... | collective-permute-start | bytes 589832 | tf_op jit(solution)/shard_map/ppermute | solution.py:30
  21.0 30.2 %collective-permute-start.1 = (bf16[1,128,768]{2,1,0:T(8,128)(2,1)S(1)}, bf16[1,128,768]{2,1,0:T(8,128)(2,1)S(1)}, u32[]{:S(2)}, u32[]{:S(2)}) collective-permute-start(bf16[1,128,768]{2,1,0:T(8,128)(2,1)S(1)} %maximum_bitcast_fusion.1), channel_id=1, source_target_pairs={{0,16},{1,17},{2,18},{3,19},{4,20},{5,21},{6,22},{7,23},{8,24},{9,... | collective-permute-start | bytes 589832 | tf_op jit(solution)/shard_map/ppermute | solution.py:30
  52.1 43.4 %collective-permute-start.3 = (bf16[2,128,768]{2,1,0:T(8,128)(2,1)S(1)}, bf16[2,128,768]{2,1,0:T(8,128)(2,1)S(1)}, u32[]{:S(2)}, u32[]{:S(2)}) collective-permute-start(bf16[2,128,768]{2,1,0:T(8,128)(2,1)S(1)} %pad_maximum_fusion.10), channel_id=1, source_target_pairs={{0,8},{1,9},{2,10},{3,11},{4,12},{5,13},{6,14},{7,15},{8,0},{9,1},... | collective-permute-start | bytes 1179656 | tf_op jit(solution)/shard_map/ppermute | solution.py:30
  95.6 24.8 %collective-permute-start.4 = (bf16[4,32,3072]{2,1,0:T(8,128)(2,1)S(1)}, bf16[4,32,3072]{2,1,0:T(8,128)(2,1)S(1)}, u32[]{:S(2)}, u32[]{:S(2)}) collective-permute-start(bf16[4,32,3072]{2,1,0:T(8,128)(2,1)S(1)} %pad_maximum_fusion.6), channel_id=1, source_target_pairs={{0,1},{1,0},{2,3},{3,2},{4,5},{5,4},{6,7},{7,6},{8,9},{9,8},{10,11... | collective-permute-start | bytes 2359304 | tf_op jit(solution)/shard_map/ppermute | solution.py:30
  96.8 27.7 %collective-permute-start.5 = (bf16[4,128,768]{2,1,0:T(8,128)(2,1)S(1)}, bf16[4,128,768]{2,1,0:T(8,128)(2,1)S(1)}, u32[]{:S(2)}, u32[]{:S(2)}) collective-permute-start(bf16[4,128,768]{2,1,0:T(8,128)(2,1)S(1)} %pad_maximum_fusion.7), channel_id=1, source_target_pairs={{0,4},{1,5},{2,6},{3,7},{4,0},{5,1},{6,2},{7,3},{8,12},{9,13},{10,... | collective-permute-start | bytes 2359304 | tf_op jit(solution)/shard_map/ppermute | solution.py:30
  124.8 51.4 %collective-permute-start.7 = (bf16[8,32,3072]{2,1,0:T(8,128)(2,1)S(1)}, bf16[8,32,3072]{2,1,0:T(8,128)(2,1)S(1)}, u32[]{:S(2)}, u32[]{:S(2)}) collective-permute-start(bf16[8,32,3072]{2,1,0:T(8,128)(2,1)S(1)} %pad_maximum_fusion.3), channel_id=1, source_target_pairs={{0,4},{1,5},{2,6},{3,7},{4,0},{5,1},{6,2},{7,3},{8,12},{9,13},{10,... | collective-permute-start | bytes 4718600 | tf_op jit(solution)/shard_map/ppermute | solution.py:30
  127.4 48.8 %collective-permute-start.8 = (bf16[8,128,768]{2,1,0:T(8,128)(2,1)S(1)}, bf16[8,128,768]{2,1,0:T(8,128)(2,1)S(1)}, u32[]{:S(2)}, u32[]{:S(2)}) collective-permute-start(bf16[8,128,768]{2,1,0:T(8,128)(2,1)S(1)} %pad_maximum_fusion.4), channel_id=1, source_target_pairs={{0,1},{1,0},{2,3},{3,2},{4,5},{5,4},{6,7},{7,6},{8,9},{9,8},{10,11... | collective-permute-start | bytes 4718600 | tf_op jit(solution)/shard_map/ppermute | solution.py:30
  198.9 31.6 %collective-permute-start.13 = (bf16[8,96,768]{2,1,0:T(8,128)(2,1)}, bf16[8,96,768]{2,1,0:T(8,128)(2,1)}, u32[]{:S(2)}, u32[]{:S(2)}) collective-permute-start(bf16[8,96,768]{2,1,0:T(8,128)(2,1)} %pad_maximum_fusion.5), channel_id=1, source_target_pairs={{0,1},{1,0},{2,3},{3,2},{4,5},{5,4},{6,7},{7,6},{8,9},{9,8},{10,11... | collective-permute-start | bytes 3538952 | tf_op jit(solution)/shard_map/ppermute | solution.py:30
  271.2 25.2 %collective-permute-start.16 = (bf16[16,120,768]{2,1,0:T(8,128)(2,1)}, bf16[16,120,768]{2,1,0:T(8,128)(2,1)}, u32[]{:S(2)}, u32[]{:S(2)}) collective-permute-start(bf16[16,120,768]{2,1,0:T(8,128)(2,1)} %bitcast.33), channel_id=1, source_target_pairs={{0,2},{1,3},{2,0},{3,1},{4,6},{5,7},{6,4},{7,5},{8,10},{9,11},{10,... | collective-permute-start | bytes 8847368 | tf_op jit(solution)/shard_map/ppermute | solution.py:30
  301.5 34.5 %collective-permute-start.18 = (bf16[8,120,768]{2,1,0:T(8,128)(2,1)S(1)}, bf16[8,120,768]{2,1,0:T(8,128)(2,1)S(1)}, u32[]{:S(2)}, u32[]{:S(2)}) collective-permute-start(bf16[8,120,768]{2,1,0:T(8,128)(2,1)S(1)} %get-tuple-element.262), channel_id=1, source_target_pairs={{0,1},{1,0},{2,3},{3,2},{4,5},{5,4},{6,7},{7,6},{8,9},{9,8},{10,11... | collective-permute-start | bytes 4423688 | tf_op jit(solution)/shard_map/ppermute | solution.py:30
  303.1 27.8 %collective-permute-start.17 = (bf16[8,96,768]{2,1,0:T(8,128)(2,1)S(1)}, bf16[8,96,768]{2,1,0:T(8,128)(2,1)S(1)}, u32[]{:S(2)}, u32[]{:S(2)}) collective-permute-start(bf16[8,96,768]{2,1,0:T(8,128)(2,1)S(1)} %get-tuple-element.261), channel_id=1, source_target_pairs={{0,4},{1,5},{2,6},{3,7},{4,0},{5,1},{6,2},{7,3},{8,12},{9,13},{10,... | collective-permute-start | bytes 3538952 | tf_op jit(solution)/shard_map/ppermute | solution.py:30
  385.4 38.9 %collective-permute-start.25 = (bf16[8,128,768]{2,1,0:T(8,128)(2,1)S(1)}, bf16[8,128,768]{2,1,0:T(8,128)(2,1)S(1)}, u32[]{:S(2)}, u32[]{:S(2)}) collective-permute-start(bf16[8,128,768]{2,1,0:T(8,128)(2,1)S(1)} %copy-done.61), channel_id=1, source_target_pairs={{0,4},{1,5},{2,6},{3,7},{4,0},{5,1},{6,2},{7,3},{8,12},{9,13},{10,... | collective-permute-start | bytes 4718600 | tf_op jit(solution)/shard_map/ppermute | solution.py:30
  387.0 30.1 %collective-permute-start.26 = (bf16[8,96,768]{2,1,0:T(8,128)(2,1)S(1)}, bf16[8,96,768]{2,1,0:T(8,128)(2,1)S(1)}, u32[]{:S(2)}, u32[]{:S(2)}) collective-permute-start(bf16[8,96,768]{2,1,0:T(8,128)(2,1)S(1)} %copy-done.71), channel_id=1, source_target_pairs={{0,1},{1,0},{2,3},{3,2},{4,5},{5,4},{6,7},{7,6},{8,9},{9,8},{10,11... | collective-permute-start | bytes 3538952 | tf_op jit(solution)/shard_map/ppermute | solution.py:30
  388.0 25.3 %collective-permute-start.24 = (bf16[2,120,768]{2,1,0:T(8,128)(2,1)S(1)}, bf16[2,120,768]{2,1,0:T(8,128)(2,1)S(1)}, u32[]{:S(2)}, u32[]{:S(2)}) collective-permute-start(bf16[2,120,768]{2,1,0:T(8,128)(2,1)S(1)} %copy-done.85), channel_id=1, source_target_pairs={{0,8},{1,9},{2,10},{3,11},{4,12},{5,13},{6,14},{7,15},{8,0},{9,1},... | collective-permute-start | bytes 1105928 | tf_op jit(solution)/shard_map/ppermute | solution.py:30
  388.0 25.2 %collective-permute-start.23 = (bf16[2,96,768]{2,1,0:T(8,128)(2,1)S(1)}, bf16[2,96,768]{2,1,0:T(8,128)(2,1)S(1)}, u32[]{:S(2)}, u32[]{:S(2)}) collective-permute-start(bf16[2,96,768]{2,1,0:T(8,128)(2,1)S(1)} %copy-done.96), channel_id=1, source_target_pairs={{0,8},{1,9},{2,10},{3,11},{4,12},{5,13},{6,14},{7,15},{8,0},{9,1},... | collective-permute-start | bytes 884744 | tf_op jit(solution)/shard_map/ppermute | solution.py:30
  429.1 29.9 %collective-permute-start.27 = (bf16[16,96,1024]{2,1,0:T(8,128)(2,1)}, bf16[16,96,1024]{2,1,0:T(8,128)(2,1)}, u32[]{:S(2)}, u32[]{:S(2)}) collective-permute-start(bf16[16,96,1024]{2,1,0:T(8,128)(2,1)} %bitcast.71), channel_id=1, source_target_pairs={{0,2},{1,3},{2,0},{3,1},{4,6},{5,7},{6,4},{7,5},{8,10},{9,11},{10,... | collective-permute-start | bytes 9437192 | tf_op jit(solution)/shard_map/ppermute | solution.py:30
  429.1 29.9 %collective-permute-start.28 = (bf16[4,128,768]{2,1,0:T(8,128)(2,1)}, bf16[4,128,768]{2,1,0:T(8,128)(2,1)}, u32[]{:S(2)}, u32[]{:S(2)}) collective-permute-start(bf16[4,128,768]{2,1,0:T(8,128)(2,1)} %get-tuple-element.311), channel_id=1, source_target_pairs={{0,1},{1,0},{2,3},{3,2},{4,5},{5,4},{6,7},{7,6},{8,9},{9,8},{10,11... | collective-permute-start | bytes 2359304 | tf_op jit(solution)/shard_map/ppermute | solution.py:30
  430.6 28.4 %collective-permute-start.29 = (bf16[4,96,768]{2,1,0:T(8,128)(2,1)}, bf16[4,96,768]{2,1,0:T(8,128)(2,1)}, u32[]{:S(2)}, u32[]{:S(2)}) collective-permute-start(bf16[4,96,768]{2,1,0:T(8,128)(2,1)} %get-tuple-element.312), channel_id=1, source_target_pairs={{0,4},{1,5},{2,6},{3,7},{4,0},{5,1},{6,2},{7,3},{8,12},{9,13},{10,... | collective-permute-start | bytes 1769480 | tf_op jit(solution)/shard_map/ppermute | solution.py:30
  473.7 75.6 %all-to-all-start = ((bf16[32,144,96]{2,1,0:T(8,128)(2,1)}), bf16[32,144,96]{2,1,0:T(8,128)(2,1)}, u32[]{:S(2)}, u32[]{:S(2)}) async-start(bf16[32,144,96]{2,1,0:T(8,128)(2,1)} %copy.176), calls=%async_computation | async-start | bytes 2359296 | tf_op jit(solution)/shard_map/all_to_all | solution.py:620
  493.3 56.0 %collective-permute-start.30 = (bf16[8,96,1024]{2,1,0:T(8,128)(2,1)}, bf16[8,96,1024]{2,1,0:T(8,128)(2,1)}, u32[]{:S(2)}, u32[]{:S(2)}) collective-permute-start(bf16[8,96,1024]{2,1,0:T(8,128)(2,1)} %get-tuple-element.321), channel_id=1, source_target_pairs={{0,1},{1,0},{2,3},{3,2},{4,5},{5,4},{6,7},{7,6},{8,9},{9,8},{10,11... | collective-permute-start | bytes 4718600 | tf_op jit(solution)/shard_map/ppermute | solution.py:30
  495.2 54.1 %collective-permute-start.31 = (bf16[2,128,768]{2,1,0:T(8,128)(2,1)}, bf16[2,128,768]{2,1,0:T(8,128)(2,1)}, u32[]{:S(2)}, u32[]{:S(2)}) collective-permute-start(bf16[2,128,768]{2,1,0:T(8,128)(2,1)} %get-tuple-element.322), channel_id=1, source_target_pairs={{0,8},{1,9},{2,10},{3,11},{4,12},{5,13},{6,14},{7,15},{8,0},{9,1},... | collective-permute-start | bytes 1179656 | tf_op jit(solution)/shard_map/ppermute | solution.py:30
  496.7 51.9 %collective-permute-start.32 = (bf16[2,96,768]{2,1,0:T(8,128)(2,1)}, bf16[2,96,768]{2,1,0:T(8,128)(2,1)S(1)}, u32[]{:S(2)}, u32[]{:S(2)}) collective-permute-start(bf16[2,96,768]{2,1,0:T(8,128)(2,1)} %get-tuple-element.323), channel_id=1, source_target_pairs={{0,8},{1,9},{2,10},{3,11},{4,12},{5,13},{6,14},{7,15},{8,0},{9,1},... | collective-permute-start | bytes 884744 | tf_op jit(solution)/shard_map/ppermute | solution.py:30
  580.3 25.9 %collective-permute-start.37 = (bf16[8,64,1024]{2,1,0:T(8,128)(2,1)}, bf16[8,64,1024]{2,1,0:T(8,128)(2,1)}, u32[]{:S(2)}, u32[]{:S(2)}) collective-permute-start(bf16[8,64,1024]{2,1,0:T(8,128)(2,1)} %get-tuple-element.358), channel_id=1, source_target_pairs={{0,1},{1,0},{2,3},{3,2},{4,5},{5,4},{6,7},{7,6},{8,9},{9,8},{10,11... | collective-permute-start | bytes 3145736 | tf_op jit(solution)/shard_map/ppermute | solution.py:30
  585.3 84.2 %collective-permute-start.49 = (bf16[1,120,768]{2,1,0:T(8,128)(2,1)}, bf16[1,120,768]{2,1,0:T(8,128)(2,1)}, u32[]{:S(2)}, u32[]{:S(2)}) collective-permute-start(bf16[1,120,768]{2,1,0:T(8,128)(2,1)} %fusion.169), channel_id=1, source_target_pairs={{0,16},{1,17},{2,18},{3,19},{4,20},{5,21},{6,22},{7,23},{8,24},{9,... | collective-permute-start | bytes 552968 | tf_op jit(solution)/shard_map/ppermute | solution.py:30
  594.6 64.1 %collective-permute-start.44 = (bf16[1,128,768]{2,1,0:T(8,128)(2,1)}, bf16[1,128,768]{2,1,0:T(8,128)(2,1)}, u32[]{:S(2)}, u32[]{:S(2)}) collective-permute-start(bf16[1,128,768]{2,1,0:T(8,128)(2,1)} %fusion.166), channel_id=1, source_target_pairs={{0,16},{1,17},{2,18},{3,19},{4,20},{5,21},{6,22},{7,23},{8,24},{9,... | collective-permute-start | bytes 589832 | tf_op jit(solution)/shard_map/ppermute | solution.py:30
  602.4 49.9 %all-to-all-start.1 = ((bf16[32,152,96]{2,1,0:T(8,128)(2,1)}), bf16[32,152,96]{2,1,0:T(8,128)(2,1)S(1)}, u32[]{:S(2)}, u32[]{:S(2)}) async-start(bf16[32,152,96]{2,1,0:T(8,128)(2,1)} %copy.185), calls=%async_computation.1 | async-start | bytes 2490368 | tf_op jit(solution)/shard_map/all_to_all | solution.py:620
  610.3 34.7 %collective-permute-start.40 = (bf16[4,64,1024]{2,1,0:T(8,128)(2,1)S(1)}, bf16[4,64,1024]{2,1,0:T(8,128)(2,1)S(1)}, u32[]{:S(2)}, u32[]{:S(2)}) collective-permute-start(bf16[4,64,1024]{2,1,0:T(8,128)(2,1)S(1)} %get-tuple-element.364), channel_id=1, source_target_pairs={{0,4},{1,5},{2,6},{3,7},{4,0},{5,1},{6,2},{7,3},{8,12},{9,13},{10,... | collective-permute-start | bytes 1572872 | tf_op jit(solution)/shard_map/ppermute | solution.py:30
  616.9 28.1 %collective-permute-start.39 = (bf16[4,32,1024]{2,1,0:T(8,128)(2,1)S(1)}, bf16[4,32,1024]{2,1,0:T(8,128)(2,1)S(1)}, u32[]{:S(2)}, u32[]{:S(2)}) collective-permute-start(bf16[4,32,1024]{2,1,0:T(8,128)(2,1)S(1)} %get-tuple-element.363), channel_id=1, source_target_pairs={{0,1},{1,0},{2,3},{3,2},{4,5},{5,4},{6,7},{7,6},{8,9},{9,8},{10,11... | collective-permute-start | bytes 786440 | tf_op jit(solution)/shard_map/ppermute | solution.py:30
  618.4 26.6 %collective-permute-start.41 = (bf16[1,96,1024]{2,1,0:T(8,128)(2,1)S(1)}, bf16[1,96,1024]{2,1,0:T(8,128)(2,1)S(1)}, u32[]{:S(2)}, u32[]{:S(2)}) collective-permute-start(bf16[1,96,1024]{2,1,0:T(8,128)(2,1)S(1)} %fusion.165), channel_id=1, source_target_pairs={{0,16},{1,17},{2,18},{3,19},{4,20},{5,21},{6,22},{7,23},{8,24},{9,... | collective-permute-start | bytes 589832 | tf_op jit(solution)/shard_map/ppermute | solution.py:30
  (167 other events, 1400.7 us)
Sparse Core Ops, SparseCore 0:
  15.8 176.8 all-gather.4
  195.6 128.5 all-gather.6
  379.8 164.6 all-gather.8

commit v3 on v2

--- a/solution.py
+++ b/solution.py
@@ -616,11 +616,11 @@
         blocks = packed.reshape(rows, 3, size, own).transpose(2, 0, 1, 3).reshape(size, rows, 3 * own)
         return jnp.pad(blocks, ((0, 0), (0, -rows % 8), (0, 3 * (own_v - own))))
 
-    def exchange(*blocks):
-        return lax.all_to_all(
-            jnp.concatenate(blocks, axis=1), ALL, split_axis=0, concat_axis=0, tiled=True
-        )
-
+    if by_permute:
+        tall = -(-x_t.shape[0] // 8) * 8
+        seen = [jnp.pad(m, ((0, tall - m.shape[0]), (0, 0))) for m in (x_t, t_low)]
+        seen = jnp.concatenate([x_v.reshape(-1, d_t)] + seen, axis=0)
+        seen = lax.all_gather(seen, ALL, axis=0)
     c1a = Chunk(t_pairs[:1], d_t, halving(2, 0))
     c1b = Chunk(t_pairs[1:], d_t, halving(0, 2))
     t_ga, t_res, i_attn = close_round([], t_ga, t_res, i_attn)
@@ -649,11 +649,6 @@
     start(c3a, c3b, c1a, c1b)
     i_cross, i_kept = tail_forward(x_v.astype(FLOAT), i_attn, w_cio, w_ciu, w_cid, image_gains[0:2])
     i_low = i_cross.astype(BFLOAT)
-    if by_permute:
-        tall = -(-x_t.shape[0] // 8) * 8
-        seen = [x_v.reshape(-1, d_t), i_low.reshape(-1, d_t)]
-        seen += [jnp.pad(m, ((0, tall - m.shape[0]), (0, 0))) for m in (x_t, t_low)]
-        seen = jnp.concatenate(seen, axis=0)
     si_packed = project(i_low, w_sip)
     si_attn = self_attend(si_packed, H_V, my_len, False)
     i_final, si_kept = tail_forward(i_cross, si_attn, w_sio, w_siu, w_sid, image_gains[2:4])
@@ -665,15 +660,15 @@
         [c1a, c1b, c3a, c3b], c1i.send, c1i.keep, i_ga, i_res
     )
     if by_permute:
-        seen = lax.all_gather(seen, ALL, axis=0)
+        seen_low_v = lax.all_gather(i_low.reshape(-1, d_t), ALL, axis=0)
 
     start(c1i, c3a, c3b)
     si_grads = self_attend_back(si_packed, H_V, my_len, False, i_ga)
     i_back = i_res + mm_t(si_grads, w_sip)
-    si_grads, i_back = close_round([c1i, c3a, c3b], si_grads, i_back)
-    self_slices = t_low
-    if by_permute:
-        self_slices = exchange(by_owner(st_grads, own_t), by_owner(si_grads, own_v))
+    self_blocks = (st_grads, si_grads)
+    if by_permute:
+        self_blocks = (by_owner(st_grads, own_t), by_owner(si_grads, own_v))
+    self_blocks, i_back = close_round([c1i, c3a, c3b], self_blocks, i_back)
 
     start(c1i, c3a, c3b)
     i_res, i_ga, i_pairs, i_gain_c = tail_backward(
@@ -681,8 +676,8 @@
     )
     c3x = Chunk(i_pairs[:1], d_v, halving(2, 0))
     c3y = Chunk(i_pairs[1:], d_v, halving(0, 2))
-    c3x.send, c3x.keep, c3y.send, c3y.keep, i_res, i_ga, t_ga, self_slices = close_round(
-        [c1i, c3a, c3b], c3x.send, c3x.keep, c3y.send, c3y.keep, i_res, i_ga, t_ga, self_slices
+    c3x.send, c3x.keep, c3y.send, c3y.keep, i_res, i_ga, t_ga = close_round(
+        [c1i, c3a, c3b], c3x.send, c3x.keep, c3y.send, c3y.keep, i_res, i_ga, t_ga
     )
 
     start(c3x, c3y, c1i)
@@ -692,51 +687,66 @@
     t_gain = jnp.stack(t_gain_c + t_gain_s)
     i_gain = jnp.stack(i_gain_c + i_gain_s)
     start(c3x, c3y, c1i)
+    blocks = t_grads
     if by_permute:
         gain_rows = [t_gain.reshape(4, size, own_t), i_gain.reshape(4, size, own_v)]
         gain_rows = [
             jnp.pad(g.astype(BFLOAT), ((0, 0), (0, 0), (0, 3 * own_v - g.shape[2]))) for g in gain_rows
         ]
         gain_rows = jnp.concatenate(gain_rows, axis=0).transpose(1, 0, 2)
-        cross_slices = exchange(by_owner(t_grads, own_c), by_owner(i_grads, own_c), gain_rows)
-    close_round([c3x, c3y, c1i])
-    start(c3x, c3y, c1i)
+        blocks = [by_owner(t_grads, own_c), by_owner(i_grads, own_c), gain_rows, *self_blocks]
+        blocks = jnp.concatenate(blocks, axis=1)
+    (blocks,) = close_round([c3x, c3y, c1i], blocks)
+    start(c3x, c3y, c3a, c3b)
     text_input_grad = t_res + mm_t(t_grads, w_ctp)
     image_input_grad = i_res + mm_t(i_grads, w_cip)
-    text_input_grad, image_input_grad = close_round([c3x, c3y, c1i], text_input_grad, image_input_grad)
-    start(c3x, c3y, c3a, c3b)
-    close_round([c3x, c3y, c3a, c3b])
-    start(c3x, c3y, c1a, c1b)
-    close_round([c3x, c3y, c1a, c1b])
+    slices, rows_all = t_low, t_low
+    if by_permute:
+        slices = lax.all_to_all(blocks, ALL, split_axis=0, concat_axis=0, tiled=True)
+        short = x_v.size // d_t
+        rows_all = (
+            seen_low_v.reshape(-1, d_v),
+            seen[:, :short].reshape(-1, d_v),
+            seen[:, short : short + tall].reshape(-1, d_t),
+            seen[:, short + tall :].reshape(-1, d_t),
+        )
+    text_input_grad, image_input_grad, rows_all = close_round(
+        [c3x, c3y, c3a, c3b], text_input_grad, image_input_grad, rows_all
+    )
+    start(c3x, c3y, c1a, c1b, c1i)
+
+    def slices_grad(rows, part, own):
+        grad = t_mm(rows, part.reshape(-1, part.shape[2]))[:, : 3 * own]
+        return grad.reshape(grad.shape[0], 3, own).transpose(1, 0, 2)
+
+    self_grads, cross_grads = t_low, t_low
+    if by_permute:
+        all_low_v, all_v, all_t, all_low_t = rows_all
+        wide_v = x_v.shape[0]
+        tall_v = -(-wide_v // 8) * 8
+        selves = tall + tall_v + 8
+        gain_sum = jnp.sum(slices[:, tall + tall_v : selves].astype(FLOAT), axis=0)
+        self_grads = (
+            slices_grad(all_low_t, slices[:, selves : selves + tall], own_t),
+            slices_grad(all_low_v, slices[:, selves + tall : selves + tall + wide_v], own_v),
+            gain_sum,
+        )
+    (self_grads,) = close_round([c3x, c3y, c1a, c1b, c1i], self_grads)
+    start(c3x, c3y)
+    if by_permute:
+        cross_grads = (
+            slices_grad(all_t, slices[:, :tall], own_c),
+            slices_grad(all_v, slices[:, tall : tall + wide_v], own_c),
+        )
+    (cross_grads,) = close_round([c3x, c3y], cross_grads)
     for m in (c1a, c1b, c3a, c3b, c1i, c3x, c3y):
         while m.step < bits:
             m.start()
             m.absorb()
 
-    def slices_grad(rows, slices, own):
-        grad = t_mm(rows, slices)[:, : 3 * own]
-        return grad.reshape(grad.shape[0], 3, own).transpose(1, 0, 2)
-
-    if by_permute:
-        short = x_v.size // d_t
-        wide_v = x_v.shape[0]
-        tall_v = -(-wide_v // 8) * 8
-
-        def rows_of(at, rows):
-            return seen[:, at : at + rows]
-
-        def flat_slices(slices, at, rows):
-            return slices[:, at : at + rows].reshape(-1, slices.shape[2])
-
-        all_v = rows_of(0, short).reshape(-1, d_v)
-        all_low_v = rows_of(short, short).reshape(-1, d_v)
-        all_t = rows_of(2 * short, tall).reshape(-1, d_t)
-        all_low_t = rows_of(2 * short + tall, tall).reshape(-1, d_t)
-        o_stp = slices_grad(all_low_t, flat_slices(self_slices, 0, tall), own_t)
-        o_sip = slices_grad(all_low_v, flat_slices(self_slices, tall, wide_v), own_v)
-        o_ctp = slices_grad(all_t, flat_slices(cross_slices, 0, tall), own_c)
-        o_cip = slices_grad(all_v, flat_slices(cross_slices, tall, wide_v), own_c)
-        gain_sum = jnp.sum(cross_slices[:, tall + tall_v :].astype(FLOAT), axis=0)
+    if by_permute:
+        o_stp, o_sip, gain_sum = self_grads
+        o_ctp, o_cip = cross_grads
         o_tg, o_ig = gain_sum[:4, :own_t], gain_sum[4:, :own_v]
     else:
 
@@ -746,7 +756,7 @@
             block = whole.finish()
             return block.reshape(3, block.shape[0] // 3, block.shape[1]).transpose(0, 2, 1)
 
-        o_stp, o_sip = by_scatter(st_grads, t_low), by_scatter(si_grads, i_low)
+        o_stp, o_sip = by_scatter(self_blocks[0], t_low), by_scatter(self_blocks[1], i_low)
         o_ctp, o_cip = by_scatter(t_grads, x_t), by_scatter(i_grads, x_v)
         at = my_index()
         t_gain, i_gain = lax.psum(t_gain, ALL), lax.psum(i_gain, ALL)

time: 726 us -> 750 us (1.033)
  local copies, waits for them, and re-layouts: 89.7 us -> 110 us
  waiting for transfers between devices: 289 us -> 301 us
    all_to_all x2 -> x1, waiting for transfers between devices: 0.01 us -> 42.1 us  [on_device(): lax.all_to_all(blocks, ALL, split_axis=0, concat_axis=0, tiled=True)]
    ppermute x50, waiting for transfers between devices: 289 us -> 259 us  [swap(): return lax.ppermute(block, ALL, [(i, i ^ 1 << bit) for i in range(size)])]
    slice x6 -> x8, local copies, waits for them, and re-layouts: 11 us -> 16.3 us  [the longest x1 8.61 us: on_device(): seen[:, short + tall:].reshape(-1, d_t)]
    all_to_all x2 -> x1, starting transfers between devices: 23.4 us -> 24.3 us  [on_device(): lax.all_to_all(blocks, ALL, split_axis=0, concat_axis=0, tiled=True)]
    unnamed x306 -> x296, local copies, waits for them, and re-layouts: 37.4 us -> 37.7 us
  transfers between devices with their start and end apart: 55 -> 55, of which waited for: 23 -> 26; matrix products, arithmetic and copies ran while one was open for 27% -> 31% of each run, Pallas kernels for 9% -> 8%
where the time goes in v3:
time: 750 us; the launch traced here: 739 us
  waiting for transfers between devices  301 us (40%)
  local copies, waits for them, and re-layouts  110 us (15%)
  matrix products  93.4 us (12%)
  starting transfers between devices  82.1 us (11%)
  other arithmetic  73.5 us (10%)
  Pallas kernels  62.3 us (8%)
  between operations  16.1 us (2%)
    ppermute x50, waiting for transfers between devices, swap(): return lax.ppermute(block, ALL, [(i, i ^ 1 << bit) for i in range(size)])  259 us
    ppermute x50, starting transfers between devices, swap(): return lax.ppermute(block, ALL, [(i, i ^ 1 << bit) for i in range(size)])  57.6 us
    dot_general x16, matrix products, mm_t(): lax.dot_general(left, right, (((1,), (1,)), ((), ())), preferred_element_...  50.5 us
    convert_element_type x28, other arithmetic, add_low(): return (left.astype(FLOAT) + right.astype(FLOAT)).astype(BFLOAT)  47.5 us
    all_to_all x1, waiting for transfers between devices, on_device(): lax.all_to_all(blocks, ALL, split_axis=0, concat_axis=0, tiled=True)  42.1 us
    unnamed x296, local copies, waits for them, and re-layouts  37.7 us
    dot_general x16, matrix products, mm(): return jnp.dot(left, right, preferred_element_type=FLOAT)  37.1 us
    pallas_call x7, Pallas kernels, pack_kernel(): pl.pallas_call(body, grid_spec=pltpu.PrefetchScalarGridSpec(num_scalar_pr...  33.7 us
  transfers between devices with their start and end apart: 55, of which 26 were waited for; matrix products, arithmetic and copies ran while one was open for 31% of the time, Pallas kernels for 8%

profile of v3, /device:TPU:0, one launch (start us, length us, event | category | flops | bytes accessed | tf_op | source)
XLA Modules:
  0.0 739.3 jit_solution(8116628330108096162)
XLA Ops:
  23.5 22.7 %collective-permute-done = bf16[1,32,3072]{2,1,0:T(8,128)(2,1)S(1)} collective-permute-done((bf16[1,32,3072]{2,1,0:T(8,128)(2,1)S(1)}, bf16[1,32,3072]{2,1,0:T(8,128)(2,1)S(1)}, u32[]{:S(2)}, u32[]{:S(2)}) %collective-permute-start) | collective-permute-done | bytes 196640 | tf_op jit(solution)/shard_map/ppermute | solution.py:30
  46.2 7.4 collective-permute-done.1
  55.8 21.3 %collective-permute-done.2 = bf16[2,32,3072]{2,1,0:T(8,128)(2,1)S(1)} collective-permute-done((bf16[2,32,3072]{2,1,0:T(8,128)(2,1)S(1)}, bf16[2,32,3072]{2,1,0:T(8,128)(2,1)S(1)}, u32[]{:S(2)}, u32[]{:S(2)}) %collective-permute-start.2) | collective-permute-done | bytes 393248 | tf_op jit(solution)/shard_map/ppermute | solution.py:30
  77.1 20.8 %collective-permute-done.3 = bf16[2,128,768]{2,1,0:T(8,128)(2,1)S(1)} collective-permute-done((bf16[2,128,768]{2,1,0:T(8,128)(2,1)S(1)}, bf16[2,128,768]{2,1,0:T(8,128)(2,1)S(1)}, u32[]{:S(2)}, u32[]{:S(2)}) %collective-permute-start.3) | collective-permute-done | bytes 393248 | tf_op jit(solution)/shard_map/ppermute | solution.py:30
  103.3 12.8 %collective-permute-done.6 = bf16[1,96,768]{2,1,0:T(8,128)(2,1)S(1)} collective-permute-done((bf16[1,96,768]{2,1,0:T(8,128)(2,1)S(1)}, bf16[1,96,768]{2,1,0:T(8,128)(2,1)S(1)}, u32[]{:S(2)}, u32[]{:S(2)}) %collective-permute-start.6) | collective-permute-done | bytes 147488 | tf_op jit(solution)/shard_map/ppermute | solution.py:30
  116.2 6.1 collective-permute-done.4
  129.8 10.5 %collective-permute-done.9 = bf16[2,96,768]{2,1,0:T(8,128)(2,1)S(1)} collective-permute-done((bf16[2,96,768]{2,1,0:T(8,128)(2,1)S(1)}, bf16[2,96,768]{2,1,0:T(8,128)(2,1)S(1)}, u32[]{:S(2)}, u32[]{:S(2)}) %collective-permute-start.9) | collective-permute-done | bytes 294944 | tf_op jit(solution)/shard_map/ppermute | solution.py:30
  140.3 38.3 %collective-permute-done.7 = bf16[8,32,3072]{2,1,0:T(8,128)(2,1)S(1)} collective-permute-done((bf16[8,32,3072]{2,1,0:T(8,128)(2,1)S(1)}, bf16[8,32,3072]{2,1,0:T(8,128)(2,1)S(1)}, u32[]{:S(2)}, u32[]{:S(2)}) %collective-permute-start.7) | collective-permute-done | bytes 1572896 | tf_op jit(solution)/shard_map/ppermute | solution.py:30
  183.1 13.8 %collective-permute-done.12 = bf16[4,96,768]{2,1,0:T(8,128)(2,1)S(1)} collective-permute-done((bf16[4,96,768]{2,1,0:T(8,128)(2,1)S(1)}, bf16[4,96,768]{2,1,0:T(8,128)(2,1)S(1)}, u32[]{:S(2)}, u32[]{:S(2)}) %collective-permute-start.12) | collective-permute-done | bytes 589856 | tf_op jit(solution)/shard_map/ppermute | solution.py:30
  221.5 11.4 %collective-permute-done.13 = bf16[8,96,768]{2,1,0:T(8,128)(2,1)} collective-permute-done((bf16[8,96,768]{2,1,0:T(8,128)(2,1)}, bf16[8,96,768]{2,1,0:T(8,128)(2,1)}, u32[]{:S(2)}, u32[]{:S(2)}) %collective-permute-start.13) | collective-permute-done | bytes 1179680 | tf_op jit(solution)/shard_map/ppermute | solution.py:30
  268.2 5.4 shard_map.396
  278.0 5.4 shard_map.395
  290.1 5.9 shard_map.397
  315.0 5.1 shard_map.399
  322.4 5.7 shard_map.398
  329.5 5.0 collective-permute-done.17
  334.4 5.3 collective-permute-done.18
  346.6 13.4 %collective-permute-done.19 = bf16[4,96,768]{2,1,0:T(8,128)(2,1)} collective-permute-done((bf16[4,96,768]{2,1,0:T(8,128)(2,1)}, bf16[4,96,768]{2,1,0:T(8,128)(2,1)}, u32[]{:S(2)}, u32[]{:S(2)}) %collective-permute-start.19) | collective-permute-done | bytes 589856 | tf_op jit(solution)/shard_map/ppermute | solution.py:30
  409.7 5.5 shard_map.401
  418.9 7.6 %collective-permute-done.25 = bf16[8,128,768]{2,1,0:T(8,128)(2,1)S(1)} collective-permute-done((bf16[8,128,768]{2,1,0:T(8,128)(2,1)S(1)}, bf16[8,128,768]{2,1,0:T(8,128)(2,1)S(1)}, u32[]{:S(2)}, u32[]{:S(2)}) %collective-permute-start.25) | collective-permute-done | bytes 1572896 | tf_op jit(solution)/shard_map/ppermute | solution.py:30
  450.4 4.9 fusion.130
  481.7 7.5 %collective-permute-done.32 = bf16[2,96,768]{2,1,0:T(8,128)(2,1)S(1)} collective-permute-done((bf16[2,96,768]{2,1,0:T(8,128)(2,1)S(1)}, bf16[2,96,768]{2,1,0:T(8,128)(2,1)S(1)}, u32[]{:S(2)}, u32[]{:S(2)}) %collective-permute-start.32) | collective-permute-done | bytes 294944 | tf_op jit(solution)/shard_map/ppermute | solution.py:30
  489.2 17.6 %collective-permute-done.30 = bf16[8,96,1024]{2,1,0:T(8,128)(2,1)S(1)} collective-permute-done((bf16[8,96,1024]{2,1,0:T(8,128)(2,1)S(1)}, bf16[8,96,1024]{2,1,0:T(8,128)(2,1)S(1)}, u32[]{:S(2)}, u32[]{:S(2)}) %collective-permute-start.30) | collective-permute-done | bytes 1572896 | tf_op jit(solution)/shard_map/ppermute | solution.py:30
  511.8 8.0 %shard_map.405 = (bf16[100,3072]{1,0:T(8,128)(2,1)S(1)}, bf16[36,3072]{1,0:T(8,128)(2,1)S(1)}) custom-call(s32[1]{0:T(128)} %dynamic_slice.308.len_ref, bf16[100,3072]{1,0:T(8,128)(2,1)S(1)} %copy-done.14, bf16[36,3072]{1,0:T(8,128)(2,1)S(1)} %fusion.27.image_ref, bf16[100,1024]{1,0:T(8,128)(2,1)S(1)} %copy-done.31, bf16[36,1024]{1,0:T(8,128)(2,1)S(1)} %fusion.133.ig_ref), custom_call_target="tpu_custom_call" | custom-call | tf_op jit(solution)/shard_map/pallas_call | solution.py:404
  519.8 16.8 %collective-permute-done.35 = bf16[4,96,1024]{2,1,0:T(8,128)(2,1)S(1)} collective-permute-done((bf16[4,96,1024]{2,1,0:T(8,128)(2,1)S(1)}, bf16[4,96,1024]{2,1,0:T(8,128)(2,1)S(1)}, u32[]{:S(2)}, u32[]{:S(2)}) %collective-permute-start.35) | collective-permute-done | bytes 786464 | tf_op jit(solution)/shard_map/ppermute | solution.py:30
  555.6 5.9 concatenate.78
  563.4 5.7 collective-permute-done.37
  575.5 24.3 %all-to-all-start = ((bf16[32,296,96]{1,2,0:T(8,128)(2,1)}), bf16[32,296,96]{1,2,0:T(8,128)(2,1)S(1)}, u32[]{:S(2)}, u32[]{:S(2)}) async-start(bf16[32,296,96]{1,2,0:T(8,128)(2,1)} %concatenate.78), calls=%async_computation | async-start | bytes 4718592 | tf_op jit(solution)/shard_map/all_to_all | solution.py:705
  602.7 5.1 reshape.962
  615.5 5.4 convolution_add_fusion.4
  623.9 42.1 %all-to-all-done = bf16[32,296,96]{1,2,0:T(8,128)(2,1)S(1)} async-done(((bf16[32,296,96]{1,2,0:T(8,128)(2,1)}), bf16[32,296,96]{1,2,0:T(8,128)(2,1)S(1)}, u32[]{:S(2)}, u32[]{:S(2)}) %all-to-all-start) | async-done | bytes 1818656 | tf_op jit(solution)/shard_map/all_to_all | solution.py:705
  682.1 8.6 %fusion.228 = (bf16[32,104,768]{2,1,0:T(8,128)(2,1)}, bf16[32,104,768]{2,1,0:T(8,128)(2,1)}) fusion(bf16[32,256,768]{2,1,0:T(8,128)(2,1)} %bitcast.392), kind=kLoop, calls=%fused_computation.417 | loop fusion | bytes 20447232 | tf_op jit(solution)/shard_map/slice | solution.py:711
  (612 shorter events, 342.0 us)
Async XLA Ops:
  7.2 207.4 %all-gather.6.cloned.1.call-start = ((), (), s32[]{:S(2)}) async-start(), calls=%async_computation.1 | async-start | bytes 19464192 | tf_op jit(solution)/shard_map/all_gather | solution.py:543
  15.6 359.1 %all-gather.8.cloned.1.call-start = ((), (), s32[]{:S(2)}) async-start(), calls=%async_computation.2 | async-start | bytes 19464192 | tf_op jit(solution)/shard_map/all_gather | solution.py:543
  19.2 583.5 %all-gather.10.cloned.1.call-start = ((), (), s32[]{:S(2)}) async-start(), calls=%async_computation.3 | async-start | bytes 2433024 | tf_op jit(solution)/shard_map/all_gather | solution.py:663
  19.3 26.9 %collective-permute-start = (bf16[1,32,3072]{2,1,0:T(8,128)(2,1)S(1)}, bf16[1,32,3072]{2,1,0:T(8,128)(2,1)S(1)}, u32[]{:S(2)}, u32[]{:S(2)}) collective-permute-start(bf16[1,32,3072]{2,1,0:T(8,128)(2,1)S(1)} %maximum_bitcast_fusion), channel_id=1, source_target_pairs={{0,16},{1,17},{2,18},{3,19},{4,20},{5,21},{6,22},{7,23},{8,24},{9,... | collective-permute-start | bytes 589832 | tf_op jit(solution)/shard_map/ppermute | solution.py:30
  23.4 30.2 %collective-permute-start.1 = (bf16[1,128,768]{2,1,0:T(8,128)(2,1)S(1)}, bf16[1,128,768]{2,1,0:T(8,128)(2,1)S(1)}, u32[]{:S(2)}, u32[]{:S(2)}) collective-permute-start(bf16[1,128,768]{2,1,0:T(8,128)(2,1)S(1)} %maximum_bitcast_fusion.1), channel_id=1, source_target_pairs={{0,16},{1,17},{2,18},{3,19},{4,20},{5,21},{6,22},{7,23},{8,24},{9,... | collective-permute-start | bytes 589832 | tf_op jit(solution)/shard_map/ppermute | solution.py:30
  54.5 43.3 %collective-permute-start.3 = (bf16[2,128,768]{2,1,0:T(8,128)(2,1)S(1)}, bf16[2,128,768]{2,1,0:T(8,128)(2,1)S(1)}, u32[]{:S(2)}, u32[]{:S(2)}) collective-permute-start(bf16[2,128,768]{2,1,0:T(8,128)(2,1)S(1)} %pad_maximum_fusion.10), channel_id=1, source_target_pairs={{0,8},{1,9},{2,10},{3,11},{4,12},{5,13},{6,14},{7,15},{8,0},{9,1},... | collective-permute-start | bytes 1179656 | tf_op jit(solution)/shard_map/ppermute | solution.py:30
  99.2 27.7 %collective-permute-start.5 = (bf16[4,128,768]{2,1,0:T(8,128)(2,1)S(1)}, bf16[4,128,768]{2,1,0:T(8,128)(2,1)S(1)}, u32[]{:S(2)}, u32[]{:S(2)}) collective-permute-start(bf16[4,128,768]{2,1,0:T(8,128)(2,1)S(1)} %pad_maximum_fusion.7), channel_id=1, source_target_pairs={{0,4},{1,5},{2,6},{3,7},{4,0},{5,1},{6,2},{7,3},{8,12},{9,13},{10,... | collective-permute-start | bytes 2359304 | tf_op jit(solution)/shard_map/ppermute | solution.py:30
  127.2 51.4 %collective-permute-start.7 = (bf16[8,32,3072]{2,1,0:T(8,128)(2,1)S(1)}, bf16[8,32,3072]{2,1,0:T(8,128)(2,1)S(1)}, u32[]{:S(2)}, u32[]{:S(2)}) collective-permute-start(bf16[8,32,3072]{2,1,0:T(8,128)(2,1)S(1)} %pad_maximum_fusion.3), channel_id=1, source_target_pairs={{0,4},{1,5},{2,6},{3,7},{4,0},{5,1},{6,2},{7,3},{8,12},{9,13},{10,... | collective-permute-start | bytes 4718600 | tf_op jit(solution)/shard_map/ppermute | solution.py:30
  129.8 48.8 %collective-permute-start.8 = (bf16[8,128,768]{2,1,0:T(8,128)(2,1)S(1)}, bf16[8,128,768]{2,1,0:T(8,128)(2,1)S(1)}, u32[]{:S(2)}, u32[]{:S(2)}) collective-permute-start(bf16[8,128,768]{2,1,0:T(8,128)(2,1)S(1)} %pad_maximum_fusion.4), channel_id=1, source_target_pairs={{0,1},{1,0},{2,3},{3,2},{4,5},{5,4},{6,7},{7,6},{8,9},{9,8},{10,11... | collective-permute-start | bytes 4718600 | tf_op jit(solution)/shard_map/ppermute | solution.py:30
  201.3 31.6 %collective-permute-start.13 = (bf16[8,96,768]{2,1,0:T(8,128)(2,1)}, bf16[8,96,768]{2,1,0:T(8,128)(2,1)}, u32[]{:S(2)}, u32[]{:S(2)}) collective-permute-start(bf16[8,96,768]{2,1,0:T(8,128)(2,1)} %pad_maximum_fusion.5), channel_id=1, source_target_pairs={{0,1},{1,0},{2,3},{3,2},{4,5},{5,4},{6,7},{7,6},{8,9},{9,8},{10,11... | collective-permute-start | bytes 3538952 | tf_op jit(solution)/shard_map/ppermute | solution.py:30
  273.6 26.2 %collective-permute-start.16 = (bf16[16,120,768]{2,1,0:T(8,128)(2,1)}, bf16[16,120,768]{2,1,0:T(8,128)(2,1)}, u32[]{:S(2)}, u32[]{:S(2)}) collective-permute-start(bf16[16,120,768]{2,1,0:T(8,128)(2,1)} %bitcast.33), channel_id=1, source_target_pairs={{0,2},{1,3},{2,0},{3,1},{4,6},{5,7},{6,4},{7,5},{8,10},{9,11},{10,... | collective-permute-start | bytes 8847368 | tf_op jit(solution)/shard_map/ppermute | solution.py:30
  305.1 34.7 %collective-permute-start.18 = (bf16[8,120,768]{2,1,0:T(8,128)(2,1)S(1)}, bf16[8,120,768]{2,1,0:T(8,128)(2,1)S(1)}, u32[]{:S(2)}, u32[]{:S(2)}) collective-permute-start(bf16[8,120,768]{2,1,0:T(8,128)(2,1)S(1)} %get-tuple-element.282), channel_id=1, source_target_pairs={{0,1},{1,0},{2,3},{3,2},{4,5},{5,4},{6,7},{7,6},{8,9},{9,8},{10,11... | collective-permute-start | bytes 4423688 | tf_op jit(solution)/shard_map/ppermute | solution.py:30
  306.5 27.9 %collective-permute-start.17 = (bf16[8,96,768]{2,1,0:T(8,128)(2,1)S(1)}, bf16[8,96,768]{2,1,0:T(8,128)(2,1)S(1)}, u32[]{:S(2)}, u32[]{:S(2)}) collective-permute-start(bf16[8,96,768]{2,1,0:T(8,128)(2,1)S(1)} %get-tuple-element.281), channel_id=1, source_target_pairs={{0,4},{1,5},{2,6},{3,7},{4,0},{5,1},{6,2},{7,3},{8,12},{9,13},{10,... | collective-permute-start | bytes 3538952 | tf_op jit(solution)/shard_map/ppermute | solution.py:30
  383.3 298.7 %all-gather.12.cloned.1.call-start = ((), (), s32[]{:S(2)}) async-start(), calls=%async_computation.4 | async-start | bytes 12976128 | tf_op jit(solution)/shard_map/all_gather | solution.py:623
  390.0 36.5 %collective-permute-start.25 = (bf16[8,128,768]{2,1,0:T(8,128)(2,1)S(1)}, bf16[8,128,768]{2,1,0:T(8,128)(2,1)S(1)}, u32[]{:S(2)}, u32[]{:S(2)}) collective-permute-start(bf16[8,128,768]{2,1,0:T(8,128)(2,1)S(1)} %copy-done.54), channel_id=1, source_target_pairs={{0,4},{1,5},{2,6},{3,7},{4,0},{5,1},{6,2},{7,3},{8,12},{9,13},{10,... | collective-permute-start | bytes 4718600 | tf_op jit(solution)/shard_map/ppermute | solution.py:30
  391.7 27.3 %collective-permute-start.26 = (bf16[8,96,768]{2,1,0:T(8,128)(2,1)S(1)}, bf16[8,96,768]{2,1,0:T(8,128)(2,1)S(1)}, u32[]{:S(2)}, u32[]{:S(2)}) collective-permute-start(bf16[8,96,768]{2,1,0:T(8,128)(2,1)S(1)} %copy-done.65), channel_id=1, source_target_pairs={{0,1},{1,0},{2,3},{3,2},{4,5},{5,4},{6,7},{7,6},{8,9},{9,8},{10,11... | collective-permute-start | bytes 3538952 | tf_op jit(solution)/shard_map/ppermute | solution.py:30
  392.9 25.2 %collective-permute-start.24 = (bf16[2,120,768]{2,1,0:T(8,128)(2,1)S(1)}, bf16[2,120,768]{2,1,0:T(8,128)(2,1)S(1)}, u32[]{:S(2)}, u32[]{:S(2)}) collective-permute-start(bf16[2,120,768]{2,1,0:T(8,128)(2,1)S(1)} %copy-done.81), channel_id=1, source_target_pairs={{0,8},{1,9},{2,10},{3,11},{4,12},{5,13},{6,14},{7,15},{8,0},{9,1},... | collective-permute-start | bytes 1105928 | tf_op jit(solution)/shard_map/ppermute | solution.py:30
  392.9 25.2 %collective-permute-start.23 = (bf16[2,96,768]{2,1,0:T(8,128)(2,1)S(1)}, bf16[2,96,768]{2,1,0:T(8,128)(2,1)S(1)}, u32[]{:S(2)}, u32[]{:S(2)}) collective-permute-start(bf16[2,96,768]{2,1,0:T(8,128)(2,1)S(1)} %copy-done.91), channel_id=1, source_target_pairs={{0,8},{1,9},{2,10},{3,11},{4,12},{5,13},{6,14},{7,15},{8,0},{9,1},... | collective-permute-start | bytes 884744 | tf_op jit(solution)/shard_map/ppermute | solution.py:30
  430.9 24.5 %collective-permute-start.27 = (bf16[16,96,1024]{2,1,0:T(8,128)(2,1)}, bf16[16,96,1024]{2,1,0:T(8,128)(2,1)}, u32[]{:S(2)}, u32[]{:S(2)}) collective-permute-start(bf16[16,96,1024]{2,1,0:T(8,128)(2,1)} %bitcast.71), channel_id=1, source_target_pairs={{0,2},{1,3},{2,0},{3,1},{4,6},{5,7},{6,4},{7,5},{8,10},{9,11},{10,... | collective-permute-start | bytes 9437192 | tf_op jit(solution)/shard_map/ppermute | solution.py:30
  462.2 44.6 %collective-permute-start.30 = (bf16[8,96,1024]{2,1,0:T(8,128)(2,1)S(1)}, bf16[8,96,1024]{2,1,0:T(8,128)(2,1)S(1)}, u32[]{:S(2)}, u32[]{:S(2)}) collective-permute-start(bf16[8,96,1024]{2,1,0:T(8,128)(2,1)S(1)} %get-tuple-element.343), channel_id=1, source_target_pairs={{0,1},{1,0},{2,3},{3,2},{4,5},{5,4},{6,7},{7,6},{8,9},{9,8},{10,11... | collective-permute-start | bytes 4718600 | tf_op jit(solution)/shard_map/ppermute | solution.py:30
  463.8 25.4 %collective-permute-start.31 = (bf16[2,128,768]{2,1,0:T(8,128)(2,1)S(1)}, bf16[2,128,768]{2,1,0:T(8,128)(2,1)S(1)}, u32[]{:S(2)}, u32[]{:S(2)}) collective-permute-start(bf16[2,128,768]{2,1,0:T(8,128)(2,1)S(1)} %get-tuple-element.344), channel_id=1, source_target_pairs={{0,8},{1,9},{2,10},{3,11},{4,12},{5,13},{6,14},{7,15},{8,0},{9,1},... | collective-permute-start | bytes 1179656 | tf_op jit(solution)/shard_map/ppermute | solution.py:30
  463.8 25.4 %collective-permute-start.32 = (bf16[2,96,768]{2,1,0:T(8,128)(2,1)S(1)}, bf16[2,96,768]{2,1,0:T(8,128)(2,1)S(1)}, u32[]{:S(2)}, u32[]{:S(2)}) collective-permute-start(bf16[2,96,768]{2,1,0:T(8,128)(2,1)S(1)} %get-tuple-element.345), channel_id=1, source_target_pairs={{0,8},{1,9},{2,10},{3,11},{4,12},{5,13},{6,14},{7,15},{8,0},{9,1},... | collective-permute-start | bytes 884744 | tf_op jit(solution)/shard_map/ppermute | solution.py:30
  508.9 27.6 %collective-permute-start.34 = (bf16[16,64,1024]{2,1,0:T(8,128)(2,1)S(1)}, bf16[16,64,1024]{2,1,0:T(8,128)(2,1)S(1)}, u32[]{:S(2)}, u32[]{:S(2)}) collective-permute-start(bf16[16,64,1024]{2,1,0:T(8,128)(2,1)S(1)} %bitcast.387), channel_id=1, source_target_pairs={{0,2},{1,3},{2,0},{3,1},{4,6},{5,7},{6,4},{7,5},{8,10},{9,11},{10,... | collective-permute-start | bytes 6291464 | tf_op jit(solution)/shard_map/ppermute | solution.py:30
  509.0 27.5 %collective-permute-start.33 = (bf16[16,32,1024]{2,1,0:T(8,128)(2,1)S(1)}, bf16[16,32,1024]{2,1,0:T(8,128)(2,1)S(1)}, u32[]{:S(2)}, u32[]{:S(2)}) collective-permute-start(bf16[16,32,1024]{2,1,0:T(8,128)(2,1)S(1)} %bitcast.388), channel_id=1, source_target_pairs={{0,2},{1,3},{2,0},{3,1},{4,6},{5,7},{6,4},{7,5},{8,10},{9,11},{10,... | collective-permute-start | bytes 3145736 | tf_op jit(solution)/shard_map/ppermute | solution.py:30
  509.5 27.0 %collective-permute-start.35 = (bf16[4,96,1024]{2,1,0:T(8,128)(2,1)S(1)}, bf16[4,96,1024]{2,1,0:T(8,128)(2,1)S(1)}, u32[]{:S(2)}, u32[]{:S(2)}) collective-permute-start(bf16[4,96,1024]{2,1,0:T(8,128)(2,1)S(1)} %get-tuple-element.364), channel_id=1, source_target_pairs={{0,4},{1,5},{2,6},{3,7},{4,0},{5,1},{6,2},{7,3},{8,12},{9,13},{10,... | collective-permute-start | bytes 2359304 | tf_op jit(solution)/shard_map/ppermute | solution.py:30
  541.2 28.0 %collective-permute-start.37 = (bf16[8,64,1024]{2,1,0:T(8,128)(2,1)}, bf16[8,64,1024]{2,1,0:T(8,128)(2,1)}, u32[]{:S(2)}, u32[]{:S(2)}) collective-permute-start(bf16[8,64,1024]{2,1,0:T(8,128)(2,1)} %get-tuple-element.377), channel_id=1, source_target_pairs={{0,1},{1,0},{2,3},{3,2},{4,5},{5,4},{6,7},{7,6},{8,9},{9,8},{10,11... | collective-permute-start | bytes 3145736 | tf_op jit(solution)/shard_map/ppermute | solution.py:30
  575.5 90.5 %all-to-all-start = ((bf16[32,296,96]{1,2,0:T(8,128)(2,1)}), bf16[32,296,96]{1,2,0:T(8,128)(2,1)S(1)}, u32[]{:S(2)}, u32[]{:S(2)}) async-start(bf16[32,296,96]{1,2,0:T(8,128)(2,1)} %concatenate.78), calls=%async_computation | async-start | bytes 4718592 | tf_op jit(solution)/shard_map/all_to_all | solution.py:705
  599.8 115.9 %collective-permute-start.46 = (bf16[1,120,768]{2,1,0:T(8,128)(2,1)}, bf16[1,120,768]{2,1,0:T(8,128)(2,1)}, u32[]{:S(2)}, u32[]{:S(2)}) collective-permute-start(bf16[1,120,768]{2,1,0:T(8,128)(2,1)} %fusion.172), channel_id=1, source_target_pairs={{0,16},{1,17},{2,18},{3,19},{4,20},{5,21},{6,22},{7,23},{8,24},{9,... | collective-permute-start | bytes 552968 | tf_op jit(solution)/shard_map/ppermute | solution.py:30
  607.8 88.5 %collective-permute-start.41 = (bf16[1,128,768]{2,1,0:T(8,128)(2,1)}, bf16[1,128,768]{2,1,0:T(8,128)(2,1)}, u32[]{:S(2)}, u32[]{:S(2)}) collective-permute-start(bf16[1,128,768]{2,1,0:T(8,128)(2,1)} %fusion.169), channel_id=1, source_target_pairs={{0,16},{1,17},{2,18},{3,19},{4,20},{5,21},{6,22},{7,23},{8,24},{9,... | collective-permute-start | bytes 589832 | tf_op jit(solution)/shard_map/ppermute | solution.py:30
  608.0 87.9 %collective-permute-start.42 = (bf16[1,96,768]{2,1,0:T(8,128)(2,1)}, bf16[1,96,768]{2,1,0:T(8,128)(2,1)}, u32[]{:S(2)}, u32[]{:S(2)}) collective-permute-start(bf16[1,96,768]{2,1,0:T(8,128)(2,1)} %fusion.181), channel_id=1, source_target_pairs={{0,16},{1,17},{2,18},{3,19},{4,20},{5,21},{6,22},{7,23},{8,24},{9,... | collective-permute-start | bytes 442376 | tf_op jit(solution)/shard_map/ppermute | solution.py:30
  620.9 78.0 %collective-permute-start.40 = (bf16[4,64,1024]{2,1,0:T(8,128)(2,1)}, bf16[4,64,1024]{2,1,0:T(8,128)(2,1)}, u32[]{:S(2)}, u32[]{:S(2)}) collective-permute-start(bf16[4,64,1024]{2,1,0:T(8,128)(2,1)} %get-tuple-element.388), channel_id=1, source_target_pairs={{0,4},{1,5},{2,6},{3,7},{4,0},{5,1},{6,2},{7,3},{8,12},{9,13},{10,... | collective-permute-start | bytes 1572872 | tf_op jit(solution)/shard_map/ppermute | solution.py:30
  622.4 76.5 %collective-permute-start.39 = (bf16[4,32,1024]{2,1,0:T(8,128)(2,1)}, bf16[4,32,1024]{2,1,0:T(8,128)(2,1)}, u32[]{:S(2)}, u32[]{:S(2)}) collective-permute-start(bf16[4,32,1024]{2,1,0:T(8,128)(2,1)} %get-tuple-element.387), channel_id=1, source_target_pairs={{0,1},{1,0},{2,3},{3,2},{4,5},{5,4},{6,7},{7,6},{8,9},{9,8},{10,11... | collective-permute-start | bytes 786440 | tf_op jit(solution)/shard_map/ppermute | solution.py:30
  (161 other events, 1436.7 us)
Sparse Core Ops, SparseCore 0:
  15.8 179.2 all-gather.5
  198.0 128.5 all-gather.7
  383.5 76.5 all-gather.9
  463.3 115.0 all-gather.11

commit v4 on v2

--- a/solution.py
+++ b/solution.py
@@ -681,8 +681,8 @@
     )
     c3x = Chunk(i_pairs[:1], d_v, halving(2, 0))
     c3y = Chunk(i_pairs[1:], d_v, halving(0, 2))
-    c3x.send, c3x.keep, c3y.send, c3y.keep, i_res, i_ga, t_ga, self_slices = close_round(
-        [c1i, c3a, c3b], c3x.send, c3x.keep, c3y.send, c3y.keep, i_res, i_ga, t_ga, self_slices
+    c3x.send, c3x.keep, c3y.send, c3y.keep, i_res, i_ga, t_ga = close_round(
+        [c1i, c3a, c3b], c3x.send, c3x.keep, c3y.send, c3y.keep, i_res, i_ga, t_ga
     )
 
     start(c3x, c3y, c1i)
@@ -703,40 +703,50 @@
     start(c3x, c3y, c1i)
     text_input_grad = t_res + mm_t(t_grads, w_ctp)
     image_input_grad = i_res + mm_t(i_grads, w_cip)
-    text_input_grad, image_input_grad = close_round([c3x, c3y, c1i], text_input_grad, image_input_grad)
+    rows_all = t_low
+    if by_permute:
+        short = x_v.size // d_t
+        wide_v = x_v.shape[0]
+        tall_v = -(-wide_v // 8) * 8
+        rows_all = (
+            seen[:, :short].reshape(-1, d_v),
+            seen[:, short : 2 * short].reshape(-1, d_v),
+            seen[:, 2 * short : 2 * short + tall].reshape(-1, d_t),
+            seen[:, 2 * short + tall :].reshape(-1, d_t),
+        )
+    text_input_grad, image_input_grad, rows_all = close_round(
+        [c3x, c3y, c1i], text_input_grad, image_input_grad, rows_all
+    )
+
+    def slices_grad(rows, part, own):
+        grad = t_mm(rows, part.reshape(-1, part.shape[2]))[:, : 3 * own]
+        return grad.reshape(grad.shape[0], 3, own).transpose(1, 0, 2)
+
     start(c3x, c3y, c3a, c3b)
-    close_round([c3x, c3y, c3a, c3b])
+    self_grads, cross_grads = t_low, t_low
+    if by_permute:
+        all_v, all_low_v, all_t, all_low_t = rows_all
+        self_grads = (
+            slices_grad(all_low_t, self_slices[:, :tall], own_t),
+            slices_grad(all_low_v, self_slices[:, tall : tall + wide_v], own_v),
+        )
+    (self_grads,) = close_round([c3x, c3y, c3a, c3b], self_grads)
     start(c3x, c3y, c1a, c1b)
-    close_round([c3x, c3y, c1a, c1b])
+    if by_permute:
+        cross_grads = (
+            slices_grad(all_t, cross_slices[:, :tall], own_c),
+            slices_grad(all_v, cross_slices[:, tall : tall + wide_v], own_c),
+            jnp.sum(cross_slices[:, tall + tall_v :].astype(FLOAT), axis=0),
+        )
+    (cross_grads,) = close_round([c3x, c3y, c1a, c1b], cross_grads)
     for m in (c1a, c1b, c3a, c3b, c1i, c3x, c3y):
         while m.step < bits:
             m.start()
             m.absorb()
 
-    def slices_grad(rows, slices, own):
-        grad = t_mm(rows, slices)[:, : 3 * own]
-        return grad.reshape(grad.shape[0], 3, own).transpose(1, 0, 2)
-
-    if by_permute:
-        short = x_v.size // d_t
-        wide_v = x_v.shape[0]
-        tall_v = -(-wide_v // 8) * 8
-
-        def rows_of(at, rows):
-            return seen[:, at : at + rows]
-
-        def flat_slices(slices, at, rows):
-            return slices[:, at : at + rows].reshape(-1, slices.shape[2])
-
-        all_v = rows_of(0, short).reshape(-1, d_v)
-        all_low_v = rows_of(short, short).reshape(-1, d_v)
-        all_t = rows_of(2 * short, tall).reshape(-1, d_t)
-        all_low_t = rows_of(2 * short + tall, tall).reshape(-1, d_t)
-        o_stp = slices_grad(all_low_t, flat_slices(self_slices, 0, tall), own_t)
-        o_sip = slices_grad(all_low_v, flat_slices(self_slices, tall, wide_v), own_v)
-        o_ctp = slices_grad(all_t, flat_slices(cross_slices, 0, tall), own_c)
-        o_cip = slices_grad(all_v, flat_slices(cross_slices, tall, wide_v), own_c)
-        gain_sum = jnp.sum(cross_slices[:, tall + tall_v :].astype(FLOAT), axis=0)
+    if by_permute:
+        o_stp, o_sip = self_grads
+        o_ctp, o_cip, gain_sum = cross_grads
         o_tg, o_ig = gain_sum[:4, :own_t], gain_sum[4:, :own_v]
     else:
 

time: 726 us -> 744 us (1.025)
  waiting for transfers between devices: 289 us -> 304 us
    ppermute x50, waiting for transfers between devices: 289 us -> 304 us  [swap(): return lax.ppermute(block, ALL, [(i, i ^ 1 << bit) for i in range(size)])]
    all_to_all x2, starting transfers between devices: 23.4 us -> 32.7 us  [exchange(): lax.all_to_all(jnp.concatenate(blocks, axis=1), ALL, split_axis=0, concat...]
    convert_element_type x28, other arithmetic: 51.7 us -> 43.1 us  [add_low(): return (left.astype(FLOAT) + right.astype(FLOAT)).astype(BFLOAT)]
    unnamed x306 -> x276, local copies, waits for them, and re-layouts: 37.4 us -> 36.9 us
  transfers between devices with their start and end apart: 55 -> 55, of which waited for: 23 -> 26; matrix products, arithmetic and copies ran while one was open for 27% -> 29% of each run, Pallas kernels for 9% -> 9%
where the time goes in v4:
time: 744 us; the launch traced here: 734 us
  waiting for transfers between devices  304 us (41%)
  local copies, waits for them, and re-layouts  93.9 us (13%)
  matrix products  93.7 us (13%)
  starting transfers between devices  88.2 us (12%)
  other arithmetic  74.3 us (10%)
  Pallas kernels  63.5 us (9%)
  between operations  16.2 us (2%)
    ppermute x50, waiting for transfers between devices, swap(): return lax.ppermute(block, ALL, [(i, i ^ 1 << bit) for i in range(size)])  304 us
    ppermute x50, starting transfers between devices, swap(): return lax.ppermute(block, ALL, [(i, i ^ 1 << bit) for i in range(size)])  55.3 us
    dot_general x16, matrix products, mm_t(): lax.dot_general(left, right, (((1,), (1,)), ((), ())), preferred_element_...  48.1 us
    convert_element_type x28, other arithmetic, add_low(): return (left.astype(FLOAT) + right.astype(FLOAT)).astype(BFLOAT)  43.1 us
    dot_general x16, matrix products, mm(): return jnp.dot(left, right, preferred_element_type=FLOAT)  37.3 us
    unnamed x276, local copies, waits for them, and re-layouts  36.9 us
    pallas_call x7, Pallas kernels, pack_kernel(): pl.pallas_call(body, grid_spec=pltpu.PrefetchScalarGridSpec(num_scalar_pr...  34.8 us
    all_to_all x2, starting transfers between devices, exchange(): lax.all_to_all(jnp.concatenate(blocks, axis=1), ALL, split_axis=0, concat...  32.7 us
  transfers between devices with their start and end apart: 55, of which 26 were waited for; matrix products, arithmetic and copies ran while one was open for 29% of the time, Pallas kernels for 9%

profile of v4, /device:TPU:0, one launch (start us, length us, event | category | flops | bytes accessed | tf_op | source)
XLA Modules:
  0.0 733.6 jit_solution(11402660738471322076)
XLA Ops:
  21.2 22.1 %collective-permute-done = bf16[1,32,3072]{2,1,0:T(8,128)(2,1)S(1)} collective-permute-done((bf16[1,32,3072]{2,1,0:T(8,128)(2,1)S(1)}, bf16[1,32,3072]{2,1,0:T(8,128)(2,1)S(1)}, u32[]{:S(2)}, u32[]{:S(2)}) %collective-permute-start) | collective-permute-done | bytes 196640 | tf_op jit(solution)/shard_map/ppermute | solution.py:30
  43.3 7.9 %collective-permute-done.1 = bf16[1,128,768]{2,1,0:T(8,128)(2,1)S(1)} collective-permute-done((bf16[1,128,768]{2,1,0:T(8,128)(2,1)S(1)}, bf16[1,128,768]{2,1,0:T(8,128)(2,1)S(1)}, u32[]{:S(2)}, u32[]{:S(2)}) %collective-permute-start.1) | collective-permute-done | bytes 196640 | tf_op jit(solution)/shard_map/ppermute | solution.py:30
  53.4 21.3 %collective-permute-done.2 = bf16[2,32,3072]{2,1,0:T(8,128)(2,1)S(1)} collective-permute-done((bf16[2,32,3072]{2,1,0:T(8,128)(2,1)S(1)}, bf16[2,32,3072]{2,1,0:T(8,128)(2,1)S(1)}, u32[]{:S(2)}, u32[]{:S(2)}) %collective-permute-start.2) | collective-permute-done | bytes 393248 | tf_op jit(solution)/shard_map/ppermute | solution.py:30
  74.7 20.8 %collective-permute-done.3 = bf16[2,128,768]{2,1,0:T(8,128)(2,1)S(1)} collective-permute-done((bf16[2,128,768]{2,1,0:T(8,128)(2,1)S(1)}, bf16[2,128,768]{2,1,0:T(8,128)(2,1)S(1)}, u32[]{:S(2)}, u32[]{:S(2)}) %collective-permute-start.3) | collective-permute-done | bytes 393248 | tf_op jit(solution)/shard_map/ppermute | solution.py:30
  101.0 12.8 %collective-permute-done.6 = bf16[1,96,768]{2,1,0:T(8,128)(2,1)S(1)} collective-permute-done((bf16[1,96,768]{2,1,0:T(8,128)(2,1)S(1)}, bf16[1,96,768]{2,1,0:T(8,128)(2,1)S(1)}, u32[]{:S(2)}, u32[]{:S(2)}) %collective-permute-start.6) | collective-permute-done | bytes 147488 | tf_op jit(solution)/shard_map/ppermute | solution.py:30
  113.8 6.7 collective-permute-done.4
  127.4 10.5 %collective-permute-done.9 = bf16[2,96,768]{2,1,0:T(8,128)(2,1)S(1)} collective-permute-done((bf16[2,96,768]{2,1,0:T(8,128)(2,1)S(1)}, bf16[2,96,768]{2,1,0:T(8,128)(2,1)S(1)}, u32[]{:S(2)}, u32[]{:S(2)}) %collective-permute-start.9) | collective-permute-done | bytes 294944 | tf_op jit(solution)/shard_map/ppermute | solution.py:30
  137.9 38.3 %collective-permute-done.7 = bf16[8,32,3072]{2,1,0:T(8,128)(2,1)S(1)} collective-permute-done((bf16[8,32,3072]{2,1,0:T(8,128)(2,1)S(1)}, bf16[8,32,3072]{2,1,0:T(8,128)(2,1)S(1)}, u32[]{:S(2)}, u32[]{:S(2)}) %collective-permute-start.7) | collective-permute-done | bytes 1572896 | tf_op jit(solution)/shard_map/ppermute | solution.py:30
  180.6 13.8 %collective-permute-done.12 = bf16[4,96,768]{2,1,0:T(8,128)(2,1)S(1)} collective-permute-done((bf16[4,96,768]{2,1,0:T(8,128)(2,1)S(1)}, bf16[4,96,768]{2,1,0:T(8,128)(2,1)S(1)}, u32[]{:S(2)}, u32[]{:S(2)}) %collective-permute-start.12) | collective-permute-done | bytes 589856 | tf_op jit(solution)/shard_map/ppermute | solution.py:30
  219.4 11.0 %collective-permute-done.13 = bf16[8,96,768]{2,1,0:T(8,128)(2,1)} collective-permute-done((bf16[8,96,768]{2,1,0:T(8,128)(2,1)}, bf16[8,96,768]{2,1,0:T(8,128)(2,1)}, u32[]{:S(2)}, u32[]{:S(2)}) %collective-permute-start.13) | collective-permute-done | bytes 1179680 | tf_op jit(solution)/shard_map/ppermute | solution.py:30
  265.1 5.4 shard_map.396
  274.8 5.2 shard_map.395
  283.4 6.0 shard_map.397
  312.3 5.0 shard_map.399
  319.7 6.0 shard_map.398
  330.7 7.5 %collective-permute-done.18 = bf16[8,120,768]{2,1,0:T(8,128)(2,1)S(1)} collective-permute-done((bf16[8,120,768]{2,1,0:T(8,128)(2,1)S(1)}, bf16[8,120,768]{2,1,0:T(8,128)(2,1)S(1)}, u32[]{:S(2)}, u32[]{:S(2)}) %collective-permute-start.18) | collective-permute-done | bytes 1474592 | tf_op jit(solution)/shard_map/ppermute | solution.py:30
  344.9 12.5 %collective-permute-done.19 = bf16[4,96,768]{2,1,0:T(8,128)(2,1)} collective-permute-done((bf16[4,96,768]{2,1,0:T(8,128)(2,1)}, bf16[4,96,768]{2,1,0:T(8,128)(2,1)}, u32[]{:S(2)}, u32[]{:S(2)}) %collective-permute-start.19) | collective-permute-done | bytes 589856 | tf_op jit(solution)/shard_map/ppermute | solution.py:30
  411.5 8.2 %collective-permute-done.26 = bf16[8,96,768]{2,1,0:T(8,128)(2,1)S(1)} collective-permute-done((bf16[8,96,768]{2,1,0:T(8,128)(2,1)S(1)}, bf16[8,96,768]{2,1,0:T(8,128)(2,1)S(1)}, u32[]{:S(2)}, u32[]{:S(2)}) %collective-permute-start.26) | collective-permute-done | bytes 1179680 | tf_op jit(solution)/shard_map/ppermute | solution.py:30
  419.7 8.2 %collective-permute-done.25 = bf16[8,128,768]{2,1,0:T(8,128)(2,1)S(1)} collective-permute-done((bf16[8,128,768]{2,1,0:T(8,128)(2,1)S(1)}, bf16[8,128,768]{2,1,0:T(8,128)(2,1)S(1)}, u32[]{:S(2)}, u32[]{:S(2)}) %collective-permute-start.25) | collective-permute-done | bytes 1572896 | tf_op jit(solution)/shard_map/ppermute | solution.py:30
  437.5 4.8 fusion.138
  442.3 18.3 %collective-permute-done.29 = bf16[4,96,768]{2,1,0:T(8,128)(2,1)S(1)} collective-permute-done((bf16[4,96,768]{2,1,0:T(8,128)(2,1)S(1)}, bf16[4,96,768]{2,1,0:T(8,128)(2,1)S(1)}, u32[]{:S(2)}, u32[]{:S(2)}) %collective-permute-start.29) | collective-permute-done | bytes 589856 | tf_op jit(solution)/shard_map/ppermute | solution.py:30
  483.6 10.1 %collective-permute-done.32 = bf16[2,96,768]{2,1,0:T(8,128)(2,1)S(1)} collective-permute-done((bf16[2,96,768]{2,1,0:T(8,128)(2,1)S(1)}, bf16[2,96,768]{2,1,0:T(8,128)(2,1)S(1)}, u32[]{:S(2)}, u32[]{:S(2)}) %collective-permute-start.32) | collective-permute-done | bytes 294944 | tf_op jit(solution)/shard_map/ppermute | solution.py:30
  493.7 24.2 %collective-permute-done.30 = bf16[8,96,1024]{2,1,0:T(8,128)(2,1)S(1)} collective-permute-done((bf16[8,96,1024]{2,1,0:T(8,128)(2,1)S(1)}, bf16[8,96,1024]{2,1,0:T(8,128)(2,1)S(1)}, u32[]{:S(2)}, u32[]{:S(2)}) %collective-permute-start.30) | collective-permute-done | bytes 1572896 | tf_op jit(solution)/shard_map/ppermute | solution.py:30
  533.7 27.9 %all-to-all-start = ((bf16[32,144,96]{2,1,0:T(8,128)(2,1)}), bf16[32,144,96]{2,1,0:T(8,128)(2,1)}, u32[]{:S(2)}, u32[]{:S(2)}) async-start(bf16[32,144,96]{2,1,0:T(8,128)(2,1)} %copy.152), calls=%async_computation | async-start | bytes 2359296 | tf_op jit(solution)/shard_map/all_to_all | solution.py:620
  573.3 8.1 %shard_map.405 = (bf16[100,3072]{1,0:T(8,128)(2,1)S(1)}, bf16[36,3072]{1,0:T(8,128)(2,1)S(1)}) custom-call(s32[1]{0:T(128)} %dynamic_slice.308.len_ref, bf16[100,3072]{1,0:T(8,128)(2,1)S(1)} %copy-done.14, bf16[36,3072]{1,0:T(8,128)(2,1)S(1)} %fusion.27.image_ref, bf16[100,1024]{1,0:T(8,128)(2,1)S(1)} %copy-done.31, bf16[36,1024]{1,0:T(8,128)(2,1)S(1)} %fusion.141.ig_ref), custom_call_target="tpu_custom_call" | custom-call | tf_op jit(solution)/shard_map/pallas_call | solution.py:404
  581.4 12.6 %collective-permute-done.35 = bf16[4,96,1024]{2,1,0:T(8,128)(2,1)} collective-permute-done((bf16[4,96,1024]{2,1,0:T(8,128)(2,1)}, bf16[4,96,1024]{2,1,0:T(8,128)(2,1)}, u32[]{:S(2)}, u32[]{:S(2)}) %collective-permute-start.35) | collective-permute-done | bytes 786464 | tf_op jit(solution)/shard_map/ppermute | solution.py:30
  609.5 4.8 all-to-all-start.1
  626.4 4.8 convolution_add_fusion.4
  635.9 15.1 %collective-permute-done.38 = bf16[2,96,1024]{2,1,0:T(8,128)(2,1)S(1)} collective-permute-done((bf16[2,96,1024]{2,1,0:T(8,128)(2,1)S(1)}, bf16[2,96,1024]{2,1,0:T(8,128)(2,1)S(1)}, u32[]{:S(2)}, u32[]{:S(2)}) %collective-permute-start.38) | collective-permute-done | bytes 393248 | tf_op jit(solution)/shard_map/ppermute | solution.py:30
  665.0 8.6 %fusion.236 = (bf16[32,104,768]{2,1,0:T(8,128)(2,1)}, bf16[32,104,768]{2,1,0:T(8,128)(2,1)}) fusion(bf16[32,304,768]{2,1,0:T(8,128)(2,1)} %bitcast.387), kind=kLoop, calls=%fused_computation.430 | loop fusion | bytes 20447232 | tf_op jit(solution)/shard_map/slice | solution.py:715
  677.7 5.1 reshape.958
  711.7 5.4 collective-permute-done.49
  (587 shorter events, 338.4 us)
Async XLA Ops:
  7.3 205.3 %all-gather.5.cloned.1.call-start = ((), (), s32[]{:S(2)}) async-start(), calls=%async_computation.2 | async-start | bytes 19464192 | tf_op jit(solution)/shard_map/all_gather | solution.py:543
  15.7 357.3 %all-gather.7.cloned.1.call-start = ((), (), s32[]{:S(2)}) async-start(), calls=%async_computation.3 | async-start | bytes 19464192 | tf_op jit(solution)/shard_map/all_gather | solution.py:543
  16.8 648.2 %all-gather.9.cloned.1.call-start = ((), (), s32[]{:S(2)}) async-start(), calls=%async_computation.4 | async-start | bytes 15409152 | tf_op jit(solution)/shard_map/all_gather | solution.py:668
  21.1 30.2 %collective-permute-start.1 = (bf16[1,128,768]{2,1,0:T(8,128)(2,1)S(1)}, bf16[1,128,768]{2,1,0:T(8,128)(2,1)S(1)}, u32[]{:S(2)}, u32[]{:S(2)}) collective-permute-start(bf16[1,128,768]{2,1,0:T(8,128)(2,1)S(1)} %maximum_bitcast_fusion.1), channel_id=1, source_target_pairs={{0,16},{1,17},{2,18},{3,19},{4,20},{5,21},{6,22},{7,23},{8,24},{9,... | collective-permute-start | bytes 589832 | tf_op jit(solution)/shard_map/ppermute | solution.py:30
  52.1 43.4 %collective-permute-start.3 = (bf16[2,128,768]{2,1,0:T(8,128)(2,1)S(1)}, bf16[2,128,768]{2,1,0:T(8,128)(2,1)S(1)}, u32[]{:S(2)}, u32[]{:S(2)}) collective-permute-start(bf16[2,128,768]{2,1,0:T(8,128)(2,1)S(1)} %pad_maximum_fusion.10), channel_id=1, source_target_pairs={{0,8},{1,9},{2,10},{3,11},{4,12},{5,13},{6,14},{7,15},{8,0},{9,1},... | collective-permute-start | bytes 1179656 | tf_op jit(solution)/shard_map/ppermute | solution.py:30
  96.8 27.7 %collective-permute-start.5 = (bf16[4,128,768]{2,1,0:T(8,128)(2,1)S(1)}, bf16[4,128,768]{2,1,0:T(8,128)(2,1)S(1)}, u32[]{:S(2)}, u32[]{:S(2)}) collective-permute-start(bf16[4,128,768]{2,1,0:T(8,128)(2,1)S(1)} %pad_maximum_fusion.7), channel_id=1, source_target_pairs={{0,4},{1,5},{2,6},{3,7},{4,0},{5,1},{6,2},{7,3},{8,12},{9,13},{10,... | collective-permute-start | bytes 2359304 | tf_op jit(solution)/shard_map/ppermute | solution.py:30
  124.9 51.4 %collective-permute-start.7 = (bf16[8,32,3072]{2,1,0:T(8,128)(2,1)S(1)}, bf16[8,32,3072]{2,1,0:T(8,128)(2,1)S(1)}, u32[]{:S(2)}, u32[]{:S(2)}) collective-permute-start(bf16[8,32,3072]{2,1,0:T(8,128)(2,1)S(1)} %pad_maximum_fusion.3), channel_id=1, source_target_pairs={{0,4},{1,5},{2,6},{3,7},{4,0},{5,1},{6,2},{7,3},{8,12},{9,13},{10,... | collective-permute-start | bytes 4718600 | tf_op jit(solution)/shard_map/ppermute | solution.py:30
  127.4 48.8 %collective-permute-start.8 = (bf16[8,128,768]{2,1,0:T(8,128)(2,1)S(1)}, bf16[8,128,768]{2,1,0:T(8,128)(2,1)S(1)}, u32[]{:S(2)}, u32[]{:S(2)}) collective-permute-start(bf16[8,128,768]{2,1,0:T(8,128)(2,1)S(1)} %pad_maximum_fusion.4), channel_id=1, source_target_pairs={{0,1},{1,0},{2,3},{3,2},{4,5},{5,4},{6,7},{7,6},{8,9},{9,8},{10,11... | collective-permute-start | bytes 4718600 | tf_op jit(solution)/shard_map/ppermute | solution.py:30
  198.9 31.6 %collective-permute-start.13 = (bf16[8,96,768]{2,1,0:T(8,128)(2,1)}, bf16[8,96,768]{2,1,0:T(8,128)(2,1)}, u32[]{:S(2)}, u32[]{:S(2)}) collective-permute-start(bf16[8,96,768]{2,1,0:T(8,128)(2,1)} %pad_maximum_fusion.5), channel_id=1, source_target_pairs={{0,1},{1,0},{2,3},{3,2},{4,5},{5,4},{6,7},{7,6},{8,9},{9,8},{10,11... | collective-permute-start | bytes 3538952 | tf_op jit(solution)/shard_map/ppermute | solution.py:30
  270.5 26.7 %collective-permute-start.16 = (bf16[16,120,768]{2,1,0:T(8,128)(2,1)}, bf16[16,120,768]{2,1,0:T(8,128)(2,1)}, u32[]{:S(2)}, u32[]{:S(2)}) collective-permute-start(bf16[16,120,768]{2,1,0:T(8,128)(2,1)} %bitcast.33), channel_id=1, source_target_pairs={{0,2},{1,3},{2,0},{3,1},{4,6},{5,7},{6,4},{7,5},{8,10},{9,11},{10,... | collective-permute-start | bytes 8847368 | tf_op jit(solution)/shard_map/ppermute | solution.py:30
  302.3 28.4 %collective-permute-start.17 = (bf16[8,96,768]{2,1,0:T(8,128)(2,1)S(1)}, bf16[8,96,768]{2,1,0:T(8,128)(2,1)S(1)}, u32[]{:S(2)}, u32[]{:S(2)}) collective-permute-start(bf16[8,96,768]{2,1,0:T(8,128)(2,1)S(1)} %get-tuple-element.277), channel_id=1, source_target_pairs={{0,4},{1,5},{2,6},{3,7},{4,0},{5,1},{6,2},{7,3},{8,12},{9,13},{10,... | collective-permute-start | bytes 3538952 | tf_op jit(solution)/shard_map/ppermute | solution.py:30
  303.9 34.4 %collective-permute-start.18 = (bf16[8,120,768]{2,1,0:T(8,128)(2,1)S(1)}, bf16[8,120,768]{2,1,0:T(8,128)(2,1)S(1)}, u32[]{:S(2)}, u32[]{:S(2)}) collective-permute-start(bf16[8,120,768]{2,1,0:T(8,128)(2,1)S(1)} %get-tuple-element.278), channel_id=1, source_target_pairs={{0,1},{1,0},{2,3},{3,2},{4,5},{5,4},{6,7},{7,6},{8,9},{9,8},{10,11... | collective-permute-start | bytes 4423688 | tf_op jit(solution)/shard_map/ppermute | solution.py:30
  389.7 38.2 %collective-permute-start.25 = (bf16[8,128,768]{2,1,0:T(8,128)(2,1)S(1)}, bf16[8,128,768]{2,1,0:T(8,128)(2,1)S(1)}, u32[]{:S(2)}, u32[]{:S(2)}) collective-permute-start(bf16[8,128,768]{2,1,0:T(8,128)(2,1)S(1)} %copy-done.52), channel_id=1, source_target_pairs={{0,4},{1,5},{2,6},{3,7},{4,0},{5,1},{6,2},{7,3},{8,12},{9,13},{10,... | collective-permute-start | bytes 4718600 | tf_op jit(solution)/shard_map/ppermute | solution.py:30
  390.2 29.5 %collective-permute-start.26 = (bf16[8,96,768]{2,1,0:T(8,128)(2,1)S(1)}, bf16[8,96,768]{2,1,0:T(8,128)(2,1)S(1)}, u32[]{:S(2)}, u32[]{:S(2)}) collective-permute-start(bf16[8,96,768]{2,1,0:T(8,128)(2,1)S(1)} %copy-done.63), channel_id=1, source_target_pairs={{0,1},{1,0},{2,3},{3,2},{4,5},{5,4},{6,7},{7,6},{8,9},{9,8},{10,11... | collective-permute-start | bytes 3538952 | tf_op jit(solution)/shard_map/ppermute | solution.py:30
  431.2 29.4 %collective-permute-start.27 = (bf16[16,96,1024]{2,1,0:T(8,128)(2,1)S(1)}, bf16[16,96,1024]{2,1,0:T(8,128)(2,1)S(1)}, u32[]{:S(2)}, u32[]{:S(2)}) collective-permute-start(bf16[16,96,1024]{2,1,0:T(8,128)(2,1)S(1)} %bitcast.385), channel_id=1, source_target_pairs={{0,2},{1,3},{2,0},{3,1},{4,6},{5,7},{6,4},{7,5},{8,10},{9,11},{10,... | collective-permute-start | bytes 9437192 | tf_op jit(solution)/shard_map/ppermute | solution.py:30
  431.2 29.3 %collective-permute-start.28 = (bf16[4,128,768]{2,1,0:T(8,128)(2,1)S(1)}, bf16[4,128,768]{2,1,0:T(8,128)(2,1)S(1)}, u32[]{:S(2)}, u32[]{:S(2)}) collective-permute-start(bf16[4,128,768]{2,1,0:T(8,128)(2,1)S(1)} %get-tuple-element.327), channel_id=1, source_target_pairs={{0,1},{1,0},{2,3},{3,2},{4,5},{5,4},{6,7},{7,6},{8,9},{9,8},{10,11... | collective-permute-start | bytes 2359304 | tf_op jit(solution)/shard_map/ppermute | solution.py:30
  432.4 28.2 %collective-permute-start.29 = (bf16[4,96,768]{2,1,0:T(8,128)(2,1)S(1)}, bf16[4,96,768]{2,1,0:T(8,128)(2,1)S(1)}, u32[]{:S(2)}, u32[]{:S(2)}) collective-permute-start(bf16[4,96,768]{2,1,0:T(8,128)(2,1)S(1)} %get-tuple-element.328), channel_id=1, source_target_pairs={{0,4},{1,5},{2,6},{3,7},{4,0},{5,1},{6,2},{7,3},{8,12},{9,13},{10,... | collective-permute-start | bytes 1769480 | tf_op jit(solution)/shard_map/ppermute | solution.py:30
  462.5 55.3 %collective-permute-start.30 = (bf16[8,96,1024]{2,1,0:T(8,128)(2,1)S(1)}, bf16[8,96,1024]{2,1,0:T(8,128)(2,1)S(1)}, u32[]{:S(2)}, u32[]{:S(2)}) collective-permute-start(bf16[8,96,1024]{2,1,0:T(8,128)(2,1)S(1)} %get-tuple-element.337), channel_id=1, source_target_pairs={{0,1},{1,0},{2,3},{3,2},{4,5},{5,4},{6,7},{7,6},{8,9},{9,8},{10,11... | collective-permute-start | bytes 4718600 | tf_op jit(solution)/shard_map/ppermute | solution.py:30
  463.5 30.2 %collective-permute-start.31 = (bf16[2,128,768]{2,1,0:T(8,128)(2,1)S(1)}, bf16[2,128,768]{2,1,0:T(8,128)(2,1)S(1)}, u32[]{:S(2)}, u32[]{:S(2)}) collective-permute-start(bf16[2,128,768]{2,1,0:T(8,128)(2,1)S(1)} %get-tuple-element.338), channel_id=1, source_target_pairs={{0,8},{1,9},{2,10},{3,11},{4,12},{5,13},{6,14},{7,15},{8,0},{9,1},... | collective-permute-start | bytes 1179656 | tf_op jit(solution)/shard_map/ppermute | solution.py:30
  463.5 30.1 %collective-permute-start.32 = (bf16[2,96,768]{2,1,0:T(8,128)(2,1)S(1)}, bf16[2,96,768]{2,1,0:T(8,128)(2,1)S(1)}, u32[]{:S(2)}, u32[]{:S(2)}) collective-permute-start(bf16[2,96,768]{2,1,0:T(8,128)(2,1)S(1)} %get-tuple-element.339), channel_id=1, source_target_pairs={{0,8},{1,9},{2,10},{3,11},{4,12},{5,13},{6,14},{7,15},{8,0},{9,1},... | collective-permute-start | bytes 884744 | tf_op jit(solution)/shard_map/ppermute | solution.py:30
  521.1 72.9 %collective-permute-start.34 = (bf16[16,64,1024]{2,1,0:T(8,128)(2,1)}, bf16[16,64,1024]{2,1,0:T(8,128)(2,1)}, u32[]{:S(2)}, u32[]{:S(2)}) collective-permute-start(bf16[16,64,1024]{2,1,0:T(8,128)(2,1)} %bitcast.92), channel_id=1, source_target_pairs={{0,2},{1,3},{2,0},{3,1},{4,6},{5,7},{6,4},{7,5},{8,10},{9,11},{10,... | collective-permute-start | bytes 6291464 | tf_op jit(solution)/shard_map/ppermute | solution.py:30
  533.7 75.8 %all-to-all-start = ((bf16[32,144,96]{2,1,0:T(8,128)(2,1)}), bf16[32,144,96]{2,1,0:T(8,128)(2,1)}, u32[]{:S(2)}, u32[]{:S(2)}) async-start(bf16[32,144,96]{2,1,0:T(8,128)(2,1)} %copy.152), calls=%async_computation | async-start | bytes 2359296 | tf_op jit(solution)/shard_map/all_to_all | solution.py:620
  561.6 32.4 %collective-permute-start.33 = (bf16[16,32,1024]{2,1,0:T(8,128)(2,1)}, bf16[16,32,1024]{2,1,0:T(8,128)(2,1)}, u32[]{:S(2)}, u32[]{:S(2)}) collective-permute-start(bf16[16,32,1024]{2,1,0:T(8,128)(2,1)} %bitcast.90), channel_id=1, source_target_pairs={{0,2},{1,3},{2,0},{3,1},{4,6},{5,7},{6,4},{7,5},{8,10},{9,11},{10,... | collective-permute-start | bytes 3145736 | tf_op jit(solution)/shard_map/ppermute | solution.py:30
  561.9 32.1 %collective-permute-start.35 = (bf16[4,96,1024]{2,1,0:T(8,128)(2,1)}, bf16[4,96,1024]{2,1,0:T(8,128)(2,1)}, u32[]{:S(2)}, u32[]{:S(2)}) collective-permute-start(bf16[4,96,1024]{2,1,0:T(8,128)(2,1)} %get-tuple-element.358), channel_id=1, source_target_pairs={{0,4},{1,5},{2,6},{3,7},{4,0},{5,1},{6,2},{7,3},{8,12},{9,13},{10,... | collective-permute-start | bytes 2359304 | tf_op jit(solution)/shard_map/ppermute | solution.py:30
  609.5 53.1 %all-to-all-start.1 = ((bf16[32,152,96]{2,1,0:T(8,128)(2,1)}), bf16[32,152,96]{2,1,0:T(8,128)(2,1)S(1)}, u32[]{:S(2)}, u32[]{:S(2)}) async-start(bf16[32,152,96]{2,1,0:T(8,128)(2,1)} %copy.163), calls=%async_computation.1 | async-start | bytes 2490368 | tf_op jit(solution)/shard_map/all_to_all | solution.py:620
  614.3 38.8 %collective-permute-start.37 = (bf16[8,64,1024]{2,1,0:T(8,128)(2,1)}, bf16[8,64,1024]{2,1,0:T(8,128)(2,1)}, u32[]{:S(2)}, u32[]{:S(2)}) collective-permute-start(bf16[8,64,1024]{2,1,0:T(8,128)(2,1)} %get-tuple-element.371), channel_id=1, source_target_pairs={{0,1},{1,0},{2,3},{3,2},{4,5},{5,4},{6,7},{7,6},{8,9},{9,8},{10,11... | collective-permute-start | bytes 3145736 | tf_op jit(solution)/shard_map/ppermute | solution.py:30
  616.3 95.4 %collective-permute-start.48 = (bf16[1,96,768]{2,1,0:T(8,128)(2,1)}, bf16[1,96,768]{2,1,0:T(8,128)(2,1)}, u32[]{:S(2)}, u32[]{:S(2)}) collective-permute-start(bf16[1,96,768]{2,1,0:T(8,128)(2,1)} %fusion.190), channel_id=1, source_target_pairs={{0,16},{1,17},{2,18},{3,19},{4,20},{5,21},{6,22},{7,23},{8,24},{9,... | collective-permute-start | bytes 442376 | tf_op jit(solution)/shard_map/ppermute | solution.py:30
  618.7 86.8 %collective-permute-start.44 = (bf16[1,128,768]{2,1,0:T(8,128)(2,1)}, bf16[1,128,768]{2,1,0:T(8,128)(2,1)}, u32[]{:S(2)}, u32[]{:S(2)}) collective-permute-start(bf16[1,128,768]{2,1,0:T(8,128)(2,1)} %fusion.177), channel_id=1, source_target_pairs={{0,16},{1,17},{2,18},{3,19},{4,20},{5,21},{6,22},{7,23},{8,24},{9,... | collective-permute-start | bytes 589832 | tf_op jit(solution)/shard_map/ppermute | solution.py:30
  623.4 27.5 %collective-permute-start.36 = (bf16[8,32,1024]{2,1,0:T(8,128)(2,1)S(1)}, bf16[8,32,1024]{2,1,0:T(8,128)(2,1)S(1)}, u32[]{:S(2)}, u32[]{:S(2)}) collective-permute-start(bf16[8,32,1024]{2,1,0:T(8,128)(2,1)S(1)} %copy-done.75), channel_id=1, source_target_pairs={{0,4},{1,5},{2,6},{3,7},{4,0},{5,1},{6,2},{7,3},{8,12},{9,13},{10,... | collective-permute-start | bytes 1572872 | tf_op jit(solution)/shard_map/ppermute | solution.py:30
  657.3 28.7 %collective-permute-start.39 = (bf16[4,32,1024]{2,1,0:T(8,128)(2,1)}, bf16[4,32,1024]{2,1,0:T(8,128)(2,1)}, u32[]{:S(2)}, u32[]{:S(2)}) collective-permute-start(bf16[4,32,1024]{2,1,0:T(8,128)(2,1)} %get-tuple-element.376), channel_id=1, source_target_pairs={{0,1},{1,0},{2,3},{3,2},{4,5},{5,4},{6,7},{7,6},{8,9},{9,8},{10,11... | collective-permute-start | bytes 786440 | tf_op jit(solution)/shard_map/ppermute | solution.py:30
  657.6 28.3 %collective-permute-start.40 = (bf16[4,64,1024]{2,1,0:T(8,128)(2,1)}, bf16[4,64,1024]{2,1,0:T(8,128)(2,1)}, u32[]{:S(2)}, u32[]{:S(2)}) collective-permute-start(bf16[4,64,1024]{2,1,0:T(8,128)(2,1)} %get-tuple-element.377), channel_id=1, source_target_pairs={{0,4},{1,5},{2,6},{3,7},{4,0},{5,1},{6,2},{7,3},{8,12},{9,13},{10,... | collective-permute-start | bytes 1572872 | tf_op jit(solution)/shard_map/ppermute | solution.py:30
  659.3 26.6 %collective-permute-start.41 = (bf16[1,96,1024]{2,1,0:T(8,128)(2,1)}, bf16[1,96,1024]{2,1,0:T(8,128)(2,1)}, u32[]{:S(2)}, u32[]{:S(2)}) collective-permute-start(bf16[1,96,1024]{2,1,0:T(8,128)(2,1)} %fusion.176), channel_id=1, source_target_pairs={{0,16},{1,17},{2,18},{3,19},{4,20},{5,21},{6,22},{7,23},{8,24},{9,... | collective-permute-start | bytes 589832 | tf_op jit(solution)/shard_map/ppermute | solution.py:30
  (151 other events, 1538.7 us)
Sparse Core Ops, SparseCore 0:
  15.8 176.8 all-gather.4
  195.6 128.6 all-gather.6
  382.0 170.4 all-gather.8
